TPU v7x, 256 devices: a whole 4x4x8 slice. The times are simulated.
256 devices in a mesh: group: 2 (over core), ctx: 8 (over z), tp: 16 (over y, x).
Axes of the slice: x: 4, y: 4, z: 8, core: 2. Of those that a mesh axis runs over, the one named last changes fastest.
Arguments:
- hidden: bfloat16 [2, 1024, 8192], P('group', 'ctx', 'tp'), may hold values from -6 to 6
- queries: bfloat16 [2, 1024, 4096], P('group', 'ctx', 'tp'), may hold values from -400 to 400
- kv_weight: bfloat16 [8192, 2048], P(None, 'tp'), may hold values from -0.0625 to 0.0625
- out_weight: bfloat16 [4096, 8192], P('tp'), may hold values from -0.375 to 0.375
- cache: bfloat16 [1024, 128, 4096], P('ctx', None, 'tp'), may hold values from -6 to 6
- page_owner: int32 [128], replicated, may hold values from 0 to 7, as said below
- page_slot: int32 [128], replicated, may hold values from 0 to 1023, as said below
- cached_len: int32 [1024], P('ctx'), may hold values from 64 to 128
Outputs:
- layer_out: bfloat16 [2, 1024, 8192], P('group', 'ctx')
Inputs may be any that keep to these rules, and one draw needn't show every extreme that they name: `page_owner`: each aligned block of 16 entries belongs to one prefill context shard; within a block no owner appears more than 2 times, and some owner appears exactly 2 times in every block; in the last block that owner is 0. `page_slot`: all slots differ; slot s is page s % 8 of request s // 8 among the owner's 128 requests.
All inputs are finite; a program needn't handle non-finite values.
Results may differ from a plain program's by a relative error of at most 0.012.
The roundings to bfloat16 on the way count: a program that leaves them out, or rounds other values in their place, can miss the bound.
Values may be sent and summed in bfloat16 or wider, within the bound.
No kernel may reach another device: no remote copies, remote signals or barrier semaphores. Data moves between devices by JAX's collectives and lax.ppermute only.
A program may use at most 128 MiB of HBM per device.

v0:
```python
import jax
import jax.numpy as jnp
from jax import lax
from jax.sharding import PartitionSpec as P

HD = 128
PAGE = 8
CAP = 2


def from_partner(block, axis, bit):
    count = lax.axis_size(axis)
    route = []
    for low in range(count):
        high = low | 1 << bit
        if high != low and high < count:
            route += [(low, high), (high, low)]
    return lax.ppermute(block, axis, route)


def span_branch(query_rows, span_kv, first_row):
    total_rows = span_kv.shape[0]
    copies = query_rows.shape[1]
    keyed = span_kv.reshape(total_rows, copies, 2, HD)
    scores = jnp.einsum(
        "icgd,jcd->cgij", query_rows, keyed[:, :, 0], preferred_element_type=jnp.float32
    ) * HD ** (-0.5)
    positions = first_row + jnp.arange(query_rows.shape[0])
    allowed = jnp.arange(total_rows)[None, :] <= positions[:, None]
    highest = jnp.max(jnp.where(allowed, scores, -jnp.inf), axis=-1, keepdims=True)
    weights = jnp.exp(jnp.where(allowed, scores - highest, -jnp.inf))
    totals = jnp.sum(weights, axis=-1)
    summed = jnp.einsum(
        "cgij,jcd->icgd",
        weights.astype(jnp.bfloat16),
        keyed[:, :, 1],
        preferred_element_type=jnp.float32,
    )
    result = summed / jnp.transpose(totals, (2, 0, 1))[..., None]
    return result.astype(jnp.bfloat16).reshape(query_rows.shape[0], -1)


def request_branch(query_rows, local_kv, cache_pages, arrived, targets, cached_len):
    row_count = query_rows.shape[0]
    copies = query_rows.shape[1]
    filled = cache_pages.at[targets].set(arrived, mode="drop")
    keyed = filled.reshape(row_count, -1, copies, 2, HD)
    position_count = keyed.shape[1]
    own_rows = local_kv.reshape(row_count, copies, 2, HD)
    scores = jnp.einsum(
        "icgd,itcd->icgt", query_rows, keyed[:, :, :, 0], preferred_element_type=jnp.float32
    ) * HD ** (-0.5)
    fresh = jnp.einsum(
        "icgd,icd->icg", query_rows, own_rows[:, :, 0], preferred_element_type=jnp.float32
    ) * HD ** (-0.5)
    allowed = (jnp.arange(position_count)[None, :] < cached_len[:, None])[:, None, None, :]
    highest = jnp.maximum(jnp.max(jnp.where(allowed, scores, -jnp.inf), axis=-1), fresh)
    weights = jnp.exp(jnp.where(allowed, scores - highest[..., None], -jnp.inf))
    fresh_weight = jnp.exp(fresh - highest)
    totals = jnp.sum(weights, axis=-1) + fresh_weight
    summed = jnp.einsum(
        "icgt,itcd->icgd",
        weights.astype(jnp.bfloat16),
        keyed[:, :, :, 1],
        preferred_element_type=jnp.float32,
    )
    own_values = own_rows[:, :, 1].astype(jnp.float32)
    summed = (
        summed
        + fresh_weight.astype(jnp.bfloat16).astype(jnp.float32)[..., None]
        * own_values[:, :, None, :]
    )
    return (summed / totals[..., None]).astype(jnp.bfloat16).reshape(row_count, -1)


def body(hidden, queries, kv_weight, out_weight, cache, page_owner, page_slot, cached_len):
    row_count = hidden.shape[1]
    ctx_count = lax.axis_size("ctx")
    my_ctx = lax.axis_index("ctx")
    role_index = lax.axis_index("group")
    fresh_kv = jnp.dot(
        lax.all_gather(hidden, "tp", axis=2, tiled=True)[0],
        kv_weight,
        preferred_element_type=jnp.float32,
    ).astype(jnp.bfloat16)
    partner_kv = from_partner(fresh_kv, "tp", 0)
    odd_rank = lax.axis_index("tp") % 2 == 1
    local_kv = jnp.concatenate(
        [jnp.where(odd_rank, partner_kv, fresh_kv), jnp.where(odd_rank, fresh_kv, partner_kv)],
        axis=1,
    )
    copies = local_kv.shape[1] // (2 * HD)
    head_count = queries.shape[2] // HD
    query_rows = queries[0].reshape(row_count, copies, head_count // copies, HD)
    span_kv = lax.all_gather(local_kv, "ctx", axis=0, tiled=True)
    page_count = row_count // PAGE
    page_width = PAGE * local_kv.shape[1]
    owners = page_owner.reshape(ctx_count, page_count)
    slots = page_slot.reshape(ctx_count, page_count)
    owner_hits = (owners[:, :, None] == jnp.arange(ctx_count)[None, None, :]).astype(jnp.int32)
    earlier = jnp.cumsum(owner_hits, axis=1) - owner_hits
    placing = jnp.sum(earlier * owner_hits, axis=2)
    my_owners = lax.dynamic_index_in_dim(owners, my_ctx, 0, keepdims=False)
    my_placing = lax.dynamic_index_in_dim(placing, my_ctx, 0, keepdims=False)
    outgoing = local_kv.reshape(page_count, page_width)
    slot_total = 2 * ctx_count * CAP
    target_slot = (ctx_count + my_owners) * CAP + my_placing
    picker = (target_slot[None, :] == jnp.arange(slot_total)[:, None]).astype(jnp.bfloat16)
    packed = jnp.dot(picker, outgoing, preferred_element_type=jnp.float32).astype(jnp.bfloat16)
    arrived = lax.all_to_all(packed, ("group", "ctx"), split_axis=0, concat_axis=0, tiled=True)[
        : ctx_count * CAP
    ]
    position_count = cache.shape[1]
    req_pages = position_count // PAGE
    half_pages = position_count // (2 * PAGE)
    matching = (owners == my_ctx)[:, :, None] & (
        placing[:, :, None] == jnp.arange(CAP)[None, None, :]
    )
    slot_of = jnp.sum(jnp.where(matching, slots[:, :, None] + 1, 0), axis=1) - 1
    targets = jnp.where(
        slot_of >= 0,
        slot_of // half_pages * req_pages + slot_of % half_pages,
        row_count * req_pages,
    ).reshape(-1)
    cache_pages = cache.reshape(row_count * req_pages, page_width)

    def prefill_side():
        return span_branch(query_rows, span_kv, my_ctx * row_count)

    def decode_side():
        return request_branch(query_rows, local_kv, cache_pages, arrived, targets, cached_len)

    attended = lax.cond(role_index == 0, prefill_side, decode_side)
    partial_out = jnp.dot(attended, out_weight, preferred_element_type=jnp.float32)
    combined = lax.psum(partial_out, "tp").astype(jnp.bfloat16)
    return combined[None]


def solution(mesh):
    return jax.shard_map(
        body,
        mesh=mesh,
        in_specs=(
            P("group", "ctx", "tp"),
            P("group", "ctx", "tp"),
            P(None, "tp"),
            P("tp", None),
            P("ctx", None, "tp"),
            P(),
            P(),
            P("ctx"),
        ),
        out_specs=P("group", "ctx", None),
        check_vma=False,
    )
```

profile of v0, /device:TPU:1, one launch (start us, length us, event | category | flops | bytes accessed | tf_op | source)
XLA Modules:
  0.0 265.5 jit_solution(4091695662875121649)
XLA Ops:
  6.5 0.7 all-gather.2.cloned.1.call-update
  7.3 0.7 broadcast_add_fusion.1
  8.0 0.7 reshape.203
  8.8 0.4 fusion.35
  9.3 56.1 %all-gather.2.cloned.1.call-done = bf16[1,128,8192]{2,1,0:T(8,128)(2,1)} async-done(((bf16[1,128,512]{2,1,0:T(8,128)(2,1)}), bf16[1,128,8192]{2,1,0:T(8,128)(2,1)}) %all-gather.2.cloned.1.call-update) | async-done | bytes 2097168 | tf_op jit(solution)/shard_map/all_gather | solution.py:82
  65.4 2.5 fusion.27
  67.9 1.0 collective-permute-start
  69.1 0.2 add_reduce_fusion
  69.2 1.5 collective-permute-done
  71.0 0.2 convolution_convert_fusion
  71.1 0.8 all_to_all.6
  71.9 9.7 %all-to-all-start = ((bf16[16,2,2048]{2,1,0:T(2,128)(2,1)}), bf16[16,2,2048]{2,1,0:T(2,128)(2,1)S(1)}, u32[]{:S(2)}, u32[]{:S(2)}) async-start(bf16[16,2,2048]{2,1,0:T(2,128)(2,1)} %all_to_all.6), calls=%async_computation | async-start | bytes 262144 | tf_op jit(solution)/shard_map/all_to_all | solution.py:110
  81.9 21.9 %all_gather.7 = bf16[1024,256]{0,1:T(8,128)(2,1)S(1)} all-gather(bf16[128,256]{0,1:T(8,128)(2,1)S(1)} %pad_maximum_fusion), channel_id=1, replica_groups=mesh['group'=2,'ctx'=8,'tp'=16] {'ctx'}, dimensions={0}, use_global_device_ids=true | all-gather | bytes 589824 | tf_op jit(solution)/shard_map/all_gather | solution.py:95
  103.8 68.7 %conditional.1 = (bf16[128,256]{1,0:T(8,128)(2,1)S(1)}) conditional(s32[]{:T(128)} %convert_element_type.62, (s32[128]{0:T(128)S(1)}, bf16[128,128,256]{2,1,0:T(8,128)(2,1)}, s32[16]{0:T(128)S(1)}, s32[16]{0:T(128)S(1)}, s32[16]{0:T(128)S(1)}, /*index=5*/s32[]{:T(128)}, bf16[16,2,2048]{2,1,0:T(2,128)(2,1)S(1)}, ...), branch_computations={%region_3.7_spmd.clone, %region_7.10_spmd} | conditional | flops 136773248 | bytes 60571468 | solution.py:133
  103.8 13.5 %reshape.205 = bf16[2048,2048]{1,0:T(8,128)(2,1)} reshape(bf16[128,128,256]{2,1,0:T(8,128)(2,1)} %get-tuple-element.266) | data formatting | bytes 16777216 | tf_op jit(solution)/shard_map/reshape | solution.py:125
  117.4 9.1 %scatter_fusion = bf16[2048,2048]{1,0:T(8,128)(2,1)} fusion(bf16[2048,2048]{1,0:T(8,128)(2,1)} %reshape.205, s32[16]{0:T(128)S(1)} %compare_select_fusion, bf16[16,2048]{1,0:T(8,128)(2,1)S(1)} %reshape.218), kind=kCustom, calls=%fused_computation | custom fusion | bytes 196672 | tf_op jit(solution)/shard_map/cond/branch_0_fun/scatter | solution.py:46
  126.5 14.2 %reshape.206 = bf16[128,128,1,2,128]{4,3,1,0,2:T(2,128)(2,1)} reshape(bf16[2048,2048]{1,0:T(8,128)(2,1)} %scatter_fusion) | data formatting | bytes 16777216 | tf_op jit(solution)/shard_map/cond/branch_0_fun/reshape | solution.py:47
  140.8 19.9 %fusion.34 = (bf16[128,128,1,1,128]{4,3,1,0,2:T(2,128)(2,1)}, bf16[128,128,1,1,128]{4,3,1,0,2:T(2,128)(2,1)}) fusion(bf16[128,128,1,2,128]{4,3,1,0,2:T(2,128)(2,1)} %reshape.206), kind=kLoop, calls=%fused_computation.73 | loop fusion | bytes 16777216 | tf_op jit(solution)/shard_map/cond/branch_0_fun/slice | solution.py:51
  161.0 0.3 fusion.18
  161.4 5.7 %select_reduce_fusion.1 = (f32[128,2]{1,0:T(8,128)S(1)}, f32[128,128,2]{1,2,0:T(2,128)S(1)}) fusion(pred[128,128]{1,0:T(8,128)(4,1)S(1)} %iota_compare_fusion.1, bf16[128,1,2,128]{3,2,0,1:T(2,128)(2,1)S(1)} %copy.85, bf16[128,128,1,1,128]{4,3,1,0,2:T(2,128)(2,1)} %get-tuple-element.350), kind=kOutput, calls=%fused_computation.31 | convolution fusion | flops 8486656 | bytes 4408320 | tf_op jit(solution)/shard_map/cond/branch_0_fun/icgd,itcd->icgt/dot_general | solution.py:50
  167.1 0.4 bitcast_reduce_fusion
  167.6 4.6 %fusion.17 = bf16[128,2,128]{2,1,0:T(2,128)(2,1)S(1)} fusion(bf16[128,128,1,1,128]{4,3,1,0,2:T(2,128)(2,1)} %get-tuple-element.351, f32[128,2]{1,0:T(8,128)S(1)} %get-tuple-element.353, f32[128,128]{1,0:T(8,128)S(1)} %copy.78, f32[128,2]{1,0:T(8,128)S(1)} %get-tuple-element.352, f32[128,128,2]{1,2,0:T(2,128)S(1)} %get-tuple-element.357, ...), kind=kOutput, calls=%fused_computation.27 | convolution fusion | flops 8617984 | bytes 4475904 | tf_op jit(solution)/shard_map/cond/branch_0_fun/icgt,itcd->icgd/dot_general | solution.py:61
  172.5 4.8 %fusion.36 = f32[128,8192]{1,0:T(8,128)} fusion(bf16[128,256]{1,0:T(8,128)(2,1)S(1)} %get-tuple-element.360, bf16[256,8192]{1,0:T(8,128)(2,1)} %param.13), kind=kOutput, calls=%fused_computation.75 | convolution fusion | flops 536870912 | bytes 8454144 | tf_op jit(solution)/shard_map/dot_general | solution.py:134
  177.4 81.3 %all-reduce.1 = bf16[128,8192]{1,0:T(8,128)(2,1)} all-reduce(f32[128,8192]{1,0:T(8,128)} %fusion.36), channel_id=1, replica_groups=mesh['group'=2,'ctx'=8,'tp'=16] {'tp'}, use_global_device_ids=true, to_apply=%region_10.11 | all-reduce | flops 1048576 | bytes 6291456 | tf_op jit(solution)/shard_map/psum | solution.py:135
  (33 shorter events, 1.4 us)
Async XLA Ops:
  6.5 58.9 %copy-start = (bf16[8192,128]{1,0:T(8,128)(2,1)S(1)}, bf16[8192,128]{1,0:T(8,128)(2,1)}, u32[]{:S(2)}) copy-start(bf16[8192,128]{1,0:T(8,128)(2,1)} %param.12) | copy-start | bytes 6291460
  6.5 75.2 %copy-start.1 = (bf16[1,128,256]{2,1,0:T(8,128)(2,1)S(1)}, bf16[1,128,256]{2,1,0:T(8,128)(2,1)}, u32[]{:S(2)}) copy-start(bf16[1,128,256]{2,1,0:T(8,128)(2,1)} %param.11) | copy-start | bytes 196612
  6.5 97.3 %copy-start.2 = (s32[128]{0:T(128)S(1)}, s32[128]{0:T(128)}, u32[]{:S(2)}) copy-start(s32[128]{0:T(128)} %param.17) | copy-start | bytes 1540
  6.5 58.9 %all-gather.2.cloned.1.call-start = ((), (), s32[]{:S(2)}) async-start(), calls=%async_computation.1 | async-start | bytes 2228224 | tf_op jit(solution)/shard_map/all_gather | solution.py:82
  67.9 2.9 %collective-permute-start = (bf16[128,128]{0,1:T(8,128)(2,1)S(1)}, bf16[128,128]{0,1:T(8,128)(2,1)S(1)}, u32[]{:S(2)}, u32[]{:S(2)}) collective-permute-start(bf16[128,128]{0,1:T(8,128)(2,1)S(1)} %fusion.27), channel_id=1, source_target_pairs={{0,1},{1,0},{2,3},{3,2},{4,5},{5,4},{6,7},{7,6},{8,9},{9,8},{10,11... | collective-permute-start | bytes 98312 | tf_op jit(solution)/shard_map/ppermute | solution.py:18
  71.9 31.9 %all-to-all-start = ((bf16[16,2,2048]{2,1,0:T(2,128)(2,1)}), bf16[16,2,2048]{2,1,0:T(2,128)(2,1)S(1)}, u32[]{:S(2)}, u32[]{:S(2)}) async-start(bf16[16,2,2048]{2,1,0:T(2,128)(2,1)} %all_to_all.6), calls=%async_computation | async-start | bytes 262144 | tf_op jit(solution)/shard_map/all_to_all | solution.py:110
Sparse Core Ops, SparseCore 0:
  9.8 55.5 all-gather.1
where the time goes:
time: 266 us; the launch traced here: 265 us
  blocking collectives  103 us (39%)
  local copies, waits for them, and re-layouts  59.3 us (22%)
  waiting for transfers between devices  58.3 us (22%)
  matrix products  18.2 us (7%)
  between operations  13.5 us (5%)
  starting transfers between devices  10.7 us (4%)
    psum x1, blocking collectives, body(): combined = lax.psum(partial_out, 'tp').astype(jnp.bfloat16)  81.3 us
    all_gather x1, waiting for transfers between devices, body(): lax.all_gather(hidden, 'tp', axis=2, tiled=True)[0]  56.1 us
    all_gather x1, blocking collectives, body(): span_kv = lax.all_gather(local_kv, 'ctx', axis=0, tiled=True)  21.9 us
    slice x1, local copies, waits for them, and re-layouts, request_branch(): keyed[:, :, :, 0]  19.9 us
    reshape x1, local copies, waits for them, and re-layouts, request_branch(): keyed = filled.reshape(row_count, -1, copies, 2, HD)  14.2 us
    reshape x1, local copies, waits for them, and re-layouts, body(): cache_pages = cache.reshape(row_count * req_pages, page_width)  13.5 us
    all_to_all x1, starting transfers between devices, body(): lax.all_to_all(packed, ('group', 'ctx'), split_axis=0, concat_axis=0, til...  9.72 us
    scatter x1, local copies, waits for them, and re-layouts, request_branch(): filled = cache_pages.at[targets].set(arrived, mode='drop')  9.11 us
  transfers between devices with their start and end apart: 3, of which 2 were waited for; matrix products, arithmetic and copies ran while one was open for 1% of the time, Pallas kernels for 0%

commit v1 on v0

v1 whole, which is shorter than its diff:
```python
import jax
import jax.numpy as jnp
from jax import lax
from jax.experimental import pallas as pl
from jax.experimental.pallas import tpu as pltpu
from jax.sharding import PartitionSpec as P

HD = 128
PAGE = 8
SIDE = 4
RANKS = 16
NCTX = 8
ROWS = 128
WIDE = 512
BLOCK = 16
SCALE = HD ** -0.5
NEG = -1e30
VMEM = pl.BlockSpec(memory_space=pltpu.VMEM)
SMEM = pl.BlockSpec(memory_space=pltpu.SMEM)
ANY = pl.BlockSpec(memory_space=pl.ANY)
F32 = jnp.float32
BF16 = jnp.bfloat16


def rank_of(group, a, b):
    return SIDE * a + b if group == 0 else SIDE * b + a


def tp_route(step_a, step_b):
    route = []
    for group in range(2):
        for a in range(SIDE):
            for b in range(SIDE):
                to = rank_of(group, (a + step_a) % SIDE, (b + step_b) % SIDE)
                route.append((group * RANKS + rank_of(group, a, b), group * RANKS + to))
    return route


def shift(block, step_a, step_b):
    return lax.ppermute(block, ("group", "tp"), tp_route(step_a, step_b))


def routed(block, groups, target):
    route = []
    for group in groups:
        for c in range(NCTX):
            for t in range(RANKS):
                g2, c2, t2 = target(group, c, t)
                route.append(((group * NCTX + c) * RANKS + t, (g2 * NCTX + c2) * RANKS + t2))
    return lax.ppermute(block, ("group", "ctx", "tp"), route)


def chunk(info, a, b):
    a, b = lax.rem(a, SIDE), lax.rem(b, SIDE)
    return jnp.where(info[0] == 0, SIDE * a + b, SIDE * b + a)


def behind(info, k, j):
    return chunk(info, info[1] + SIDE - k, info[2] + SIDE - j)


def ahead(info, k, j):
    return chunk(info, info[1] + k, info[2] + j)


def nt(x, y):
    return lax.dot_general(x, y, (((1,), (1,)), ((), ())), preferred_element_type=F32)


def cache_kernel(info, q_ref, cache_ref, len_ref, req_ref, slot_ref, o_ref, m_ref, l_ref):
    @pl.when(info[0] == 1)
    def _():
        i = pl.program_id(0)
        rows = pl.ds(pl.multiple_of(i * BLOCK, BLOCK), BLOCK)
        q = q_ref[0, rows, :]
        q = jnp.concatenate([q[:, :HD], q[:, HD:]], axis=0)
        keys = cache_ref[:, :, :HD].reshape(BLOCK * HD, HD)
        values = cache_ref[:, :, HD:].reshape(BLOCK * HD, HD)
        wide = nt(keys, q).reshape(BLOCK, HD, 2 * BLOCK)
        shape = (BLOCK, HD, 2 * BLOCK)
        own = lax.broadcasted_iota(jnp.int32, shape, 0) == lax.rem(
            lax.broadcasted_iota(jnp.int32, shape, 2), BLOCK
        )
        scores = jnp.sum(jnp.where(own, wide, 0.0), axis=0).T * SCALE
        row_hit = (
            lax.broadcasted_iota(jnp.int32, (BLOCK, HD), 0) + i * BLOCK == req_ref[...]
        ).astype(BF16)
        col_hit = (
            lax.broadcasted_iota(jnp.int32, (HD, HD), 0) // PAGE == slot_ref[...]
        ).astype(BF16)
        filled = nt(row_hit, col_hit)
        position = lax.broadcasted_iota(jnp.int32, (BLOCK, HD), 1)
        open_ = jnp.where((position < len_ref[...]) & (filled < 0.5), 1.0, 0.0)
        allowed = jnp.concatenate([open_, open_], axis=0) > 0.5
        scores = jnp.where(allowed, scores, NEG)
        top = jnp.max(scores, axis=1, keepdims=True)
        weights = jnp.where(allowed, jnp.exp(scores - top), 0.0)
        total = jnp.sum(weights, axis=1, keepdims=True)
        spread = jnp.concatenate([weights] * BLOCK, axis=1)
        shape = (2 * BLOCK, BLOCK * HD)
        own = (
            lax.rem(lax.broadcasted_iota(jnp.int32, shape, 0), BLOCK)
            == lax.broadcasted_iota(jnp.int32, shape, 1) // HD
        )
        spread = jnp.where(own, spread, 0.0).astype(BF16)
        summed = jnp.dot(spread, values, preferred_element_type=F32)
        for h in range(2):
            part = slice(h * BLOCK, (h + 1) * BLOCK)
            o_ref[h] = summed[part]
            m_ref[h] = jnp.broadcast_to(top[part], (BLOCK, HD))
            l_ref[h] = jnp.broadcast_to(total[part], (BLOCK, HD))


def cache_attention(info, queries, cache, lens, req, slot):
    steps = ROWS // BLOCK
    whole = lambda *shape: pl.BlockSpec(shape, lambda i, info: (0,) * len(shape))
    out = pl.BlockSpec((2, BLOCK, HD), lambda i, info: (0, i, 0))
    return pl.pallas_call(
        cache_kernel,
        grid_spec=pltpu.PrefetchScalarGridSpec(
            num_scalar_prefetch=1,
            grid=(steps,),
            in_specs=[
                whole(1, ROWS, 2 * HD),
                pl.BlockSpec((BLOCK, HD, 2 * HD), lambda i, info: (i * info[0], 0, 0)),
                pl.BlockSpec((BLOCK, HD), lambda i, info: (i, 0)),
                whole(1, HD),
                whole(1, HD),
            ],
            out_specs=[out] * 3,
        ),
        out_shape=[jax.ShapeDtypeStruct((2, ROWS, HD), F32)] * 3,
        compiler_params=pltpu.CompilerParams(vmem_limit_bytes=16 << 20),
        cost_estimate=pl.CostEstimate(
            flops=2_000_000_000, bytes_accessed=9 << 20, transcendentals=1 << 16
        ),
        name="cache_attention",
    )(info, queries, cache, lens, req, slot)


def project_first(info, held_ref, w_ref, acc_ref):
    total = jnp.zeros((ROWS, HD), F32)
    for j in range(SIDE):
        start = pl.multiple_of(behind(info, 0, j) * WIDE, WIDE)
        total += jnp.dot(held_ref[j], w_ref[pl.ds(start, WIDE), :], preferred_element_type=F32)
    acc_ref[...] = total


def project_rest(info, acc_ref, r1_ref, r2_ref, r3_ref, w_ref, kv_ref):
    total = acc_ref[...]
    for k, ref in ((1, r1_ref), (2, r2_ref), (3, r3_ref)):
        for j in range(SIDE):
            start = pl.multiple_of(behind(info, k, j) * WIDE, WIDE)
            total += jnp.dot(ref[j], w_ref[pl.ds(start, WIDE), :], preferred_element_type=F32)
    kv_ref[...] = total.astype(BF16)


def pair_kernel(info, own_ref, partner_ref, near_ref, cross_ref, x_ref):
    @pl.when(info[4] == 0)
    def _():
        x_ref[0] = own_ref[...]
        x_ref[1] = partner_ref[...]
        x_ref[2] = near_ref[...]
        x_ref[3] = cross_ref[...]

    @pl.when(info[4] == 1)
    def _():
        x_ref[0] = partner_ref[...]
        x_ref[1] = own_ref[...]
        x_ref[2] = cross_ref[...]
        x_ref[3] = near_ref[...]


def block_ctx(info, n):
    base = lax.rem(info[3] + NCTX - 2 * (n // 2), NCTX)
    return base if n % 2 == 0 else base + 1 - 2 * lax.rem(base, 2)


def span_kernel(info, q_ref, x0_ref, x1_ref, x2_ref, x3_ref, out_ref):
    @pl.when(info[0] == 0)
    def _():
        refs = (x0_ref, x1_ref, x2_ref, x3_ref)
        keys = [refs[n // 2][2 * (n % 2)] for n in range(NCTX)]
        values = [refs[n // 2][2 * (n % 2) + 1] for n in range(NCTX)]
        row = lax.broadcasted_iota(jnp.int32, (ROWS, HD), 0)
        col = lax.broadcasted_iota(jnp.int32, (ROWS, HD), 1)
        offset = row - col
        limits = [(block_ctx(info, n) - info[3]) * ROWS for n in range(NCTX)]
        for h in range(2):
            q = q_ref[0, :, h * HD : (h + 1) * HD]
            scores = [
                jnp.where(offset >= limits[n], nt(q, keys[n]) * SCALE, NEG)
                for n in range(NCTX)
            ]
            top = scores[0]
            for s in scores[1:]:
                top = jnp.maximum(top, s)
            top = jnp.max(top, axis=1, keepdims=True)
            total = jnp.zeros((ROWS, HD), F32)
            summed = jnp.zeros((ROWS, HD), F32)
            for n in range(NCTX):
                w = jnp.where(offset >= limits[n], jnp.exp(scores[n] - top), 0.0)
                total += w
                summed += jnp.dot(w.astype(BF16), values[n], preferred_element_type=F32)
            total = jnp.sum(total, axis=1, keepdims=True)
            out_ref[:, h * HD : (h + 1) * HD] = (summed / total).astype(BF16)


def finish_kernel(
    info, q_ref, x_ref, span_ref, own_ref, len_ref, req_ref, pos_ref, o_ref, m_ref, l_ref, w_ref,
    s0_ref, s1_ref, s2_ref, s3_ref, att_ref,
):
    @pl.when(info[0] == 0)
    def _():
        att_ref[...] = x_ref[...]

    @pl.when(info[0] == 1)
    def _():
        row = lax.broadcasted_iota(jnp.int32, (ROWS, HD), 0)
        allowed = []
        for n in range(NCTX):
            at = pl.ds(block_ctx(info, n), 1)
            allowed.append((req_ref[at, :] == row) & (pos_ref[at, :] < len_ref[...]))
        key_new = own_ref[0].astype(F32)
        value_new = own_ref[1].astype(F32)
        for h in range(2):
            q = q_ref[0, :, h * HD : (h + 1) * HD]
            scores = [
                jnp.where(allowed[n], nt(q, span_ref[2 * n]) * SCALE, NEG) for n in range(NCTX)
            ]
            fresh = jnp.sum(q.astype(F32) * key_new, axis=1, keepdims=True) * SCALE
            top = scores[0]
            for s in scores[1:]:
                top = jnp.maximum(top, s)
            top = jnp.max(top, axis=1, keepdims=True)
            top = jnp.maximum(jnp.maximum(top, fresh), m_ref[h])
            old = jnp.exp(m_ref[h] - top)
            new = jnp.exp(fresh - top)
            total = jnp.zeros((ROWS, HD), F32)
            summed = o_ref[h] * old + new.astype(BF16).astype(F32) * value_new
            for n in range(NCTX):
                w = jnp.where(allowed[n], jnp.exp(scores[n] - top), 0.0)
                total += w
                summed += jnp.dot(
                    w.astype(BF16), span_ref[2 * n + 1], preferred_element_type=F32
                )
            total = jnp.sum(total, axis=1, keepdims=True) + l_ref[h] * old + new
            att_ref[:, h * HD : (h + 1) * HD] = (summed / total).astype(BF16)

    att = att_ref[...]
    for k, ref in ((1, s1_ref), (3, s3_ref), (2, s2_ref), (0, s0_ref)):
        for j in range(SIDE):
            start = pl.multiple_of(ahead(info, k, j) * WIDE, WIDE)
            part = jnp.dot(att, w_ref[:, pl.ds(start, WIDE)], preferred_element_type=F32)
            ref[j] = part.astype(ref.dtype)


def sum_sets(s0_ref, r1_ref, r2_ref, r3_ref, u0_ref, u1_ref, u2_ref, u3_ref):
    for j, ref in enumerate((u0_ref, u1_ref, u2_ref, u3_ref)):
        total = s0_ref[j] + r1_ref[j].astype(F32) + r2_ref[j].astype(F32) + r3_ref[j].astype(F32)
        ref[...] = total.astype(ref.dtype)


def sum_chunks(u0_ref, r1_ref, r2_ref, r3_ref, out_ref):
    total = u0_ref[...] + r1_ref[...].astype(F32) + r2_ref[...].astype(F32) + r3_ref[...].astype(F32)
    out_ref[...] = total.astype(BF16)


def place_kernel(info, t0_ref, t1_ref, t2_ref, t3_ref, out_ref, sems):
    copies = []
    for k, ref in enumerate((t0_ref, t1_ref, t2_ref, t3_ref)):
        for j in range(SIDE):
            start = pl.multiple_of(behind(info, k, j) * WIDE, WIDE)
            copies.append(
                pltpu.make_async_copy(
                    ref.at[j], out_ref.at[:, pl.ds(start, WIDE)], sems.at[k * SIDE + j]
                )
            )
    for copy in copies:
        copy.start()
    for copy in copies:
        copy.wait()


def call(kernel, outs, in_specs, out_specs, flops, *args, scratch=(), limit=24 << 20):
    size = sum(x.size * x.dtype.itemsize for x in args)
    return pl.pallas_call(
        kernel,
        out_shape=outs,
        in_specs=in_specs,
        out_specs=out_specs,
        scratch_shapes=list(scratch),
        compiler_params=pltpu.CompilerParams(vmem_limit_bytes=limit),
        cost_estimate=pl.CostEstimate(flops=flops, bytes_accessed=size, transcendentals=0),
        name=kernel.__name__,
    )(*args)


def body(hidden, queries, kv_weight, out_weight, cache, page_owner, page_slot, cached_len):
    group = lax.axis_index("group")
    ctx = lax.axis_index("ctx")
    rank = lax.axis_index("tp")
    high, low = rank // SIDE, rank % SIDE
    a = jnp.where(group == 0, high, low)
    b = jnp.where(group == 0, low, high)
    info = jnp.stack([group, a, b, ctx, rank % 2]).astype(jnp.int32)
    st = jax.ShapeDtypeStruct

    h = hidden[0]
    near = [h] + [shift(h, 0, k) for k in range(1, SIDE)]
    held = jnp.stack(near)

    lens = jnp.broadcast_to(cached_len[:, None], (ROWS, HD))
    mine = page_owner == ctx
    req = jnp.where(mine, page_slot // PAGE, -1)
    slot = page_slot % PAGE
    tied, held = lax.optimization_barrier((queries, held))
    old = cache_attention(info, tied, cache, lens, req[None], slot[None])
    req_tok = jnp.repeat(req, PAGE).reshape(NCTX, ROWS)
    pos_tok = (slot[:, None] * PAGE + jnp.arange(PAGE)[None, :]).reshape(NCTX, ROWS)

    arrived = [shift(held, k, 0) for k in range(1, SIDE)]
    acc = call(
        project_first, st((ROWS, HD), F32), [SMEM, VMEM, VMEM], VMEM, 70_000_000,
        info, held, kv_weight,
    )
    acc, old = lax.optimization_barrier((acc, old))
    kv = call(
        project_rest, st((ROWS, HD), BF16), [SMEM] + [VMEM] * 5, VMEM, 200_000_000,
        info, acc, *arrived, kv_weight,
    )

    partner = routed(kv, (0, 1), lambda g, c, t: (g, c, t ^ 1))
    beside = routed(kv, (0,), lambda g, c, t: (g, c ^ 1, t))
    cross = routed(kv, (0,), lambda g, c, t: (g, c ^ 1, t ^ 1))
    x0 = call(
        pair_kernel, st((4, ROWS, HD), BF16), [SMEM] + [VMEM] * 4, VMEM, 1000,
        info, kv, partner, beside, cross,
    )
    xs = [x0] + [routed(x0, (0,), lambda g, c, t, k=k: (g, (c + k) % NCTX, t)) for k in (2, 4, 6)]
    span = routed(jnp.concatenate(xs), (0,), lambda g, c, t: (1, c, t))
    att = call(
        span_kernel, st((ROWS, 2 * HD), BF16), [SMEM] + [VMEM] * 5, VMEM, 200_000_000,
        info, queries, *xs,
    )
    sets = call(
        finish_kernel,
        [st((SIDE, ROWS, WIDE), F32)] + [st((SIDE, ROWS, WIDE), BF16)] * 3,
        [SMEM] + [VMEM] * 11, [VMEM] * 4, 800_000_000,
        info, queries, att, span, x0, lens, req_tok, pos_tok, *old, out_weight,
        scratch=[pltpu.VMEM((ROWS, 2 * HD), BF16)],
    )

    got = [shift(sets[k], k, 0) for k in range(1, SIDE)]
    sums = call(
        sum_sets, [st((ROWS, WIDE), F32)] + [st((ROWS, WIDE), BF16)] * 3,
        [VMEM] * 4, [VMEM] * 4, 1_000_000, sets[0], *got,
    )
    got = [shift(sums[k], 0, k) for k in range(1, SIDE)]
    done = call(
        sum_chunks, st((ROWS, WIDE), BF16), [VMEM] * 4, VMEM, 1_000_000, sums[0], *got
    )
    line = jnp.stack([done] + [shift(done, 0, k) for k in range(1, SIDE)])
    lines = [line] + [shift(line, k, 0) for k in range(1, SIDE)]
    out = call(
        place_kernel, st((ROWS, RANKS * WIDE), BF16), [SMEM] + [VMEM] * 4, ANY, 1000,
        info, *lines, scratch=[pltpu.SemaphoreType.DMA((RANKS,))],
    )
    return out[None]


def solution(mesh):
    return jax.shard_map(
        body,
        mesh=mesh,
        in_specs=(
            P("group", "ctx", "tp"),
            P("group", "ctx", "tp"),
            P(None, "tp"),
            P("tp", None),
            P("ctx", None, "tp"),
            P(),
            P(),
            P("ctx"),
        ),
        out_specs=P("group", "ctx", None),
        check_vma=False,
    )
```

time: 266 us -> 129 us (0.48)
  the two profiles are of different devices: /device:TPU:1 before, /device:TPU:32 now
where the time goes in v1:
time: 129 us; the launch traced here: 128 us
  waiting for transfers between devices  59.2 us (46%)
  starting transfers between devices  48.1 us (37%)
  local copies, waits for them, and re-layouts  9.42 us (7%)
  Pallas kernels  8.75 us (7%)
  other arithmetic  2.46 us (2%)
    ppermute x18, waiting for transfers between devices, shift(): return lax.ppermute(block, ('group', 'tp'), tp_route(step_a, step_b))  50.9 us
    ppermute x18, starting transfers between devices, shift(): return lax.ppermute(block, ('group', 'tp'), tp_route(step_a, step_b))  24.5 us
    ppermute x7, starting transfers between devices, routed(): return lax.ppermute(block, ('group', 'ctx', 'tp'), route)  23.7 us
    ppermute x7, waiting for transfers between devices, routed(): return lax.ppermute(block, ('group', 'ctx', 'tp'), route)  8.38 us
    unnamed x12, local copies, waits for them, and re-layouts  8 us
    pallas_call x8, Pallas kernels, call(): pl.pallas_call(kernel, out_shape=outs, in_specs=in_specs, out_specs=out_s...  7.96 us
  transfers between devices with their start and end apart: 25, of which 19 were waited for; matrix products, arithmetic and copies ran while one was open for 2% of the time, Pallas kernels for 3%

profile of v1, /device:TPU:32, one launch (start us, length us, event | category | flops | bytes accessed | tf_op | source)
XLA Modules:
  0.0 128.4 jit_solution(4167250643817557722)
XLA Ops:
  0.0 2.8 %collective-permute-start.2 = (bf16[128,512]{1,0:T(8,128)(2,1)}, bf16[128,512]{1,0:T(8,128)(2,1)S(1)}, u32[]{:S(2)}, u32[]{:S(2)}) collective-permute-start(bf16[128,512]{1,0:T(8,128)(2,1)} %bitcast.19), channel_id=1, source_target_pairs={{0,3},{1,0},{2,1},{3,2},{4,7},{5,4},{6,5},{7,6},{8,11},{9,8},{10,9... | collective-permute-start | bytes 393224 | tf_op jit(solution)/shard_map/ppermute | solution.py:40
  4.4 2.5 %collective-permute-done.2 = bf16[128,512]{1,0:T(8,128)(2,1)S(1)} collective-permute-done((bf16[128,512]{1,0:T(8,128)(2,1)}, bf16[128,512]{1,0:T(8,128)(2,1)S(1)}, u32[]{:S(2)}, u32[]{:S(2)}) %collective-permute-start.2) | collective-permute-done | bytes 131104 | tf_op jit(solution)/shard_map/ppermute | solution.py:40
  7.0 2.5 %collective-permute-done.1 = bf16[128,512]{1,0:T(8,128)(2,1)S(1)} collective-permute-done((bf16[128,512]{1,0:T(8,128)(2,1)}, bf16[128,512]{1,0:T(8,128)(2,1)S(1)}, u32[]{:S(2)}, u32[]{:S(2)}) %collective-permute-start.1) | collective-permute-done | bytes 131104 | tf_op jit(solution)/shard_map/ppermute | solution.py:40
  11.8 3.1 %collective-permute-start.5 = (bf16[4,128,512]{2,1,0:T(8,128)(2,1)S(1)}, bf16[4,128,512]{2,1,0:T(8,128)(2,1)S(1)}, u32[]{:S(2)}, u32[]{:S(2)}) collective-permute-start(bf16[4,128,512]{2,1,0:T(8,128)(2,1)S(1)} %pad_maximum_fusion.held_ref), channel_id=1, source_target_pairs={{0,12},{1,13},{2,14},{3,15},{4,0},{5,1},{6,2},{7,3},{8,4},{9,5},{1... | collective-permute-start | bytes 1572872 | tf_op jit(solution)/shard_map/ppermute | solution.py:40
  21.1 3.4 %copy-done = bf16[128,128,256]{2,1,0:T(8,128)(2,1)S(1)} copy-done((bf16[128,128,256]{2,1,0:T(8,128)(2,1)S(1)}, bf16[128,128,256]{2,1,0:T(8,128)(2,1)}, u32[]{:S(2)}) %copy-start) | copy-done | bytes 8388632
  27.2 4.0 %collective-permute-done.3.r1_ref = bf16[4,128,512]{2,1,0:T(8,128)(2,1)S(1)} collective-permute-done((bf16[4,128,512]{2,1,0:T(8,128)(2,1)S(1)}, bf16[4,128,512]{2,1,0:T(8,128)(2,1)S(1)}, u32[]{:S(2)}, u32[]{:S(2)}) %collective-permute-start.3) | collective-permute-done | bytes 524320 | tf_op jit(solution)/shard_map/ppermute | solution.py:40
  34.3 2.7 %collective-permute-start.7 = (bf16[128,128]{1,0:T(8,128)(2,1)S(1)}, bf16[128,128]{1,0:T(8,128)(2,1)S(1)}, u32[]{:S(2)}, u32[]{:S(2)}) collective-permute-start(bf16[128,128]{1,0:T(8,128)(2,1)S(1)} %project_rest.1.own_ref), channel_id=1, source_target_pairs={{0,16},{1,17},{2,18},{3,19},{4,20},{5,21},{6,22},{7,23},{8,24},{9,... | collective-permute-start | bytes 98312 | tf_op jit(solution)/shard_map/ppermute | solution.py:50
  37.0 2.8 %collective-permute-start.6 = (bf16[128,128]{1,0:T(8,128)(2,1)S(1)}, bf16[128,128]{1,0:T(8,128)(2,1)S(1)}, u32[]{:S(2)}, u32[]{:S(2)}) collective-permute-start(bf16[128,128]{1,0:T(8,128)(2,1)S(1)} %project_rest.1.own_ref), channel_id=1, source_target_pairs={{0,1},{1,0},{2,3},{3,2},{4,5},{5,4},{6,7},{7,6},{8,9},{9,8},{10,11... | collective-permute-start | bytes 98312 | tf_op jit(solution)/shard_map/ppermute | solution.py:50
  42.2 7.3 %collective-permute-start.11 = (bf16[4,128,128]{2,1,0:T(8,128)(2,1)S(1)}, bf16[4,128,128]{2,1,0:T(8,128)(2,1)S(1)}, u32[]{:S(2)}, u32[]{:S(2)}) collective-permute-start(bf16[4,128,128]{2,1,0:T(8,128)(2,1)S(1)} %pair_kernel.1.x0_ref.own_ref), channel_id=1, source_target_pairs={{0,96},{1,97},{2,98},{3,99},{4,100},{5,101},{6,102},{7,103},{8,104... | collective-permute-start | bytes 393224 | tf_op jit(solution)/shard_map/ppermute | solution.py:50
  49.6 3.3 %collective-permute-start.10 = (bf16[4,128,128]{2,1,0:T(8,128)(2,1)S(1)}, bf16[4,128,128]{2,1,0:T(8,128)(2,1)S(1)}, u32[]{:S(2)}, u32[]{:S(2)}) collective-permute-start(bf16[4,128,128]{2,1,0:T(8,128)(2,1)S(1)} %pair_kernel.1.x0_ref.own_ref), channel_id=1, source_target_pairs={{0,64},{1,65},{2,66},{3,67},{4,68},{5,69},{6,70},{7,71},{8,72},{9,... | collective-permute-start | bytes 393224 | tf_op jit(solution)/shard_map/ppermute | solution.py:50
  52.9 4.3 %collective-permute-start.9 = (bf16[4,128,128]{2,1,0:T(8,128)(2,1)S(1)}, bf16[4,128,128]{2,1,0:T(8,128)(2,1)S(1)}, u32[]{:S(2)}, u32[]{:S(2)}) collective-permute-start(bf16[4,128,128]{2,1,0:T(8,128)(2,1)S(1)} %pair_kernel.1.x0_ref.own_ref), channel_id=1, source_target_pairs={{0,32},{1,33},{2,34},{3,35},{4,36},{5,37},{6,38},{7,39},{8,40},{9,... | collective-permute-start | bytes 393224 | tf_op jit(solution)/shard_map/ppermute | solution.py:50
  57.2 3.1 %collective-permute-done.10.x2_ref = bf16[4,128,128]{2,1,0:T(8,128)(2,1)S(1)} collective-permute-done((bf16[4,128,128]{2,1,0:T(8,128)(2,1)S(1)}, bf16[4,128,128]{2,1,0:T(8,128)(2,1)S(1)}, u32[]{:S(2)}, u32[]{:S(2)}) %collective-permute-start.10) | collective-permute-done | bytes 131104 | tf_op jit(solution)/shard_map/ppermute | solution.py:50
  60.3 3.4 %collective-permute-done.9.x1_ref = bf16[4,128,128]{2,1,0:T(8,128)(2,1)S(1)} collective-permute-done((bf16[4,128,128]{2,1,0:T(8,128)(2,1)S(1)}, bf16[4,128,128]{2,1,0:T(8,128)(2,1)S(1)}, u32[]{:S(2)}, u32[]{:S(2)}) %collective-permute-start.9) | collective-permute-done | bytes 131104 | tf_op jit(solution)/shard_map/ppermute | solution.py:50
  67.6 2.2 %copy-done.3 = bf16[256,8192]{1,0:T(8,128)(2,1)S(1)} copy-done((bf16[256,8192]{1,0:T(8,128)(2,1)S(1)}, bf16[256,8192]{1,0:T(8,128)(2,1)}, u32[]{:S(2)}) %copy-start.3) | copy-done | bytes 4194328
  71.2 2.1 %collective-permute-start.14 = (bf16[4,128,512]{2,1,0:T(8,128)(2,1)S(1)}, bf16[4,128,512]{2,1,0:T(8,128)(2,1)S(1)}, u32[]{:S(2)}, u32[]{:S(2)}) collective-permute-start(bf16[4,128,512]{2,1,0:T(8,128)(2,1)S(1)} %get-tuple-element.33), channel_id=1, source_target_pairs={{0,8},{1,9},{2,10},{3,11},{4,12},{5,13},{6,14},{7,15},{8,0},{9,1},... | collective-permute-start | bytes 1572872 | tf_op jit(solution)/shard_map/ppermute | solution.py:40
  74.4 12.7 %collective-permute-done.13.r1_ref = bf16[4,128,512]{2,1,0:T(8,128)(2,1)S(1)} collective-permute-done((bf16[4,128,512]{2,1,0:T(8,128)(2,1)S(1)}, bf16[4,128,512]{2,1,0:T(8,128)(2,1)S(1)}, u32[]{:S(2)}, u32[]{:S(2)}) %collective-permute-start.13) | collective-permute-done | bytes 524320 | tf_op jit(solution)/shard_map/ppermute | solution.py:40
  88.3 2.2 %collective-permute-start.16 = (bf16[128,512]{1,0:T(8,128)(2,1)S(1)}, bf16[128,512]{1,0:T(8,128)(2,1)S(1)}, u32[]{:S(2)}, u32[]{:S(2)}) collective-permute-start(bf16[128,512]{1,0:T(8,128)(2,1)S(1)} %get-tuple-element.36), channel_id=1, source_target_pairs={{0,1},{1,2},{2,3},{3,0},{4,5},{5,6},{6,7},{7,4},{8,9},{9,10},{10,1... | collective-permute-start | bytes 393224 | tf_op jit(solution)/shard_map/ppermute | solution.py:40
  94.8 2.2 %collective-permute-done.17.r2_ref = bf16[128,512]{1,0:T(8,128)(2,1)S(1)} collective-permute-done((bf16[128,512]{1,0:T(8,128)(2,1)S(1)}, bf16[128,512]{1,0:T(8,128)(2,1)S(1)}, u32[]{:S(2)}, u32[]{:S(2)}) %collective-permute-start.17) | collective-permute-done | bytes 131104 | tf_op jit(solution)/shard_map/ppermute | solution.py:40
  97.1 2.8 %collective-permute-start.21 = (bf16[128,512]{1,0:T(8,128)(2,1)S(1)}, bf16[128,512]{1,0:T(8,128)(2,1)S(1)}, u32[]{:S(2)}, u32[]{:S(2)}) collective-permute-start(bf16[128,512]{1,0:T(8,128)(2,1)S(1)} %sum_chunks.1), channel_id=1, source_target_pairs={{0,3},{1,0},{2,1},{3,2},{4,7},{5,4},{6,5},{7,6},{8,11},{9,8},{10,9... | collective-permute-start | bytes 393224 | tf_op jit(solution)/shard_map/ppermute | solution.py:40
  100.8 3.0 %collective-permute-done.21 = bf16[128,512]{1,0:T(8,128)(2,1)S(1)} collective-permute-done((bf16[128,512]{1,0:T(8,128)(2,1)S(1)}, bf16[128,512]{1,0:T(8,128)(2,1)S(1)}, u32[]{:S(2)}, u32[]{:S(2)}) %collective-permute-start.21) | collective-permute-done | bytes 131104 | tf_op jit(solution)/shard_map/ppermute | solution.py:40
  103.8 2.6 %collective-permute-done.20 = bf16[128,512]{1,0:T(8,128)(2,1)S(1)} collective-permute-done((bf16[128,512]{1,0:T(8,128)(2,1)S(1)}, bf16[128,512]{1,0:T(8,128)(2,1)S(1)}, u32[]{:S(2)}, u32[]{:S(2)}) %collective-permute-start.20) | collective-permute-done | bytes 131104 | tf_op jit(solution)/shard_map/ppermute | solution.py:40
  107.8 2.4 %collective-permute-start.24 = (bf16[4,128,512]{2,1,0:T(8,128)(2,1)S(1)}, bf16[4,128,512]{2,1,0:T(8,128)(2,1)S(1)}, u32[]{:S(2)}, u32[]{:S(2)}) collective-permute-start(bf16[4,128,512]{2,1,0:T(8,128)(2,1)S(1)} %pad_maximum_fusion.2.t0_ref), channel_id=1, source_target_pairs={{0,12},{1,13},{2,14},{3,15},{4,0},{5,1},{6,2},{7,3},{8,4},{9,5},{1... | collective-permute-start | bytes 1572872 | tf_op jit(solution)/shard_map/ppermute | solution.py:40
  111.2 11.4 %collective-permute-done.24.t3_ref = bf16[4,128,512]{2,1,0:T(8,128)(2,1)S(1)} collective-permute-done((bf16[4,128,512]{2,1,0:T(8,128)(2,1)S(1)}, bf16[4,128,512]{2,1,0:T(8,128)(2,1)S(1)}, u32[]{:S(2)}, u32[]{:S(2)}) %collective-permute-start.24) | collective-permute-done | bytes 524320 | tf_op jit(solution)/shard_map/ppermute | solution.py:40
  122.6 3.7 %collective-permute-done.22.t1_ref = bf16[4,128,512]{2,1,0:T(8,128)(2,1)S(1)} collective-permute-done((bf16[4,128,512]{2,1,0:T(8,128)(2,1)S(1)}, bf16[4,128,512]{2,1,0:T(8,128)(2,1)S(1)}, u32[]{:S(2)}, u32[]{:S(2)}) %collective-permute-start.22) | collective-permute-done | bytes 524320 | tf_op jit(solution)/shard_map/ppermute | solution.py:40
  (63 shorter events, 35.6 us)
Async XLA Ops:
  0.0 7.0 %collective-permute-start.2 = (bf16[128,512]{1,0:T(8,128)(2,1)}, bf16[128,512]{1,0:T(8,128)(2,1)S(1)}, u32[]{:S(2)}, u32[]{:S(2)}) collective-permute-start(bf16[128,512]{1,0:T(8,128)(2,1)} %bitcast.19), channel_id=1, source_target_pairs={{0,3},{1,0},{2,1},{3,2},{4,7},{5,4},{6,5},{7,6},{8,11},{9,8},{10,9... | collective-permute-start | bytes 393224 | tf_op jit(solution)/shard_map/ppermute | solution.py:40
  2.8 6.8 %collective-permute-start.1 = (bf16[128,512]{1,0:T(8,128)(2,1)}, bf16[128,512]{1,0:T(8,128)(2,1)S(1)}, u32[]{:S(2)}, u32[]{:S(2)}) collective-permute-start(bf16[128,512]{1,0:T(8,128)(2,1)} %bitcast.20), channel_id=1, source_target_pairs={{0,2},{1,3},{2,0},{3,1},{4,6},{5,7},{6,4},{7,5},{8,10},{9,11},{10,... | collective-permute-start | bytes 393224 | tf_op jit(solution)/shard_map/ppermute | solution.py:40
  3.6 7.3 %collective-permute-start = (bf16[128,512]{1,0:T(8,128)(2,1)}, bf16[128,512]{1,0:T(8,128)(2,1)S(1)}, u32[]{:S(2)}, u32[]{:S(2)}) collective-permute-start(bf16[128,512]{1,0:T(8,128)(2,1)} %bitcast.21), channel_id=1, source_target_pairs={{0,1},{1,2},{2,3},{3,0},{4,5},{5,6},{6,7},{7,4},{8,9},{9,10},{10,1... | collective-permute-start | bytes 393224 | tf_op jit(solution)/shard_map/ppermute | solution.py:40
  11.8 15.4 %collective-permute-start.5 = (bf16[4,128,512]{2,1,0:T(8,128)(2,1)S(1)}, bf16[4,128,512]{2,1,0:T(8,128)(2,1)S(1)}, u32[]{:S(2)}, u32[]{:S(2)}) collective-permute-start(bf16[4,128,512]{2,1,0:T(8,128)(2,1)S(1)} %pad_maximum_fusion.held_ref), channel_id=1, source_target_pairs={{0,12},{1,13},{2,14},{3,15},{4,0},{5,1},{6,2},{7,3},{8,4},{9,5},{1... | collective-permute-start | bytes 1572872 | tf_op jit(solution)/shard_map/ppermute | solution.py:40
  14.9 12.3 %collective-permute-start.4 = (bf16[4,128,512]{2,1,0:T(8,128)(2,1)S(1)}, bf16[4,128,512]{2,1,0:T(8,128)(2,1)S(1)}, u32[]{:S(2)}, u32[]{:S(2)}) collective-permute-start(bf16[4,128,512]{2,1,0:T(8,128)(2,1)S(1)} %pad_maximum_fusion.held_ref), channel_id=1, source_target_pairs={{0,8},{1,9},{2,10},{3,11},{4,12},{5,13},{6,14},{7,15},{8,0},{9,1},... | collective-permute-start | bytes 1572872 | tf_op jit(solution)/shard_map/ppermute | solution.py:40
  15.5 15.7 %collective-permute-start.3 = (bf16[4,128,512]{2,1,0:T(8,128)(2,1)S(1)}, bf16[4,128,512]{2,1,0:T(8,128)(2,1)S(1)}, u32[]{:S(2)}, u32[]{:S(2)}) collective-permute-start(bf16[4,128,512]{2,1,0:T(8,128)(2,1)S(1)} %pad_maximum_fusion.held_ref), channel_id=1, source_target_pairs={{0,4},{1,5},{2,6},{3,7},{4,8},{5,9},{6,10},{7,11},{8,12},{9,13},{1... | collective-permute-start | bytes 1572872 | tf_op jit(solution)/shard_map/ppermute | solution.py:40
  32.4 7.4 %collective-permute-start.8 = (bf16[128,128]{1,0:T(8,128)(2,1)S(1)}, bf16[128,128]{1,0:T(8,128)(2,1)S(1)}, u32[]{:S(2)}, u32[]{:S(2)}) collective-permute-start(bf16[128,128]{1,0:T(8,128)(2,1)S(1)} %project_rest.1.own_ref), channel_id=1, source_target_pairs={{0,17},{1,16},{2,19},{3,18},{4,21},{5,20},{6,23},{7,22},{8,25},{9,... | collective-permute-start | bytes 98312 | tf_op jit(solution)/shard_map/ppermute | solution.py:50
  34.3 5.8 %collective-permute-start.7 = (bf16[128,128]{1,0:T(8,128)(2,1)S(1)}, bf16[128,128]{1,0:T(8,128)(2,1)S(1)}, u32[]{:S(2)}, u32[]{:S(2)}) collective-permute-start(bf16[128,128]{1,0:T(8,128)(2,1)S(1)} %project_rest.1.own_ref), channel_id=1, source_target_pairs={{0,16},{1,17},{2,18},{3,19},{4,20},{5,21},{6,22},{7,23},{8,24},{9,... | collective-permute-start | bytes 98312 | tf_op jit(solution)/shard_map/ppermute | solution.py:50
  37.0 4.7 %collective-permute-start.6 = (bf16[128,128]{1,0:T(8,128)(2,1)S(1)}, bf16[128,128]{1,0:T(8,128)(2,1)S(1)}, u32[]{:S(2)}, u32[]{:S(2)}) collective-permute-start(bf16[128,128]{1,0:T(8,128)(2,1)S(1)} %project_rest.1.own_ref), channel_id=1, source_target_pairs={{0,1},{1,0},{2,3},{3,2},{4,5},{5,4},{6,7},{7,6},{8,9},{9,8},{10,11... | collective-permute-start | bytes 98312 | tf_op jit(solution)/shard_map/ppermute | solution.py:50
  42.2 15.0 %collective-permute-start.11 = (bf16[4,128,128]{2,1,0:T(8,128)(2,1)S(1)}, bf16[4,128,128]{2,1,0:T(8,128)(2,1)S(1)}, u32[]{:S(2)}, u32[]{:S(2)}) collective-permute-start(bf16[4,128,128]{2,1,0:T(8,128)(2,1)S(1)} %pair_kernel.1.x0_ref.own_ref), channel_id=1, source_target_pairs={{0,96},{1,97},{2,98},{3,99},{4,100},{5,101},{6,102},{7,103},{8,104... | collective-permute-start | bytes 393224 | tf_op jit(solution)/shard_map/ppermute | solution.py:50
  49.6 10.8 %collective-permute-start.10 = (bf16[4,128,128]{2,1,0:T(8,128)(2,1)S(1)}, bf16[4,128,128]{2,1,0:T(8,128)(2,1)S(1)}, u32[]{:S(2)}, u32[]{:S(2)}) collective-permute-start(bf16[4,128,128]{2,1,0:T(8,128)(2,1)S(1)} %pair_kernel.1.x0_ref.own_ref), channel_id=1, source_target_pairs={{0,64},{1,65},{2,66},{3,67},{4,68},{5,69},{6,70},{7,71},{8,72},{9,... | collective-permute-start | bytes 393224 | tf_op jit(solution)/shard_map/ppermute | solution.py:50
  52.9 10.8 %collective-permute-start.9 = (bf16[4,128,128]{2,1,0:T(8,128)(2,1)S(1)}, bf16[4,128,128]{2,1,0:T(8,128)(2,1)S(1)}, u32[]{:S(2)}, u32[]{:S(2)}) collective-permute-start(bf16[4,128,128]{2,1,0:T(8,128)(2,1)S(1)} %pair_kernel.1.x0_ref.own_ref), channel_id=1, source_target_pairs={{0,32},{1,33},{2,34},{3,35},{4,36},{5,37},{6,38},{7,39},{8,40},{9,... | collective-permute-start | bytes 393224 | tf_op jit(solution)/shard_map/ppermute | solution.py:50
  71.1 16.1 %collective-permute-start.13 = (bf16[4,128,512]{2,1,0:T(8,128)(2,1)S(1)}, bf16[4,128,512]{2,1,0:T(8,128)(2,1)S(1)}, u32[]{:S(2)}, u32[]{:S(2)}) collective-permute-start(bf16[4,128,512]{2,1,0:T(8,128)(2,1)S(1)} %get-tuple-element.32), channel_id=1, source_target_pairs={{0,4},{1,5},{2,6},{3,7},{4,8},{5,9},{6,10},{7,11},{8,12},{9,13},{1... | collective-permute-start | bytes 1572872 | tf_op jit(solution)/shard_map/ppermute | solution.py:40
  71.2 16.0 %collective-permute-start.14 = (bf16[4,128,512]{2,1,0:T(8,128)(2,1)S(1)}, bf16[4,128,512]{2,1,0:T(8,128)(2,1)S(1)}, u32[]{:S(2)}, u32[]{:S(2)}) collective-permute-start(bf16[4,128,512]{2,1,0:T(8,128)(2,1)S(1)} %get-tuple-element.33), channel_id=1, source_target_pairs={{0,8},{1,9},{2,10},{3,11},{4,12},{5,13},{6,14},{7,15},{8,0},{9,1},... | collective-permute-start | bytes 1572872 | tf_op jit(solution)/shard_map/ppermute | solution.py:40
  73.2 14.8 %collective-permute-start.15 = (bf16[4,128,512]{2,1,0:T(8,128)(2,1)S(1)}, bf16[4,128,512]{2,1,0:T(8,128)(2,1)S(1)}, u32[]{:S(2)}, u32[]{:S(2)}) collective-permute-start(bf16[4,128,512]{2,1,0:T(8,128)(2,1)S(1)} %get-tuple-element.34), channel_id=1, source_target_pairs={{0,12},{1,13},{2,14},{3,15},{4,0},{5,1},{6,2},{7,3},{8,4},{9,5},{1... | collective-permute-start | bytes 1572872 | tf_op jit(solution)/shard_map/ppermute | solution.py:40
  88.3 6.4 %collective-permute-start.16 = (bf16[128,512]{1,0:T(8,128)(2,1)S(1)}, bf16[128,512]{1,0:T(8,128)(2,1)S(1)}, u32[]{:S(2)}, u32[]{:S(2)}) collective-permute-start(bf16[128,512]{1,0:T(8,128)(2,1)S(1)} %get-tuple-element.36), channel_id=1, source_target_pairs={{0,1},{1,2},{2,3},{3,0},{4,5},{5,6},{6,7},{7,4},{8,9},{9,10},{10,1... | collective-permute-start | bytes 393224 | tf_op jit(solution)/shard_map/ppermute | solution.py:40
  90.5 6.5 %collective-permute-start.17 = (bf16[128,512]{1,0:T(8,128)(2,1)S(1)}, bf16[128,512]{1,0:T(8,128)(2,1)S(1)}, u32[]{:S(2)}, u32[]{:S(2)}) collective-permute-start(bf16[128,512]{1,0:T(8,128)(2,1)S(1)} %get-tuple-element.37), channel_id=1, source_target_pairs={{0,2},{1,3},{2,0},{3,1},{4,6},{5,7},{6,4},{7,5},{8,10},{9,11},{10,... | collective-permute-start | bytes 393224 | tf_op jit(solution)/shard_map/ppermute | solution.py:40
  91.3 5.7 %collective-permute-start.18 = (bf16[128,512]{1,0:T(8,128)(2,1)S(1)}, bf16[128,512]{1,0:T(8,128)(2,1)S(1)}, u32[]{:S(2)}, u32[]{:S(2)}) collective-permute-start(bf16[128,512]{1,0:T(8,128)(2,1)S(1)} %get-tuple-element.38), channel_id=1, source_target_pairs={{0,3},{1,0},{2,1},{3,2},{4,7},{5,4},{6,5},{7,6},{8,11},{9,8},{10,9... | collective-permute-start | bytes 393224 | tf_op jit(solution)/shard_map/ppermute | solution.py:40
  97.1 6.7 %collective-permute-start.21 = (bf16[128,512]{1,0:T(8,128)(2,1)S(1)}, bf16[128,512]{1,0:T(8,128)(2,1)S(1)}, u32[]{:S(2)}, u32[]{:S(2)}) collective-permute-start(bf16[128,512]{1,0:T(8,128)(2,1)S(1)} %sum_chunks.1), channel_id=1, source_target_pairs={{0,3},{1,0},{2,1},{3,2},{4,7},{5,4},{6,5},{7,6},{8,11},{9,8},{10,9... | collective-permute-start | bytes 393224 | tf_op jit(solution)/shard_map/ppermute | solution.py:40
  99.8 6.6 %collective-permute-start.20 = (bf16[128,512]{1,0:T(8,128)(2,1)S(1)}, bf16[128,512]{1,0:T(8,128)(2,1)S(1)}, u32[]{:S(2)}, u32[]{:S(2)}) collective-permute-start(bf16[128,512]{1,0:T(8,128)(2,1)S(1)} %sum_chunks.1), channel_id=1, source_target_pairs={{0,2},{1,3},{2,0},{3,1},{4,6},{5,7},{6,4},{7,5},{8,10},{9,11},{10,... | collective-permute-start | bytes 393224 | tf_op jit(solution)/shard_map/ppermute | solution.py:40
  100.7 7.0 %collective-permute-start.19 = (bf16[128,512]{1,0:T(8,128)(2,1)S(1)}, bf16[128,512]{1,0:T(8,128)(2,1)S(1)}, u32[]{:S(2)}, u32[]{:S(2)}) collective-permute-start(bf16[128,512]{1,0:T(8,128)(2,1)S(1)} %sum_chunks.1), channel_id=1, source_target_pairs={{0,1},{1,2},{2,3},{3,0},{4,5},{5,6},{6,7},{7,4},{8,9},{9,10},{10,1... | collective-permute-start | bytes 393224 | tf_op jit(solution)/shard_map/ppermute | solution.py:40
  107.8 14.8 %collective-permute-start.24 = (bf16[4,128,512]{2,1,0:T(8,128)(2,1)S(1)}, bf16[4,128,512]{2,1,0:T(8,128)(2,1)S(1)}, u32[]{:S(2)}, u32[]{:S(2)}) collective-permute-start(bf16[4,128,512]{2,1,0:T(8,128)(2,1)S(1)} %pad_maximum_fusion.2.t0_ref), channel_id=1, source_target_pairs={{0,12},{1,13},{2,14},{3,15},{4,0},{5,1},{6,2},{7,3},{8,4},{9,5},{1... | collective-permute-start | bytes 1572872 | tf_op jit(solution)/shard_map/ppermute | solution.py:40
  110.2 12.4 %collective-permute-start.23 = (bf16[4,128,512]{2,1,0:T(8,128)(2,1)S(1)}, bf16[4,128,512]{2,1,0:T(8,128)(2,1)S(1)}, u32[]{:S(2)}, u32[]{:S(2)}) collective-permute-start(bf16[4,128,512]{2,1,0:T(8,128)(2,1)S(1)} %pad_maximum_fusion.2.t0_ref), channel_id=1, source_target_pairs={{0,8},{1,9},{2,10},{3,11},{4,12},{5,13},{6,14},{7,15},{8,0},{9,1},... | collective-permute-start | bytes 1572872 | tf_op jit(solution)/shard_map/ppermute | solution.py:40
  110.2 16.0 %collective-permute-start.22 = (bf16[4,128,512]{2,1,0:T(8,128)(2,1)S(1)}, bf16[4,128,512]{2,1,0:T(8,128)(2,1)S(1)}, u32[]{:S(2)}, u32[]{:S(2)}) collective-permute-start(bf16[4,128,512]{2,1,0:T(8,128)(2,1)S(1)} %pad_maximum_fusion.2.t0_ref), channel_id=1, source_target_pairs={{0,4},{1,5},{2,6},{3,7},{4,8},{5,9},{6,10},{7,11},{8,12},{9,13},{1... | collective-permute-start | bytes 1572872 | tf_op jit(solution)/shard_map/ppermute | solution.py:40
  (7 other events, 57.2 us)

commit v2 on v1

v2 whole, which is shorter than its diff:
```python
import jax
import jax.numpy as jnp
from jax import lax
from jax.experimental import pallas as pl
from jax.experimental.pallas import tpu as pltpu
from jax.sharding import PartitionSpec as P

HD = 128
PAGE = 8
SIDE = 4
RANKS = 16
NCTX = 8
ROWS = 128
WIDE = 512
BLOCK = 16
HALF = 64
SCALE = HD ** -0.5
NEG = -1e30
VMEM = pl.BlockSpec(memory_space=pltpu.VMEM)
SMEM = pl.BlockSpec(memory_space=pltpu.SMEM)
HBM = pl.BlockSpec(memory_space=pltpu.HBM)
F32 = jnp.float32
BF16 = jnp.bfloat16


def rank_of(group, a, b):
    return SIDE * a + b if group == 0 else SIDE * b + a


def tp_route(step_a, step_b):
    route = []
    for group in range(2):
        for a in range(SIDE):
            for b in range(SIDE):
                to = rank_of(group, (a + step_a) % SIDE, (b + step_b) % SIDE)
                route.append((group * RANKS + rank_of(group, a, b), group * RANKS + to))
    return route


def shift(block, step_a, step_b):
    return lax.ppermute(block, ("group", "tp"), tp_route(step_a, step_b))


def routed(block, groups, target):
    route = []
    for group in groups:
        for c in range(NCTX):
            for t in range(RANKS):
                g2, c2, t2 = target(group, c, t)
                route.append(((group * NCTX + c) * RANKS + t, (g2 * NCTX + c2) * RANKS + t2))
    return lax.ppermute(block, ("group", "ctx", "tp"), route)


def chunk(info, a, b):
    a, b = lax.rem(a, SIDE), lax.rem(b, SIDE)
    return jnp.where(info[0] == 0, SIDE * a + b, SIDE * b + a)


def behind(info, k, j):
    return chunk(info, info[1] + SIDE - k, info[2] + SIDE - j)


def nt(x, y):
    return lax.dot_general(x, y, (((1,), (1,)), ((), ())), preferred_element_type=F32)


def relay(low, high, step):
    left_low = step(low, 1)
    right_high = step(high, -1)
    left_high = step(high, 1)
    right_low = step(low, -1)
    far_low = step(left_low, 1)
    far_high = step(right_high, -1)
    return left_low, left_high, right_low, right_high, far_low, far_high


def along_a(block, k):
    return shift(block, k, 0)


def along_b(block, k):
    return shift(block, 0, k)


def cache_kernel(
    info, q_ref, other_ref, cache_ref, len_ref, req_ref, slot_ref, out_ref, q_buf, buf, sems
):
    base = info[0] * HALF
    steps = HALF // BLOCK
    copies = [
        pltpu.make_async_copy(
            cache_ref.at[pl.ds(base + i * BLOCK, BLOCK)], buf.at[i], sems.at[i]
        )
        for i in range(steps)
    ]
    for copy in copies:
        copy.start()

    @pl.when(info[0] == 0)
    def _():
        q_buf[...] = other_ref[0, :HALF, :]

    @pl.when(info[0] == 1)
    def _():
        q_buf[...] = q_ref[0, HALF:, :]

    col_hit = (
        lax.broadcasted_iota(jnp.int32, (HD, HD), 0) // PAGE == slot_ref[...]
    ).astype(BF16)
    lens = len_ref[pl.ds(base, HALF), :]
    for i in range(steps):
        copies[i].wait()
        rows = slice(i * BLOCK, (i + 1) * BLOCK)
        q = q_buf[rows, :]
        q = jnp.concatenate([q[:, :HD], q[:, HD:]], axis=0)
        keys = buf[i, :, :, :HD].reshape(BLOCK * HD, HD)
        values = buf[i, :, :, HD:].reshape(BLOCK * HD, HD)
        wide = nt(keys, q).reshape(BLOCK, HD, 2 * BLOCK)
        shape = (BLOCK, HD, 2 * BLOCK)
        own = lax.broadcasted_iota(jnp.int32, shape, 0) == lax.rem(
            lax.broadcasted_iota(jnp.int32, shape, 2), BLOCK
        )
        scores = jnp.sum(jnp.where(own, wide, 0.0), axis=0).T * SCALE
        row_hit = (
            lax.broadcasted_iota(jnp.int32, (BLOCK, HD), 0) + base + i * BLOCK == req_ref[...]
        ).astype(BF16)
        filled = nt(row_hit, col_hit)
        position = lax.broadcasted_iota(jnp.int32, (BLOCK, HD), 1)
        open_ = jnp.where((position < lens[rows]) & (filled < 0.5), 1.0, 0.0)
        allowed = jnp.concatenate([open_, open_], axis=0) > 0.5
        scores = jnp.where(allowed, scores, NEG)
        top = jnp.max(scores, axis=1, keepdims=True)
        weights = jnp.where(allowed, jnp.exp(scores - top), 0.0)
        total = jnp.sum(weights, axis=1, keepdims=True)
        spread = jnp.concatenate([weights] * BLOCK, axis=1)
        shape = (2 * BLOCK, BLOCK * HD)
        own = (
            lax.rem(lax.broadcasted_iota(jnp.int32, shape, 0), BLOCK)
            == lax.broadcasted_iota(jnp.int32, shape, 1) // HD
        )
        spread = jnp.where(own, spread, 0.0).astype(BF16)
        summed = jnp.dot(spread, values, preferred_element_type=F32)
        lane = lax.broadcasted_iota(jnp.int32, (2 * BLOCK, HD), 1)
        stats = jnp.where(lane < HALF, top, total)
        for h in range(2):
            part = slice(h * BLOCK, (h + 1) * BLOCK)
            out_ref[0, h, rows, :] = summed[part]
            out_ref[1, h, rows, :] = stats[part]


def project_first(info, low_ref, high_ref, w_ref, acc_ref):
    total = jnp.zeros((ROWS, HD), F32)
    for j in range(SIDE):
        ref = (low_ref, high_ref)[j // 2]
        start = pl.multiple_of(behind(info, 0, j) * WIDE, WIDE)
        total += jnp.dot(ref[j % 2], w_ref[pl.ds(start, WIDE), :], preferred_element_type=F32)
    acc_ref[...] = total


def project_near(info, acc_ref, l0_ref, l1_ref, r0_ref, r1_ref, w_ref, out_ref):
    total = acc_ref[...]
    for k, refs in ((1, (l0_ref, l1_ref)), (3, (r0_ref, r1_ref))):
        for j in range(SIDE):
            start = pl.multiple_of(behind(info, k, j) * WIDE, WIDE)
            total += jnp.dot(
                refs[j // 2][j % 2], w_ref[pl.ds(start, WIDE), :], preferred_element_type=F32
            )
    out_ref[...] = total


def project_far(info, acc_ref, f0_ref, f1_ref, w_ref, kv_ref):
    total = acc_ref[...]
    for j in range(SIDE):
        ref = (f0_ref, f1_ref)[j // 2]
        start = pl.multiple_of(behind(info, 2, j) * WIDE, WIDE)
        total += jnp.dot(ref[j % 2], w_ref[pl.ds(start, WIDE), :], preferred_element_type=F32)
    kv_ref[...] = total.astype(BF16)


def pack_kernel(info, own_ref, pair_ref, swap_ref, cross_ref, span_ref, new_ref, half_ref):
    def put(ref, first, second):
        ref[0] = first[...]
        ref[1] = second[...]

    @pl.when(info[4] == 0)
    def _():
        put(new_ref, own_ref, pair_ref)

    @pl.when(info[4] == 1)
    def _():
        put(new_ref, pair_ref, own_ref)

    @pl.when(info[0] == 0)
    def _():
        span_ref[...] = new_ref[...]
        half_ref[...] = new_ref[0]

    @pl.when((info[0] == 1) & (info[4] == 0))
    def _():
        put(span_ref, swap_ref, cross_ref)
        half_ref[...] = cross_ref[...]

    @pl.when((info[0] == 1) & (info[4] == 1))
    def _():
        put(span_ref, cross_ref, swap_ref)
        half_ref[...] = swap_ref[...]


def attend(q, keys, values, allowed, start):
    scores = [jnp.where(m, nt(q, k[...]) * SCALE, NEG) for m, k in zip(allowed, keys)]
    top = scores[0]
    for s in scores[1:]:
        top = jnp.maximum(top, s)
    top = jnp.max(top, axis=1, keepdims=True)
    top, total, summed = start(top)
    sums = jnp.zeros((ROWS, HD), F32)
    for s, m, v in zip(scores, allowed, values):
        w = jnp.where(m, jnp.exp(s - top), 0.0)
        sums += w
        summed += jnp.dot(w.astype(BF16), v[...], preferred_element_type=F32)
    total += jnp.sum(sums, axis=1, keepdims=True)
    return (summed / total).astype(BF16)


def finish_kernel(
    info, q_ref, span_ref, new_ref, z1_ref, z2_ref, z3_ref, z4_ref, r1_ref, r2_ref, r3_ref, r4_ref,
    len_ref, req_ref, pos_ref, mine_ref, theirs_ref, w_ref,
    s0_ref, s1l_ref, s1h_ref, s2l_ref, s2h_ref, s3l_ref, s3h_ref, att_ref, w_buf, sems,
):
    order = [(k, j) for k in (2, 1, 3, 0) for j in range(SIDE)]
    copies = []
    for n, (k, j) in enumerate(order):
        start = pl.multiple_of(chunk(info, info[1] + k, j) * WIDE, WIDE)
        copies.append(
            pltpu.make_async_copy(w_ref.at[:, pl.ds(start, WIDE)], w_buf.at[n], sems.at[n])
        )
        copies[-1].start()
    row = lax.broadcasted_iota(jnp.int32, (ROWS, HD), 0)
    col = lax.broadcasted_iota(jnp.int32, (ROWS, HD), 1)
    ctx = info[3]
    near = [(z1_ref, r1_ref), (z2_ref, r2_ref), (z3_ref, r3_ref)]

    @pl.when(info[0] == 0)
    def _():
        places = [lax.rem(ctx + NCTX - k, NCTX) for k in range(5)]
        places += [lax.rem(ctx + k, NCTX) for k in range(1, 4)]
        refs = [span_ref] + [z for z, _ in near] + [None] + [r for _, r in near]
        keys = [z4_ref if r is None else r.at[0] for r in refs]
        values = [r4_ref if r is None else r.at[1] for r in refs]
        allowed = [row - col >= (p - ctx) * ROWS for p in places]
        zero = jnp.zeros((ROWS, HD), F32)
        for h in range(2):
            lanes = slice(h * HD, (h + 1) * HD)
            att_ref[:, lanes] = attend(
                q_ref[0, :, lanes], keys, values, allowed, lambda top: (top, 0.0, zero)
            )

    @pl.when(info[0] == 1)
    def _():
        places = [lax.rem(ctx + k, NCTX) for k in range(5)]
        places += [lax.rem(ctx + NCTX - k, NCTX) for k in range(1, 4)]
        refs = [span_ref] + [z for z, _ in near] + [None] + [r for _, r in near]
        keys = [r4_ref if r is None else r.at[0] for r in refs]
        values = [z4_ref if r is None else r.at[1] for r in refs]
        allowed = [
            (req_ref[pl.ds(p, 1), :] == row) & (pos_ref[pl.ds(p, 1), :] < len_ref[...])
            for p in places
        ]
        key_new = new_ref[0].astype(F32)
        value_new = new_ref[1].astype(F32)
        for h in range(2):
            lanes = slice(h * HD, (h + 1) * HD)
            q = q_ref[0, :, lanes]
            fresh = jnp.sum(q.astype(F32) * key_new, axis=1, keepdims=True) * SCALE
            summed = jnp.concatenate([theirs_ref[0, h], mine_ref[0, h]], axis=0)
            stats = jnp.concatenate([theirs_ref[1, h], mine_ref[1, h]], axis=0)
            highest, total = stats[:, :1], stats[:, HALF : HALF + 1]

            def start(top):
                top = jnp.maximum(jnp.maximum(top, fresh), highest)
                old = jnp.exp(highest - top)
                new = jnp.exp(fresh - top)
                rounded = new.astype(BF16).astype(F32)
                return top, total * old + new, summed * old + rounded * value_new

            att_ref[:, lanes] = attend(q, keys, values, allowed, start)

    att = att_ref[...]
    outs = {1: (s1l_ref, s1h_ref), 2: (s2l_ref, s2h_ref), 3: (s3l_ref, s3h_ref)}
    for n, (k, j) in enumerate(order):
        copies[n].wait()
        part = jnp.dot(att, w_buf[n], preferred_element_type=F32)
        if k == 0:
            s0_ref[j] = part
        else:
            outs[k][j // 2][j % 2] = part.astype(BF16)


def add_kernel(own_ref, got_ref, out_ref):
    out_ref[...] = (own_ref[...].astype(F32) + got_ref[...].astype(F32)).astype(BF16)


def fold_kernel(s0_ref, ll_ref, lh_ref, rl_ref, rh_ref, low_ref, high_ref):
    for n, (left, right, out) in enumerate(((ll_ref, rl_ref, low_ref), (lh_ref, rh_ref, high_ref))):
        total = s0_ref[2 * n : 2 * n + 2] + left[...].astype(F32) + right[...].astype(F32)
        out[...] = total.astype(BF16)


def line_kernel(
    low_ref, high_ref, ll_ref, lh_ref, rl_ref, rh_ref, fl_ref, fh_ref, out_low_ref, out_high_ref
):
    for own, far, left, right, out in (
        (low_ref, fl_ref, ll_ref, rl_ref, out_low_ref),
        (high_ref, fh_ref, lh_ref, rh_ref, out_high_ref),
    ):
        first = own[...].astype(F32) + far[...].astype(F32)
        second = left[...].astype(F32) + right[...].astype(F32)
        out[...] = (first + second).astype(BF16)


def place(info, sources, out_ref, sems):
    copies = []
    for k, low, high in sources:
        for j in range(SIDE):
            start = pl.multiple_of(chunk(info, info[1] + SIDE - k, j) * WIDE, WIDE)
            ref = (low, high)[j // 2].at[j % 2]
            copies.append(
                pltpu.make_async_copy(
                    ref, out_ref.at[:, pl.ds(start, WIDE)], sems.at[len(copies)]
                )
            )
            copies[-1].start()
    for copy in copies:
        copy.wait()


def place_near(info, tl_ref, th_ref, ll_ref, lh_ref, rl_ref, rh_ref, out_ref, sems):
    place(info, ((0, tl_ref, th_ref), (1, ll_ref, lh_ref), (3, rl_ref, rh_ref)), out_ref, sems)


def place_far(info, held_ref, fl_ref, fh_ref, out_ref, sems):
    place(info, ((2, fl_ref, fh_ref),), out_ref, sems)


def call(kernel, outs, in_specs, out_specs, flops, *args, scratch=(), limit=24 << 20, aliases=None):
    size = sum(x.size * x.dtype.itemsize for x in args)
    return pl.pallas_call(
        kernel,
        out_shape=outs,
        in_specs=in_specs,
        out_specs=out_specs,
        scratch_shapes=list(scratch),
        input_output_aliases=aliases or {},
        compiler_params=pltpu.CompilerParams(vmem_limit_bytes=limit),
        cost_estimate=pl.CostEstimate(flops=flops, bytes_accessed=size, transcendentals=0),
        name=kernel.__name__,
    )(*args)


def body(hidden, queries, kv_weight, out_weight, cache, page_owner, page_slot, cached_len):
    group = lax.axis_index("group")
    ctx = lax.axis_index("ctx")
    rank = lax.axis_index("tp")
    high, low = rank // SIDE, rank % SIDE
    a = jnp.where(group == 0, high, low)
    b = jnp.where(group == 0, low, high)
    info = jnp.stack([group, a, b, ctx, rank % 2]).astype(jnp.int32)
    st = jax.ShapeDtypeStruct
    dma = pltpu.SemaphoreType.DMA
    both = (0, 1)
    swap = lambda x: routed(x, both, lambda g, c, t: (1 - g, c, t))
    half = st((2, ROWS, WIDE), BF16)

    h = hidden[0]
    near = [h] + [shift(h, 0, k) for k in range(1, SIDE)]
    other_queries = swap(queries)
    held = (jnp.stack(near[:2]), jnp.stack(near[2:]))
    ll, lh, rl, rh, fl, fh = relay(*held, along_a)

    lens = jnp.broadcast_to(cached_len[:, None], (ROWS, HD))
    mine = page_owner == ctx
    req = jnp.where(mine, page_slot // PAGE, -1)
    slot = page_slot % PAGE
    req_tok = jnp.repeat(req, PAGE).reshape(NCTX, ROWS)
    pos_tok = (slot[:, None] * PAGE + jnp.arange(PAGE)[None, :]).reshape(NCTX, ROWS)

    acc = call(
        project_first, st((ROWS, HD), F32), [SMEM] + [VMEM] * 3, VMEM, 70_000_000,
        info, *held, kv_weight,
    )
    tied, ll, rh = lax.optimization_barrier((queries, ll, rh))
    old = call(
        cache_kernel, st((2, 2, HALF, HD), F32), [SMEM, VMEM, VMEM, HBM, VMEM, VMEM, VMEM], VMEM,
        1_000_000_000, info, tied, other_queries, cache, lens, req[None], slot[None],
        scratch=[
            pltpu.VMEM((HALF, 2 * HD), BF16),
            pltpu.VMEM((HALF // BLOCK, BLOCK, HD, 2 * HD), BF16),
            dma((HALF // BLOCK,)),
        ],
        limit=54 << 20,
    )
    acc = call(
        project_near, st((ROWS, HD), F32), [SMEM] + [VMEM] * 6, VMEM, 140_000_000,
        info, acc, ll, lh, rl, rh, kv_weight,
    )
    acc, old = lax.optimization_barrier((acc, old))
    other_old = swap(old)
    kv = call(
        project_far, st((ROWS, HD), BF16), [SMEM] + [VMEM] * 4, VMEM, 70_000_000,
        info, acc, fl, fh, kv_weight,
    )

    pair = routed(kv, both, lambda g, c, t: (g, c, t ^ 1))
    swapped = swap(kv)
    cross = routed(kv, both, lambda g, c, t: (1 - g, c, t ^ 1))
    span, new, part = call(
        pack_kernel, [st((2, ROWS, HD), BF16)] * 2 + [st((ROWS, HD), BF16)],
        [SMEM] + [VMEM] * 4, [VMEM] * 3, 1000, info, kv, pair, swapped, cross,
    )

    def along_z(block, k):
        return routed(
            block, both, lambda g, c, t: (g, (c + (k if g == 0 else NCTX - k)) % NCTX, t)
        )

    zs = [along_z(x, k) for k, x in ((1, span), (2, span), (3, span), (4, part))]
    rs = [swap(z) for z in zs]
    small = st((2, ROWS, WIDE), BF16)
    sets = call(
        finish_kernel, [st((SIDE, ROWS, WIDE), F32)] + [small] * 6,
        [SMEM] + [VMEM] * 16 + [HBM], [VMEM] * 7, 800_000_000,
        info, queries, span, new, *zs, *rs, lens, req_tok, pos_tok, old, other_old, out_weight,
        scratch=[
            pltpu.VMEM((ROWS, 2 * HD), BF16),
            pltpu.VMEM((RANKS, 2 * HD, WIDE), BF16),
            dma((RANKS,)),
        ],
    )
    s0, s1l, s1h, s2l, s2h, s3l, s3h = sets
    to_right = shift(s2l, 1, 0)
    to_left = shift(s2h, -1, 0)
    lh = shift(s1h, 1, 0)
    rl = shift(s3l, -1, 0)
    add = lambda x, y: call(add_kernel, small, [VMEM] * 2, VMEM, 1000, x, y)
    ll = shift(add(s1l, to_right), 1, 0)
    rh = shift(add(s3h, to_left), -1, 0)
    line = call(fold_kernel, [small] * 2, [VMEM] * 5, [VMEM] * 2, 1000, s0, ll, lh, rl, rh)
    line = call(
        line_kernel, [small] * 2, [VMEM] * 8, [VMEM] * 2, 1000, *line, *relay(*line, along_b)
    )
    ll, lh, rl, rh, fl, fh = relay(*line, along_a)
    whole = st((ROWS, RANKS * WIDE), BF16)
    out = call(
        place_near, whole, [SMEM] + [VMEM] * 6, HBM, 1000, info, *line, ll, lh, rl, rh,
        scratch=[dma((3 * SIDE,))],
    )
    out = call(
        place_far, whole, [SMEM, HBM, VMEM, VMEM], HBM, 1000, info, out, fl, fh,
        scratch=[dma((SIDE,))], aliases={1: 0},
    )
    return out[None]


def solution(mesh):
    return jax.shard_map(
        body,
        mesh=mesh,
        in_specs=(
            P("group", "ctx", "tp"),
            P("group", "ctx", "tp"),
            P(None, "tp"),
            P("tp", None),
            P("ctx", None, "tp"),
            P(),
            P(),
            P("ctx"),
        ),
        out_specs=P("group", "ctx", None),
        check_vma=False,
    )
```

time: 129 us -> 115 us (0.89)
  the two profiles are of different devices: /device:TPU:32 before, /device:TPU:6 now
where the time goes in v2:
time: 115 us
  starting transfers between devices  53 us (46%)
  waiting for transfers between devices  34.3 us (30%)
  Pallas kernels  18.3 us (16%)
  local copies, waits for them, and re-layouts  5.93 us (5%)
  other arithmetic  2.84 us (2%)
    ppermute x27, starting transfers between devices, shift(): return lax.ppermute(block, ('group', 'tp'), tp_route(step_a, step_b))  38.9 us
    ppermute x27, waiting for transfers between devices, shift(): return lax.ppermute(block, ('group', 'tp'), tp_route(step_a, step_b))  23.8 us
    pallas_call x12, Pallas kernels, call(): pl.pallas_call(kernel, out_shape=outs, in_specs=in_specs, out_specs=out_s...  18.3 us
    ppermute x13, starting transfers between devices, routed(): return lax.ppermute(block, ('group', 'ctx', 'tp'), route)  14.1 us
    ppermute x13, waiting for transfers between devices, routed(): return lax.ppermute(block, ('group', 'ctx', 'tp'), route)  10.5 us
    unnamed x22, local copies, waits for them, and re-layouts  4.53 us
  transfers between devices with their start and end apart: 40, of which 18 were waited for; matrix products, arithmetic and copies ran while one was open for 4% of the time, Pallas kernels for 8%

profile of v2, /device:TPU:6, one launch (start us, length us, event | category | flops | bytes accessed | tf_op | source)
XLA Modules:
  0.0 114.8 jit_solution(6502201087984561583)
XLA Ops:
  0.0 2.2 %collective-permute-start = (bf16[128,512]{1,0:T(8,128)(2,1)}, bf16[128,512]{1,0:T(8,128)(2,1)S(1)}, u32[]{:S(2)}, u32[]{:S(2)}) collective-permute-start(bf16[128,512]{1,0:T(8,128)(2,1)} %bitcast.13), channel_id=1, source_target_pairs={{0,1},{1,2},{2,3},{3,0},{4,5},{5,6},{6,7},{7,4},{8,9},{9,10},{10,1... | collective-permute-start | bytes 393224 | tf_op jit(solution)/shard_map/ppermute | solution.py:41
  7.8 2.2 %collective-permute-done.2 = bf16[128,512]{1,0:T(8,128)(2,1)S(1)} collective-permute-done((bf16[128,512]{1,0:T(8,128)(2,1)}, bf16[128,512]{1,0:T(8,128)(2,1)S(1)}, u32[]{:S(2)}, u32[]{:S(2)}) %collective-permute-start.2) | collective-permute-done | bytes 131104 | tf_op jit(solution)/shard_map/ppermute | solution.py:41
  16.5 2.9 %collective-permute-start.9 = (bf16[2,128,512]{2,1,0:T(8,128)(2,1)S(1)}, bf16[2,128,512]{2,1,0:T(8,128)(2,1)S(1)}, u32[]{:S(2)}, u32[]{:S(2)}) collective-permute-start(bf16[2,128,512]{2,1,0:T(8,128)(2,1)S(1)} %collective-permute-done.4.r1_ref), channel_id=1, source_target_pairs={{0,12},{1,13},{2,14},{3,15},{4,0},{5,1},{6,2},{7,3},{8,4},{9,5},{1... | collective-permute-start | bytes 786440 | tf_op jit(solution)/shard_map/ppermute | solution.py:41
  25.6 6.0 %cache_kernel.1.mine_ref = f32[2,2,64,128]{3,2,1,0:T(8,128)} custom-call(s32[5]{0:T(128)} %copy-done.6, bf16[1,128,256]{2,1,0:T(8,128)(2,1)} %q_ref.2, bf16[1,128,256]{2,1,0:T(8,128)(2,1)} %copy-done.8, bf16[128,128,256]{2,1,0:T(8,128)(2,1)} %cache_ref.1, s32[128,128]{1,0:T(8,128)} %broadcast_in_dim.26.len_ref, s32[1,128]{1,0:T(1,128)} %bitcast.19, ...), custom_call_target="tpu_custom_call" | custom-call | flops 1000000000 | bytes 8586260 | tf_op jit(solution)/shard_map/cache_kernel/pallas_call | solution.py:347
  32.6 2.0 %collective-permute-start.11 = (bf16[128,128]{1,0:T(8,128)(2,1)S(1)}, bf16[128,128]{1,0:T(8,128)(2,1)S(1)}, u32[]{:S(2)}, u32[]{:S(2)}) collective-permute-start(bf16[128,128]{1,0:T(8,128)(2,1)S(1)} %project_far.1.own_ref), channel_id=1, source_target_pairs={{0,128},{1,129},{2,130},{3,131},{4,132},{5,133},{6,134},{7,135},{8... | collective-permute-start | bytes 98312 | tf_op jit(solution)/shard_map/ppermute | solution.py:51
  36.0 2.6 %collective-permute-done.10.pair_ref = bf16[128,128]{1,0:T(8,128)(2,1)S(1)} collective-permute-done((bf16[128,128]{1,0:T(8,128)(2,1)S(1)}, bf16[128,128]{1,0:T(8,128)(2,1)S(1)}, u32[]{:S(2)}, u32[]{:S(2)}) %collective-permute-start.10) | collective-permute-done | bytes 32800 | tf_op jit(solution)/shard_map/ppermute | solution.py:51
  39.1 4.9 %collective-permute-start.15 = (bf16[2,128,128]{2,1,0:T(8,128)(2,1)S(1)}, bf16[2,128,128]{2,1,0:T(8,128)(2,1)S(1)}, u32[]{:S(2)}, u32[]{:S(2)}) collective-permute-start(bf16[2,128,128]{2,1,0:T(8,128)(2,1)S(1)} %get-tuple-element.28.span_ref), channel_id=1, source_target_pairs={{0,48},{1,49},{2,50},{3,51},{4,52},{5,53},{6,54},{7,55},{8,56},{9,... | collective-permute-start | bytes 196616 | tf_op jit(solution)/shard_map/ppermute | solution.py:51
  44.0 3.6 %collective-permute-start.14 = (bf16[2,128,128]{2,1,0:T(8,128)(2,1)S(1)}, bf16[2,128,128]{2,1,0:T(8,128)(2,1)S(1)}, u32[]{:S(2)}, u32[]{:S(2)}) collective-permute-start(bf16[2,128,128]{2,1,0:T(8,128)(2,1)S(1)} %get-tuple-element.28.span_ref), channel_id=1, source_target_pairs={{0,32},{1,33},{2,34},{3,35},{4,36},{5,37},{6,38},{7,39},{8,40},{9,... | collective-permute-start | bytes 196616 | tf_op jit(solution)/shard_map/ppermute | solution.py:51
  50.4 6.1 %collective-permute-done.16.z4_ref = bf16[128,128]{1,0:T(8,128)(2,1)S(1)} collective-permute-done((bf16[128,128]{1,0:T(8,128)(2,1)S(1)}, bf16[128,128]{1,0:T(8,128)(2,1)S(1)}, u32[]{:S(2)}, u32[]{:S(2)}) %collective-permute-start.16) | collective-permute-done | bytes 32800 | tf_op jit(solution)/shard_map/ppermute | solution.py:51
  58.4 2.2 %copy-done.2 = bf16[256,8192]{1,0:T(8,128)(2,1)S(1)} copy-done((bf16[256,8192]{1,0:T(8,128)(2,1)S(1)}, bf16[256,8192]{1,0:T(8,128)(2,1)}, u32[]{:S(2)}) %copy-start.2) | copy-done | bytes 4194328
  60.6 5.4 %finish_kernel.1 = (f32[4,128,512]{2,1,0:T(8,128)S(1)}, bf16[2,128,512]{2,1,0:T(8,128)(2,1)S(1)}, bf16[2,128,512]{2,1,0:T(8,128)(2,1)S(1)}, bf16[2,128,512]{2,1,...) custom-call(s32[5]{0:T(128)S(1)} %copy-done.7, ...), custom_call_target="tpu_custom_call" | custom-call | flops 800000000 | bytes 5185556 | tf_op jit(solution)/shard_map/finish_kernel/pallas_call | solution.py:347
  66.1 3.2 %collective-permute-start.26 = (bf16[2,128,512]{2,1,0:T(8,128)(2,1)S(1)}, bf16[2,128,512]{2,1,0:T(8,128)(2,1)S(1)}, u32[]{:S(2)}, u32[]{:S(2)}) collective-permute-start(bf16[2,128,512]{2,1,0:T(8,128)(2,1)S(1)} %get-tuple-element.38), channel_id=1, source_target_pairs={{0,12},{1,13},{2,14},{3,15},{4,0},{5,1},{6,2},{7,3},{8,4},{9,5},{1... | collective-permute-start | bytes 786440 | tf_op jit(solution)/shard_map/ppermute | solution.py:41
  69.3 3.2 %collective-permute-start.25 = (bf16[2,128,512]{2,1,0:T(8,128)(2,1)S(1)}, bf16[2,128,512]{2,1,0:T(8,128)(2,1)S(1)}, u32[]{:S(2)}, u32[]{:S(2)}) collective-permute-start(bf16[2,128,512]{2,1,0:T(8,128)(2,1)S(1)} %get-tuple-element.36), channel_id=1, source_target_pairs={{0,12},{1,13},{2,14},{3,15},{4,0},{5,1},{6,2},{7,3},{8,4},{9,5},{1... | collective-permute-start | bytes 786440 | tf_op jit(solution)/shard_map/ppermute | solution.py:41
  74.1 3.3 %collective-permute-start.27 = (bf16[2,128,512]{2,1,0:T(8,128)(2,1)S(1)}, bf16[2,128,512]{2,1,0:T(8,128)(2,1)S(1)}, u32[]{:S(2)}, u32[]{:S(2)}) collective-permute-start(bf16[2,128,512]{2,1,0:T(8,128)(2,1)S(1)} %add_kernel.3), channel_id=1, source_target_pairs={{0,12},{1,13},{2,14},{3,15},{4,0},{5,1},{6,2},{7,3},{8,4},{9,5},{1... | collective-permute-start | bytes 786440 | tf_op jit(solution)/shard_map/ppermute | solution.py:41
  77.4 4.2 %collective-permute-done.23.ll_ref = bf16[2,128,512]{2,1,0:T(8,128)(2,1)S(1)} collective-permute-done((bf16[2,128,512]{2,1,0:T(8,128)(2,1)S(1)}, bf16[2,128,512]{2,1,0:T(8,128)(2,1)S(1)}, u32[]{:S(2)}, u32[]{:S(2)}) %collective-permute-start.23) | collective-permute-done | bytes 262176 | tf_op jit(solution)/shard_map/ppermute | solution.py:41
  82.0 1.9 %collective-permute-start.31 = (bf16[2,128,512]{2,1,0:T(8,128)(2,1)S(1)}, bf16[2,128,512]{2,1,0:T(8,128)(2,1)S(1)}, u32[]{:S(2)}, u32[]{:S(2)}) collective-permute-start(bf16[2,128,512]{2,1,0:T(8,128)(2,1)S(1)} %get-tuple-element.40.high_ref), channel_id=1, source_target_pairs={{0,3},{1,0},{2,1},{3,2},{4,7},{5,4},{6,5},{7,6},{8,11},{9,8},{10,9... | collective-permute-start | bytes 786440 | tf_op jit(solution)/shard_map/ppermute | solution.py:41
  84.0 3.1 %collective-permute-start.29 = (bf16[2,128,512]{2,1,0:T(8,128)(2,1)S(1)}, bf16[2,128,512]{2,1,0:T(8,128)(2,1)S(1)}, u32[]{:S(2)}, u32[]{:S(2)}) collective-permute-start(bf16[2,128,512]{2,1,0:T(8,128)(2,1)S(1)} %get-tuple-element.40.high_ref), channel_id=1, source_target_pairs={{0,1},{1,2},{2,3},{3,0},{4,5},{5,6},{6,7},{7,4},{8,9},{9,10},{10,1... | collective-permute-start | bytes 786440 | tf_op jit(solution)/shard_map/ppermute | solution.py:41
  90.3 2.1 %collective-permute-done.30.rl_ref = bf16[2,128,512]{2,1,0:T(8,128)(2,1)S(1)} collective-permute-done((bf16[2,128,512]{2,1,0:T(8,128)(2,1)S(1)}, bf16[2,128,512]{2,1,0:T(8,128)(2,1)S(1)}, u32[]{:S(2)}, u32[]{:S(2)}) %collective-permute-start.30) | collective-permute-done | bytes 262176 | tf_op jit(solution)/shard_map/ppermute | solution.py:41
  92.4 2.3 %collective-permute-done.32.fl_ref = bf16[2,128,512]{2,1,0:T(8,128)(2,1)S(1)} collective-permute-done((bf16[2,128,512]{2,1,0:T(8,128)(2,1)S(1)}, bf16[2,128,512]{2,1,0:T(8,128)(2,1)S(1)}, u32[]{:S(2)}, u32[]{:S(2)}) %collective-permute-start.32) | collective-permute-done | bytes 262176 | tf_op jit(solution)/shard_map/ppermute | solution.py:41
  94.6 2.5 %collective-permute-done.33.fh_ref = bf16[2,128,512]{2,1,0:T(8,128)(2,1)S(1)} collective-permute-done((bf16[2,128,512]{2,1,0:T(8,128)(2,1)S(1)}, bf16[2,128,512]{2,1,0:T(8,128)(2,1)S(1)}, u32[]{:S(2)}, u32[]{:S(2)}) %collective-permute-start.33) | collective-permute-done | bytes 262176 | tf_op jit(solution)/shard_map/ppermute | solution.py:41
  97.5 3.5 %collective-permute-start.37 = (bf16[2,128,512]{2,1,0:T(8,128)(2,1)S(1)}, bf16[2,128,512]{2,1,0:T(8,128)(2,1)S(1)}, u32[]{:S(2)}, u32[]{:S(2)}) collective-permute-start(bf16[2,128,512]{2,1,0:T(8,128)(2,1)S(1)} %get-tuple-element.42.th_ref), channel_id=1, source_target_pairs={{0,12},{1,13},{2,14},{3,15},{4,0},{5,1},{6,2},{7,3},{8,4},{9,5},{1... | collective-permute-start | bytes 786440 | tf_op jit(solution)/shard_map/ppermute | solution.py:41
  100.9 1.9 %collective-permute-start.36 = (bf16[2,128,512]{2,1,0:T(8,128)(2,1)S(1)}, bf16[2,128,512]{2,1,0:T(8,128)(2,1)S(1)}, u32[]{:S(2)}, u32[]{:S(2)}) collective-permute-start(bf16[2,128,512]{2,1,0:T(8,128)(2,1)S(1)} %get-tuple-element.41.tl_ref), channel_id=1, source_target_pairs={{0,12},{1,13},{2,14},{3,15},{4,0},{5,1},{6,2},{7,3},{8,4},{9,5},{1... | collective-permute-start | bytes 786440 | tf_op jit(solution)/shard_map/ppermute | solution.py:41
  103.0 2.2 %collective-permute-done.34.ll_ref = bf16[2,128,512]{2,1,0:T(8,128)(2,1)S(1)} collective-permute-done((bf16[2,128,512]{2,1,0:T(8,128)(2,1)S(1)}, bf16[2,128,512]{2,1,0:T(8,128)(2,1)S(1)}, u32[]{:S(2)}, u32[]{:S(2)}) %collective-permute-start.34) | collective-permute-done | bytes 262176 | tf_op jit(solution)/shard_map/ppermute | solution.py:41
  105.2 3.3 %collective-permute-start.39 = (bf16[2,128,512]{2,1,0:T(8,128)(2,1)S(1)}, bf16[2,128,512]{2,1,0:T(8,128)(2,1)S(1)}, u32[]{:S(2)}, u32[]{:S(2)}) collective-permute-start(bf16[2,128,512]{2,1,0:T(8,128)(2,1)S(1)} %collective-permute-done.37.rh_ref), channel_id=1, source_target_pairs={{0,12},{1,13},{2,14},{3,15},{4,0},{5,1},{6,2},{7,3},{8,4},{9,5},{1... | collective-permute-start | bytes 786440 | tf_op jit(solution)/shard_map/ppermute | solution.py:41
  (105 shorter events, 37.5 us)
Async XLA Ops:
  2.2 7.8 %collective-permute-start.2 = (bf16[128,512]{1,0:T(8,128)(2,1)}, bf16[128,512]{1,0:T(8,128)(2,1)S(1)}, u32[]{:S(2)}, u32[]{:S(2)}) collective-permute-start(bf16[128,512]{1,0:T(8,128)(2,1)} %bitcast.14), channel_id=1, source_target_pairs={{0,3},{1,0},{2,1},{3,2},{4,7},{5,4},{6,5},{7,6},{8,11},{9,8},{10,9... | collective-permute-start | bytes 393224 | tf_op jit(solution)/shard_map/ppermute | solution.py:41
  2.2 7.8 %collective-permute-start.1 = (bf16[128,512]{1,0:T(8,128)(2,1)}, bf16[128,512]{1,0:T(8,128)(2,1)S(1)}, u32[]{:S(2)}, u32[]{:S(2)}) collective-permute-start(bf16[128,512]{1,0:T(8,128)(2,1)} %bitcast.15), channel_id=1, source_target_pairs={{0,2},{1,3},{2,0},{3,1},{4,6},{5,7},{6,4},{7,5},{8,10},{9,11},{10,... | collective-permute-start | bytes 393224 | tf_op jit(solution)/shard_map/ppermute | solution.py:41
  6.1 8.4 %collective-permute-start.3 = (bf16[2,128,512]{2,1,0:T(8,128)(2,1)S(1)}, bf16[2,128,512]{2,1,0:T(8,128)(2,1)S(1)}, u32[]{:S(2)}, u32[]{:S(2)}) collective-permute-start(bf16[2,128,512]{2,1,0:T(8,128)(2,1)S(1)} %pad_maximum_fusion.low_ref), channel_id=1, source_target_pairs={{0,4},{1,5},{2,6},{3,7},{4,8},{5,9},{6,10},{7,11},{8,12},{9,13},{1... | collective-permute-start | bytes 786440 | tf_op jit(solution)/shard_map/ppermute | solution.py:41
  11.8 13.1 %collective-permute-start.7 = (bf16[1,128,256]{2,1,0:T(8,128)(2,1)}, bf16[1,128,256]{2,1,0:T(8,128)(2,1)S(1)}, u32[]{:S(2)}, u32[]{:S(2)}) collective-permute-start(bf16[1,128,256]{2,1,0:T(8,128)(2,1)} %q_ref.2), channel_id=1, source_target_pairs={{0,128},{1,129},{2,130},{3,131},{4,132},{5,133},{6,134},{7,135},{8... | collective-permute-start | bytes 196616 | tf_op jit(solution)/shard_map/ppermute | solution.py:51
  11.8 11.3 %collective-permute-start.6 = (bf16[2,128,512]{2,1,0:T(8,128)(2,1)S(1)}, bf16[2,128,512]{2,1,0:T(8,128)(2,1)S(1)}, u32[]{:S(2)}, u32[]{:S(2)}) collective-permute-start(bf16[2,128,512]{2,1,0:T(8,128)(2,1)S(1)} %pad_maximum_fusion.low_ref), channel_id=1, source_target_pairs={{0,12},{1,13},{2,14},{3,15},{4,0},{5,1},{6,2},{7,3},{8,4},{9,5},{1... | collective-permute-start | bytes 786440 | tf_op jit(solution)/shard_map/ppermute | solution.py:41
  12.6 10.6 %collective-permute-start.5 = (bf16[2,128,512]{2,1,0:T(8,128)(2,1)S(1)}, bf16[2,128,512]{2,1,0:T(8,128)(2,1)S(1)}, u32[]{:S(2)}, u32[]{:S(2)}) collective-permute-start(bf16[2,128,512]{2,1,0:T(8,128)(2,1)S(1)} %pad_maximum_fusion.1.high_ref), channel_id=1, source_target_pairs={{0,4},{1,5},{2,6},{3,7},{4,8},{5,9},{6,10},{7,11},{8,12},{9,13},{1... | collective-permute-start | bytes 786440 | tf_op jit(solution)/shard_map/ppermute | solution.py:41
  14.5 17.1 %collective-permute-start.8 = (bf16[2,128,512]{2,1,0:T(8,128)(2,1)S(1)}, bf16[2,128,512]{2,1,0:T(8,128)(2,1)S(1)}, u32[]{:S(2)}, u32[]{:S(2)}) collective-permute-start(bf16[2,128,512]{2,1,0:T(8,128)(2,1)S(1)} %collective-permute-done.3.l0_ref), channel_id=1, source_target_pairs={{0,4},{1,5},{2,6},{3,7},{4,8},{5,9},{6,10},{7,11},{8,12},{9,13},{1... | collective-permute-start | bytes 786440 | tf_op jit(solution)/shard_map/ppermute | solution.py:41
  16.5 15.2 %collective-permute-start.9 = (bf16[2,128,512]{2,1,0:T(8,128)(2,1)S(1)}, bf16[2,128,512]{2,1,0:T(8,128)(2,1)S(1)}, u32[]{:S(2)}, u32[]{:S(2)}) collective-permute-start(bf16[2,128,512]{2,1,0:T(8,128)(2,1)S(1)} %collective-permute-done.4.r1_ref), channel_id=1, source_target_pairs={{0,12},{1,13},{2,14},{3,15},{4,0},{5,1},{6,2},{7,3},{8,4},{9,5},{1... | collective-permute-start | bytes 786440 | tf_op jit(solution)/shard_map/ppermute | solution.py:41
  39.1 17.3 %collective-permute-start.15 = (bf16[2,128,128]{2,1,0:T(8,128)(2,1)S(1)}, bf16[2,128,128]{2,1,0:T(8,128)(2,1)S(1)}, u32[]{:S(2)}, u32[]{:S(2)}) collective-permute-start(bf16[2,128,128]{2,1,0:T(8,128)(2,1)S(1)} %get-tuple-element.28.span_ref), channel_id=1, source_target_pairs={{0,48},{1,49},{2,50},{3,51},{4,52},{5,53},{6,54},{7,55},{8,56},{9,... | collective-permute-start | bytes 196616 | tf_op jit(solution)/shard_map/ppermute | solution.py:51
  44.0 12.9 %collective-permute-start.14 = (bf16[2,128,128]{2,1,0:T(8,128)(2,1)S(1)}, bf16[2,128,128]{2,1,0:T(8,128)(2,1)S(1)}, u32[]{:S(2)}, u32[]{:S(2)}) collective-permute-start(bf16[2,128,128]{2,1,0:T(8,128)(2,1)S(1)} %get-tuple-element.28.span_ref), channel_id=1, source_target_pairs={{0,32},{1,33},{2,34},{3,35},{4,36},{5,37},{6,38},{7,39},{8,40},{9,... | collective-permute-start | bytes 196616 | tf_op jit(solution)/shard_map/ppermute | solution.py:51
  47.6 9.5 %collective-permute-start.13 = (bf16[2,128,128]{2,1,0:T(8,128)(2,1)S(1)}, bf16[2,128,128]{2,1,0:T(8,128)(2,1)S(1)}, u32[]{:S(2)}, u32[]{:S(2)}) collective-permute-start(bf16[2,128,128]{2,1,0:T(8,128)(2,1)S(1)} %get-tuple-element.28.span_ref), channel_id=1, source_target_pairs={{0,16},{1,17},{2,18},{3,19},{4,20},{5,21},{6,22},{7,23},{8,24},{9,... | collective-permute-start | bytes 196616 | tf_op jit(solution)/shard_map/ppermute | solution.py:51
  48.6 7.8 %collective-permute-start.16 = (bf16[128,128]{1,0:T(8,128)(2,1)S(1)}, bf16[128,128]{1,0:T(8,128)(2,1)S(1)}, u32[]{:S(2)}, u32[]{:S(2)}) collective-permute-start(bf16[128,128]{1,0:T(8,128)(2,1)S(1)} %get-tuple-element.30), channel_id=1, source_target_pairs={{0,64},{1,65},{2,66},{3,67},{4,68},{5,69},{6,70},{7,71},{8,72},{9,... | collective-permute-start | bytes 98312 | tf_op jit(solution)/shard_map/ppermute | solution.py:51
  49.5 8.2 %collective-permute-start.21 = (f32[2,2,64,128]{3,2,1,0:T(8,128)S(1)}, f32[2,2,64,128]{3,2,1,0:T(8,128)S(1)}, u32[]{:S(2)}, u32[]{:S(2)}) collective-permute-start(f32[2,2,64,128]{3,2,1,0:T(8,128)S(1)} %copy-done.4), channel_id=1, source_target_pairs={{0,128},{1,129},{2,130},{3,131},{4,132},{5,133},{6,134},{7,135},{8... | collective-permute-start | bytes 393224 | tf_op jit(solution)/shard_map/ppermute | solution.py:51
  66.0 7.7 %collective-permute-start.22 = (bf16[2,128,512]{2,1,0:T(8,128)(2,1)S(1)}, bf16[2,128,512]{2,1,0:T(8,128)(2,1)S(1)}, u32[]{:S(2)}, u32[]{:S(2)}) collective-permute-start(bf16[2,128,512]{2,1,0:T(8,128)(2,1)S(1)} %get-tuple-element.34), channel_id=1, source_target_pairs={{0,4},{1,5},{2,6},{3,7},{4,8},{5,9},{6,10},{7,11},{8,12},{9,13},{1... | collective-permute-start | bytes 786440 | tf_op jit(solution)/shard_map/ppermute | solution.py:41
  66.1 7.9 %collective-permute-start.26 = (bf16[2,128,512]{2,1,0:T(8,128)(2,1)S(1)}, bf16[2,128,512]{2,1,0:T(8,128)(2,1)S(1)}, u32[]{:S(2)}, u32[]{:S(2)}) collective-permute-start(bf16[2,128,512]{2,1,0:T(8,128)(2,1)S(1)} %get-tuple-element.38), channel_id=1, source_target_pairs={{0,12},{1,13},{2,14},{3,15},{4,0},{5,1},{6,2},{7,3},{8,4},{9,5},{1... | collective-permute-start | bytes 786440 | tf_op jit(solution)/shard_map/ppermute | solution.py:41
  69.3 8.1 %collective-permute-start.24 = (bf16[2,128,512]{2,1,0:T(8,128)(2,1)S(1)}, bf16[2,128,512]{2,1,0:T(8,128)(2,1)S(1)}, u32[]{:S(2)}, u32[]{:S(2)}) collective-permute-start(bf16[2,128,512]{2,1,0:T(8,128)(2,1)S(1)} %get-tuple-element.35), channel_id=1, source_target_pairs={{0,4},{1,5},{2,6},{3,7},{4,8},{5,9},{6,10},{7,11},{8,12},{9,13},{1... | collective-permute-start | bytes 786440 | tf_op jit(solution)/shard_map/ppermute | solution.py:41
  69.3 8.1 %collective-permute-start.25 = (bf16[2,128,512]{2,1,0:T(8,128)(2,1)S(1)}, bf16[2,128,512]{2,1,0:T(8,128)(2,1)S(1)}, u32[]{:S(2)}, u32[]{:S(2)}) collective-permute-start(bf16[2,128,512]{2,1,0:T(8,128)(2,1)S(1)} %get-tuple-element.36), channel_id=1, source_target_pairs={{0,12},{1,13},{2,14},{3,15},{4,0},{5,1},{6,2},{7,3},{8,4},{9,5},{1... | collective-permute-start | bytes 786440 | tf_op jit(solution)/shard_map/ppermute | solution.py:41
  73.7 7.9 %collective-permute-start.23 = (bf16[2,128,512]{2,1,0:T(8,128)(2,1)S(1)}, bf16[2,128,512]{2,1,0:T(8,128)(2,1)S(1)}, u32[]{:S(2)}, u32[]{:S(2)}) collective-permute-start(bf16[2,128,512]{2,1,0:T(8,128)(2,1)S(1)} %add_kernel.2), channel_id=1, source_target_pairs={{0,4},{1,5},{2,6},{3,7},{4,8},{5,9},{6,10},{7,11},{8,12},{9,13},{1... | collective-permute-start | bytes 786440 | tf_op jit(solution)/shard_map/ppermute | solution.py:41
  83.9 8.5 %collective-permute-start.30 = (bf16[2,128,512]{2,1,0:T(8,128)(2,1)S(1)}, bf16[2,128,512]{2,1,0:T(8,128)(2,1)S(1)}, u32[]{:S(2)}, u32[]{:S(2)}) collective-permute-start(bf16[2,128,512]{2,1,0:T(8,128)(2,1)S(1)} %get-tuple-element.39.low_ref), channel_id=1, source_target_pairs={{0,3},{1,0},{2,1},{3,2},{4,7},{5,4},{6,5},{7,6},{8,11},{9,8},{10,9... | collective-permute-start | bytes 786440 | tf_op jit(solution)/shard_map/ppermute | solution.py:41
  84.0 8.3 %collective-permute-start.29 = (bf16[2,128,512]{2,1,0:T(8,128)(2,1)S(1)}, bf16[2,128,512]{2,1,0:T(8,128)(2,1)S(1)}, u32[]{:S(2)}, u32[]{:S(2)}) collective-permute-start(bf16[2,128,512]{2,1,0:T(8,128)(2,1)S(1)} %get-tuple-element.40.high_ref), channel_id=1, source_target_pairs={{0,1},{1,2},{2,3},{3,0},{4,5},{5,6},{6,7},{7,4},{8,9},{9,10},{10,1... | collective-permute-start | bytes 786440 | tf_op jit(solution)/shard_map/ppermute | solution.py:41
  97.4 7.8 %collective-permute-start.34 = (bf16[2,128,512]{2,1,0:T(8,128)(2,1)S(1)}, bf16[2,128,512]{2,1,0:T(8,128)(2,1)S(1)}, u32[]{:S(2)}, u32[]{:S(2)}) collective-permute-start(bf16[2,128,512]{2,1,0:T(8,128)(2,1)S(1)} %get-tuple-element.41.tl_ref), channel_id=1, source_target_pairs={{0,4},{1,5},{2,6},{3,7},{4,8},{5,9},{6,10},{7,11},{8,12},{9,13},{1... | collective-permute-start | bytes 786440 | tf_op jit(solution)/shard_map/ppermute | solution.py:41
  97.5 7.7 %collective-permute-start.37 = (bf16[2,128,512]{2,1,0:T(8,128)(2,1)S(1)}, bf16[2,128,512]{2,1,0:T(8,128)(2,1)S(1)}, u32[]{:S(2)}, u32[]{:S(2)}) collective-permute-start(bf16[2,128,512]{2,1,0:T(8,128)(2,1)S(1)} %get-tuple-element.42.th_ref), channel_id=1, source_target_pairs={{0,12},{1,13},{2,14},{3,15},{4,0},{5,1},{6,2},{7,3},{8,4},{9,5},{1... | collective-permute-start | bytes 786440 | tf_op jit(solution)/shard_map/ppermute | solution.py:41
  105.2 8.1 %collective-permute-start.38 = (bf16[2,128,512]{2,1,0:T(8,128)(2,1)S(1)}, bf16[2,128,512]{2,1,0:T(8,128)(2,1)S(1)}, u32[]{:S(2)}, u32[]{:S(2)}) collective-permute-start(bf16[2,128,512]{2,1,0:T(8,128)(2,1)S(1)} %collective-permute-done.34.ll_ref), channel_id=1, source_target_pairs={{0,4},{1,5},{2,6},{3,7},{4,8},{5,9},{6,10},{7,11},{8,12},{9,13},{1... | collective-permute-start | bytes 786440 | tf_op jit(solution)/shard_map/ppermute | solution.py:41
  105.2 8.1 %collective-permute-start.39 = (bf16[2,128,512]{2,1,0:T(8,128)(2,1)S(1)}, bf16[2,128,512]{2,1,0:T(8,128)(2,1)S(1)}, u32[]{:S(2)}, u32[]{:S(2)}) collective-permute-start(bf16[2,128,512]{2,1,0:T(8,128)(2,1)S(1)} %collective-permute-done.37.rh_ref), channel_id=1, source_target_pairs={{0,12},{1,13},{2,14},{3,15},{4,0},{5,1},{6,2},{7,3},{8,4},{9,5},{1... | collective-permute-start | bytes 786440 | tf_op jit(solution)/shard_map/ppermute | solution.py:41
  (27 other events, 192.0 us)

commit v3 on v2

--- a/solution.py
+++ b/solution.py
@@ -12,7 +12,8 @@
 NCTX = 8
 ROWS = 128
 WIDE = 512
-BLOCK = 16
+QUARTER = 2048
+BLOCK = 32
 HALF = 64
 SCALE = HD ** -0.5
 NEG = -1e30
@@ -87,14 +88,13 @@
 ):
     base = info[0] * HALF
     steps = HALF // BLOCK
-    copies = [
-        pltpu.make_async_copy(
-            cache_ref.at[pl.ds(base + i * BLOCK, BLOCK)], buf.at[i], sems.at[i]
-        )
-        for i in range(steps)
-    ]
-    for copy in copies:
-        copy.start()
+
+    def fetch(i):
+        start = pl.multiple_of(base + i * BLOCK, BLOCK)
+        return pltpu.make_async_copy(cache_ref.at[pl.ds(start, BLOCK)], buf.at[i], sems.at[i])
+
+    for i in range(steps):
+        fetch(i).start()
 
     @pl.when(info[0] == 0)
     def _():
@@ -107,45 +107,45 @@
     col_hit = (
         lax.broadcasted_iota(jnp.int32, (HD, HD), 0) // PAGE == slot_ref[...]
     ).astype(BF16)
-    lens = len_ref[pl.ds(base, HALF), :]
-    for i in range(steps):
-        copies[i].wait()
-        rows = slice(i * BLOCK, (i + 1) * BLOCK)
+    row_of = lax.rem(lax.broadcasted_iota(jnp.int32, (2 * BLOCK, HD), 0), BLOCK)
+    position = lax.broadcasted_iota(jnp.int32, (BLOCK, HD), 1)
+    lane = lax.broadcasted_iota(jnp.int32, (2 * BLOCK, HD), 1)
+
+    def step(i, carry):
+        fetch(i).wait()
+        rows = pl.ds(pl.multiple_of(i * BLOCK, BLOCK), BLOCK)
         q = q_buf[rows, :]
         q = jnp.concatenate([q[:, :HD], q[:, HD:]], axis=0)
         keys = buf[i, :, :, :HD].reshape(BLOCK * HD, HD)
         values = buf[i, :, :, HD:].reshape(BLOCK * HD, HD)
-        wide = nt(keys, q).reshape(BLOCK, HD, 2 * BLOCK)
-        shape = (BLOCK, HD, 2 * BLOCK)
-        own = lax.broadcasted_iota(jnp.int32, shape, 0) == lax.rem(
-            lax.broadcasted_iota(jnp.int32, shape, 2), BLOCK
-        )
-        scores = jnp.sum(jnp.where(own, wide, 0.0), axis=0).T * SCALE
+        wide = nt(q, keys)
+        scores = wide[:, :HD]
+        for r in range(1, BLOCK):
+            scores = jnp.where(row_of == r, wide[:, r * HD : (r + 1) * HD], scores)
+        scores = scores * SCALE
         row_hit = (
-            lax.broadcasted_iota(jnp.int32, (BLOCK, HD), 0) + base + i * BLOCK == req_ref[...]
+            lax.broadcasted_iota(jnp.int32, (BLOCK, HD), 0) + (base + i * BLOCK) == req_ref[...]
         ).astype(BF16)
         filled = nt(row_hit, col_hit)
-        position = lax.broadcasted_iota(jnp.int32, (BLOCK, HD), 1)
-        open_ = jnp.where((position < lens[rows]) & (filled < 0.5), 1.0, 0.0)
+        lens = len_ref[pl.ds(pl.multiple_of(base + i * BLOCK, BLOCK), BLOCK), :]
+        open_ = jnp.where((position < lens) & (filled < 0.5), 1.0, 0.0)
         allowed = jnp.concatenate([open_, open_], axis=0) > 0.5
         scores = jnp.where(allowed, scores, NEG)
         top = jnp.max(scores, axis=1, keepdims=True)
         weights = jnp.where(allowed, jnp.exp(scores - top), 0.0)
         total = jnp.sum(weights, axis=1, keepdims=True)
-        spread = jnp.concatenate([weights] * BLOCK, axis=1)
-        shape = (2 * BLOCK, BLOCK * HD)
-        own = (
-            lax.rem(lax.broadcasted_iota(jnp.int32, shape, 0), BLOCK)
-            == lax.broadcasted_iota(jnp.int32, shape, 1) // HD
+        spread = jnp.concatenate(
+            [jnp.where(row_of == r, weights, 0.0).astype(BF16) for r in range(BLOCK)], axis=1
         )
-        spread = jnp.where(own, spread, 0.0).astype(BF16)
         summed = jnp.dot(spread, values, preferred_element_type=F32)
-        lane = lax.broadcasted_iota(jnp.int32, (2 * BLOCK, HD), 1)
         stats = jnp.where(lane < HALF, top, total)
         for h in range(2):
             part = slice(h * BLOCK, (h + 1) * BLOCK)
             out_ref[0, h, rows, :] = summed[part]
             out_ref[1, h, rows, :] = stats[part]
+        return carry
+
+    lax.fori_loop(0, steps, step, 0)
 
 
 def project_first(info, low_ref, high_ref, w_ref, acc_ref):
@@ -224,17 +224,8 @@
 
 def finish_kernel(
     info, q_ref, span_ref, new_ref, z1_ref, z2_ref, z3_ref, z4_ref, r1_ref, r2_ref, r3_ref, r4_ref,
-    len_ref, req_ref, pos_ref, mine_ref, theirs_ref, w_ref,
-    s0_ref, s1l_ref, s1h_ref, s2l_ref, s2h_ref, s3l_ref, s3h_ref, att_ref, w_buf, sems,
+    len_ref, req_ref, pos_ref, mine_ref, theirs_ref, att_ref,
 ):
-    order = [(k, j) for k in (2, 1, 3, 0) for j in range(SIDE)]
-    copies = []
-    for n, (k, j) in enumerate(order):
-        start = pl.multiple_of(chunk(info, info[1] + k, j) * WIDE, WIDE)
-        copies.append(
-            pltpu.make_async_copy(w_ref.at[:, pl.ds(start, WIDE)], w_buf.at[n], sems.at[n])
-        )
-        copies[-1].start()
     row = lax.broadcasted_iota(jnp.int32, (ROWS, HD), 0)
     col = lax.broadcasted_iota(jnp.int32, (ROWS, HD), 1)
     ctx = info[3]
@@ -285,25 +276,33 @@
 
             att_ref[:, lanes] = attend(q, keys, values, allowed, start)
 
-    att = att_ref[...]
-    outs = {1: (s1l_ref, s1h_ref), 2: (s2l_ref, s2h_ref), 3: (s3l_ref, s3h_ref)}
-    for n, (k, j) in enumerate(order):
-        copies[n].wait()
-        part = jnp.dot(att, w_buf[n], preferred_element_type=F32)
-        if k == 0:
-            s0_ref[j] = part
-        else:
-            outs[k][j // 2][j % 2] = part.astype(BF16)
-
-
-def add_kernel(own_ref, got_ref, out_ref):
-    out_ref[...] = (own_ref[...].astype(F32) + got_ref[...].astype(F32)).astype(BF16)
-
-
-def fold_kernel(s0_ref, ll_ref, lh_ref, rl_ref, rh_ref, low_ref, high_ref):
-    for n, (left, right, out) in enumerate(((ll_ref, rl_ref, low_ref), (lh_ref, rh_ref, high_ref))):
-        total = s0_ref[2 * n : 2 * n + 2] + left[...].astype(F32) + right[...].astype(F32)
-        out[...] = total.astype(BF16)
+
+def fetch_kernel(info, w_ref, w0_ref, w1_ref, w2_ref, w3_ref, sems):
+    copies = []
+    for k, ref in enumerate((w0_ref, w1_ref, w2_ref, w3_ref)):
+        start = pl.multiple_of(lax.rem(info[2] + k, SIDE) * QUARTER, QUARTER)
+        copies.append(pltpu.make_async_copy(w_ref.at[:, pl.ds(start, QUARTER)], ref, sems.at[k]))
+        copies[-1].start()
+    for copy in copies:
+        copy.wait()
+
+
+def output_first(att_ref, w_ref, out_ref):
+    for n in range(SIDE):
+        cols = slice(n * WIDE, (n + 1) * WIDE)
+        out_ref[:, cols] = jnp.dot(att_ref[...], w_ref[:, cols], preferred_element_type=F32)
+
+
+def output_rest(
+    acc_ref, a1_ref, a2_ref, a3_ref, w1_ref, w2_ref, w3_ref, low_ref, high_ref
+):
+    for n in range(SIDE):
+        cols = slice(n * WIDE, (n + 1) * WIDE)
+        total = acc_ref[:, cols]
+        for att, w in ((a1_ref, w1_ref), (a2_ref, w2_ref), (a3_ref, w3_ref)):
+            total += jnp.dot(att[...], w[:, cols], preferred_element_type=F32)
+        half = (low_ref, high_ref)[n // 2]
+        half[:, (n % 2) * WIDE : (n % 2 + 1) * WIDE] = total.astype(BF16)
 
 
 def line_kernel(
@@ -321,13 +320,11 @@
 def place(info, sources, out_ref, sems):
     copies = []
     for k, low, high in sources:
-        for j in range(SIDE):
-            start = pl.multiple_of(chunk(info, info[1] + SIDE - k, j) * WIDE, WIDE)
-            ref = (low, high)[j // 2].at[j % 2]
+        start = lax.rem(info[2] + SIDE - k, SIDE) * QUARTER
+        for n, ref in enumerate((low, high)):
+            cols = pl.ds(pl.multiple_of(start + n * QUARTER // 2, QUARTER // 2), QUARTER // 2)
             copies.append(
-                pltpu.make_async_copy(
-                    ref, out_ref.at[:, pl.ds(start, WIDE)], sems.at[len(copies)]
-                )
+                pltpu.make_async_copy(ref, out_ref.at[:, cols], sems.at[len(copies)])
             )
             copies[-1].start()
     for copy in copies:
@@ -369,7 +366,6 @@
     dma = pltpu.SemaphoreType.DMA
     both = (0, 1)
     swap = lambda x: routed(x, both, lambda g, c, t: (1 - g, c, t))
-    half = st((2, ROWS, WIDE), BF16)
 
     h = hidden[0]
     near = [h] + [shift(h, 0, k) for k in range(1, SIDE)]
@@ -388,7 +384,33 @@
         project_first, st((ROWS, HD), F32), [SMEM] + [VMEM] * 3, VMEM, 70_000_000,
         info, *held, kv_weight,
     )
-    tied, ll, rh = lax.optimization_barrier((queries, ll, rh))
+    fetched = call(
+        fetch_kernel, [st((2 * HD, QUARTER), BF16)] * 4, [SMEM, HBM], [VMEM] * 4, 1000,
+        info, out_weight, scratch=[dma((4,))],
+    )
+    *fetched, ll, rh = lax.optimization_barrier((*fetched, ll, rh))
+    weights = [shift(fetched[k], 0, k) for k in (1, 3)]
+    acc = call(
+        project_near, st((ROWS, HD), F32), [SMEM] + [VMEM] * 6, VMEM, 140_000_000,
+        info, acc, ll, lh, rl, rh, kv_weight,
+    )
+    kv = call(
+        project_far, st((ROWS, HD), BF16), [SMEM] + [VMEM] * 4, VMEM, 70_000_000,
+        info, acc, fl, fh, kv_weight,
+    )
+
+    pair = routed(kv, both, lambda g, c, t: (g, c, t ^ 1))
+    swapped = swap(kv)
+    cross = routed(kv, both, lambda g, c, t: (1 - g, c, t ^ 1))
+    span, new, part = call(
+        pack_kernel, [st((2, ROWS, HD), BF16)] * 2 + [st((ROWS, HD), BF16)],
+        [SMEM] + [VMEM] * 4, [VMEM] * 3, 1000, info, kv, pair, swapped, cross,
+    )
+
+    tied, part, far_weight, *weights = lax.optimization_barrier(
+        (queries, part, fetched[2], *weights)
+    )
+    weights = [fetched[0], weights[0], shift(far_weight, 0, 2), weights[1]]
     old = call(
         cache_kernel, st((2, 2, HALF, HD), F32), [SMEM, VMEM, VMEM, HBM, VMEM, VMEM, VMEM], VMEM,
         1_000_000_000, info, tied, other_queries, cache, lens, req[None], slot[None],
@@ -399,24 +421,7 @@
         ],
         limit=54 << 20,
     )
-    acc = call(
-        project_near, st((ROWS, HD), F32), [SMEM] + [VMEM] * 6, VMEM, 140_000_000,
-        info, acc, ll, lh, rl, rh, kv_weight,
-    )
-    acc, old = lax.optimization_barrier((acc, old))
     other_old = swap(old)
-    kv = call(
-        project_far, st((ROWS, HD), BF16), [SMEM] + [VMEM] * 4, VMEM, 70_000_000,
-        info, acc, fl, fh, kv_weight,
-    )
-
-    pair = routed(kv, both, lambda g, c, t: (g, c, t ^ 1))
-    swapped = swap(kv)
-    cross = routed(kv, both, lambda g, c, t: (1 - g, c, t ^ 1))
-    span, new, part = call(
-        pack_kernel, [st((2, ROWS, HD), BF16)] * 2 + [st((ROWS, HD), BF16)],
-        [SMEM] + [VMEM] * 4, [VMEM] * 3, 1000, info, kv, pair, swapped, cross,
-    )
 
     def along_z(block, k):
         return routed(
@@ -425,38 +430,30 @@
 
     zs = [along_z(x, k) for k, x in ((1, span), (2, span), (3, span), (4, part))]
     rs = [swap(z) for z in zs]
-    small = st((2, ROWS, WIDE), BF16)
-    sets = call(
-        finish_kernel, [st((SIDE, ROWS, WIDE), F32)] + [small] * 6,
-        [SMEM] + [VMEM] * 16 + [HBM], [VMEM] * 7, 800_000_000,
-        info, queries, span, new, *zs, *rs, lens, req_tok, pos_tok, old, other_old, out_weight,
-        scratch=[
-            pltpu.VMEM((ROWS, 2 * HD), BF16),
-            pltpu.VMEM((RANKS, 2 * HD, WIDE), BF16),
-            dma((RANKS,)),
-        ],
-    )
-    s0, s1l, s1h, s2l, s2h, s3l, s3h = sets
-    to_right = shift(s2l, 1, 0)
-    to_left = shift(s2h, -1, 0)
-    lh = shift(s1h, 1, 0)
-    rl = shift(s3l, -1, 0)
-    add = lambda x, y: call(add_kernel, small, [VMEM] * 2, VMEM, 1000, x, y)
-    ll = shift(add(s1l, to_right), 1, 0)
-    rh = shift(add(s3h, to_left), -1, 0)
-    line = call(fold_kernel, [small] * 2, [VMEM] * 5, [VMEM] * 2, 1000, s0, ll, lh, rl, rh)
+    att = call(
+        finish_kernel, st((ROWS, 2 * HD), BF16), [SMEM] + [VMEM] * 16, VMEM, 200_000_000,
+        info, queries, span, new, *zs, *rs, lens, req_tok, pos_tok, old, other_old,
+    )
+    atts = [shift(att, 0, k) for k in range(1, SIDE)]
+    small = st((ROWS, QUARTER // 2), BF16)
+    total = call(
+        output_first, st((ROWS, QUARTER), F32), [VMEM] * 2, VMEM, 130_000_000, att, weights[0]
+    )
     line = call(
-        line_kernel, [small] * 2, [VMEM] * 8, [VMEM] * 2, 1000, *line, *relay(*line, along_b)
-    )
-    ll, lh, rl, rh, fl, fh = relay(*line, along_a)
+        output_rest, [small] * 2, [VMEM] * 7, [VMEM] * 2, 400_000_000, total, *atts, *weights[1:]
+    )
+    line = call(
+        line_kernel, [small] * 2, [VMEM] * 8, [VMEM] * 2, 1000, *line, *relay(*line, along_a)
+    )
+    ll, lh, rl, rh, fl, fh = relay(*line, along_b)
     whole = st((ROWS, RANKS * WIDE), BF16)
     out = call(
         place_near, whole, [SMEM] + [VMEM] * 6, HBM, 1000, info, *line, ll, lh, rl, rh,
-        scratch=[dma((3 * SIDE,))],
+        scratch=[dma((6,))],
     )
     out = call(
         place_far, whole, [SMEM, HBM, VMEM, VMEM], HBM, 1000, info, out, fl, fh,
-        scratch=[dma((SIDE,))], aliases={1: 0},
+        scratch=[dma((2,))], aliases={1: 0},
     )
     return out[None]
 

time: 115 us -> 123 us (1.070)
  waiting for transfers between devices: 34.3 us -> 44.9 us
  starting transfers between devices: 53 us -> 50.9 us
    ppermute x27, waiting for transfers between devices: 23.8 us -> 38.6 us  [shift(): return lax.ppermute(block, ('group', 'tp'), tp_route(step_a, step_b))]
    ppermute x27, starting transfers between devices: 38.9 us -> 34.3 us  [shift(): return lax.ppermute(block, ('group', 'tp'), tp_route(step_a, step_b))]
    ppermute x13, waiting for transfers between devices: 10.5 us -> 6.22 us  [routed(): return lax.ppermute(block, ('group', 'ctx', 'tp'), route)]
    ppermute x13, starting transfers between devices: 14.1 us -> 16.6 us  [routed(): return lax.ppermute(block, ('group', 'ctx', 'tp'), route)]
    unnamed x22 -> x30, local copies, waits for them, and re-layouts: 4.53 us -> 5.34 us
  transfers between devices with their start and end apart: 40 -> 40, of which waited for: 18 -> 21; matrix products, arithmetic and copies ran while one was open for 4% -> 3% of each run, Pallas kernels for 8% -> 11%
where the time goes in v3:
time: 123 us
  starting transfers between devices  50.9 us (41%)
  waiting for transfers between devices  44.9 us (37%)
  Pallas kernels  17.5 us (14%)
  local copies, waits for them, and re-layouts  6.73 us (5%)
  other arithmetic  2.07 us (2%)
    ppermute x27, waiting for transfers between devices, shift(): return lax.ppermute(block, ('group', 'tp'), tp_route(step_a, step_b))  38.6 us
    ppermute x27, starting transfers between devices, shift(): return lax.ppermute(block, ('group', 'tp'), tp_route(step_a, step_b))  34.3 us
    pallas_call x12, Pallas kernels, call(): pl.pallas_call(kernel, out_shape=outs, in_specs=in_specs, out_specs=out_s...  17.5 us
    ppermute x13, starting transfers between devices, routed(): return lax.ppermute(block, ('group', 'ctx', 'tp'), route)  16.6 us
    ppermute x13, waiting for transfers between devices, routed(): return lax.ppermute(block, ('group', 'ctx', 'tp'), route)  6.22 us
    unnamed x30, local copies, waits for them, and re-layouts  5.34 us
  transfers between devices with their start and end apart: 40, of which 21 were waited for; matrix products, arithmetic and copies ran while one was open for 3% of the time, Pallas kernels for 11%

profile of v3, /device:TPU:6, one launch (start us, length us, event | category | flops | bytes accessed | tf_op | source)
XLA Modules:
  0.0 122.6 jit_solution(6546436885644966936)
XLA Ops:
  4.6 2.1 %collective-permute-done.1 = bf16[128,512]{1,0:T(8,128)(2,1)S(1)} collective-permute-done((bf16[128,512]{1,0:T(8,128)(2,1)}, bf16[128,512]{1,0:T(8,128)(2,1)S(1)}, u32[]{:S(2)}, u32[]{:S(2)}) %collective-permute-start.1) | collective-permute-done | bytes 131104 | tf_op jit(solution)/shard_map/ppermute | solution.py:42
  8.1 3.1 %collective-permute-start.4 = (bf16[2,128,512]{2,1,0:T(8,128)(2,1)S(1)}, bf16[2,128,512]{2,1,0:T(8,128)(2,1)S(1)}, u32[]{:S(2)}, u32[]{:S(2)}) collective-permute-start(bf16[2,128,512]{2,1,0:T(8,128)(2,1)S(1)} %pad_maximum_fusion.1.high_ref), channel_id=1, source_target_pairs={{0,12},{1,13},{2,14},{3,15},{4,0},{5,1},{6,2},{7,3},{8,4},{9,5},{1... | collective-permute-start | bytes 786440 | tf_op jit(solution)/shard_map/ppermute | solution.py:42
  12.4 2.2 %copy-done.1 = bf16[256,8192]{1,0:T(8,128)(2,1)S(1)} copy-done((bf16[256,8192]{1,0:T(8,128)(2,1)S(1)}, bf16[256,8192]{1,0:T(8,128)(2,1)}, u32[]{:S(2)}) %copy-start.1) | copy-done | bytes 4194328
  14.6 2.0 %fetch_kernel.1 = (bf16[256,2048]{1,0:T(8,128)(2,1)S(1)}, bf16[256,2048]{1,0:T(8,128)(2,1)S(1)}, bf16[256,2048]{1,0:T(8,128)(2,1)}, bf16[256,2048]{1,0:T(8,128)(2,1)S(1)}) custom-call(s32[5]{0:T(128)S(1)} %stack.38.info, bf16[256,8192]{1,0:T(8,128)(2,1)S(1)} %copy-done.1), custom_call_target="tpu_custom_call" | custom-call | flops 1000 | bytes 4194324 | tf_op jit(solution)/shard_map/fetch_kernel/pallas_call | solution.py:344
  16.5 3.6 %collective-permute-done.3.l0_ref = bf16[2,128,512]{2,1,0:T(8,128)(2,1)S(1)} collective-permute-done((bf16[2,128,512]{2,1,0:T(8,128)(2,1)S(1)}, bf16[2,128,512]{2,1,0:T(8,128)(2,1)S(1)}, u32[]{:S(2)}, u32[]{:S(2)}) %collective-permute-start.3) | collective-permute-done | bytes 262176 | tf_op jit(solution)/shard_map/ppermute | solution.py:42
  22.2 3.2 %collective-permute-start.6 = (bf16[2,128,512]{2,1,0:T(8,128)(2,1)S(1)}, bf16[2,128,512]{2,1,0:T(8,128)(2,1)S(1)}, u32[]{:S(2)}, u32[]{:S(2)}) collective-permute-start(bf16[2,128,512]{2,1,0:T(8,128)(2,1)S(1)} %pad_maximum_fusion.low_ref), channel_id=1, source_target_pairs={{0,12},{1,13},{2,14},{3,15},{4,0},{5,1},{6,2},{7,3},{8,4},{9,5},{1... | collective-permute-start | bytes 786440 | tf_op jit(solution)/shard_map/ppermute | solution.py:42
  25.5 7.2 %collective-permute-done.5.l1_ref = bf16[2,128,512]{2,1,0:T(8,128)(2,1)S(1)} collective-permute-done((bf16[2,128,512]{2,1,0:T(8,128)(2,1)S(1)}, bf16[2,128,512]{2,1,0:T(8,128)(2,1)S(1)}, u32[]{:S(2)}, u32[]{:S(2)}) %collective-permute-start.5) | collective-permute-done | bytes 262176 | tf_op jit(solution)/shard_map/ppermute | solution.py:42
  36.0 4.3 %collective-permute-done.7.f0_ref = bf16[2,128,512]{2,1,0:T(8,128)(2,1)S(1)} collective-permute-done((bf16[2,128,512]{2,1,0:T(8,128)(2,1)S(1)}, bf16[2,128,512]{2,1,0:T(8,128)(2,1)S(1)}, u32[]{:S(2)}, u32[]{:S(2)}) %collective-permute-start.7) | collective-permute-done | bytes 262176 | tf_op jit(solution)/shard_map/ppermute | solution.py:42
  41.3 2.0 %collective-permute-start.9 = (bf16[128,128]{1,0:T(8,128)(2,1)S(1)}, bf16[128,128]{1,0:T(8,128)(2,1)S(1)}, u32[]{:S(2)}, u32[]{:S(2)}) collective-permute-start(bf16[128,128]{1,0:T(8,128)(2,1)S(1)} %project_far.1.own_ref), channel_id=1, source_target_pairs={{0,1},{1,0},{2,3},{3,2},{4,5},{5,4},{6,7},{7,6},{8,9},{9,8},{10,11... | collective-permute-start | bytes 98312 | tf_op jit(solution)/shard_map/ppermute | solution.py:52
  47.3 2.5 %collective-permute-start.27 = (bf16[256,2048]{1,0:T(8,128)(2,1)}, bf16[256,2048]{1,0:T(8,128)(2,1)}, u32[]{:S(2)}, u32[]{:S(2)}) collective-permute-start(bf16[256,2048]{1,0:T(8,128)(2,1)} %get-tuple-element.43), channel_id=1, source_target_pairs={{0,2},{1,3},{2,0},{3,1},{4,6},{5,7},{6,4},{7,5},{8,10},{9,11},{10,... | collective-permute-start | bytes 3145736 | tf_op jit(solution)/shard_map/ppermute | solution.py:42
  50.3 1.9 %collective-permute-start.12 = (bf16[2,128,128]{2,1,0:T(8,128)(2,1)S(1)}, bf16[2,128,128]{2,1,0:T(8,128)(2,1)S(1)}, u32[]{:S(2)}, u32[]{:S(2)}) collective-permute-start(bf16[2,128,128]{2,1,0:T(8,128)(2,1)S(1)} %get-tuple-element.33.span_ref), channel_id=1, source_target_pairs={{0,16},{1,17},{2,18},{3,19},{4,20},{5,21},{6,22},{7,23},{8,24},{9,... | collective-permute-start | bytes 196616 | tf_op jit(solution)/shard_map/ppermute | solution.py:52
  52.2 3.3 %collective-permute-start.13 = (bf16[2,128,128]{2,1,0:T(8,128)(2,1)S(1)}, bf16[2,128,128]{2,1,0:T(8,128)(2,1)S(1)}, u32[]{:S(2)}, u32[]{:S(2)}) collective-permute-start(bf16[2,128,128]{2,1,0:T(8,128)(2,1)S(1)} %get-tuple-element.33.span_ref), channel_id=1, source_target_pairs={{0,32},{1,33},{2,34},{3,35},{4,36},{5,37},{6,38},{7,39},{8,40},{9,... | collective-permute-start | bytes 196616 | tf_op jit(solution)/shard_map/ppermute | solution.py:52
  55.5 4.0 %collective-permute-start.14 = (bf16[2,128,128]{2,1,0:T(8,128)(2,1)S(1)}, bf16[2,128,128]{2,1,0:T(8,128)(2,1)S(1)}, u32[]{:S(2)}, u32[]{:S(2)}) collective-permute-start(bf16[2,128,128]{2,1,0:T(8,128)(2,1)S(1)} %get-tuple-element.33.span_ref), channel_id=1, source_target_pairs={{0,48},{1,49},{2,50},{3,51},{4,52},{5,53},{6,54},{7,55},{8,56},{9,... | collective-permute-start | bytes 196616 | tf_op jit(solution)/shard_map/ppermute | solution.py:52
  61.3 2.4 %collective-permute-done.14.z3_ref = bf16[2,128,128]{2,1,0:T(8,128)(2,1)S(1)} collective-permute-done((bf16[2,128,128]{2,1,0:T(8,128)(2,1)S(1)}, bf16[2,128,128]{2,1,0:T(8,128)(2,1)S(1)}, u32[]{:S(2)}, u32[]{:S(2)}) %collective-permute-start.14) | collective-permute-done | bytes 65568 | tf_op jit(solution)/shard_map/ppermute | solution.py:52
  63.7 4.4 %collective-permute-start.17 = (bf16[128,128]{1,0:T(8,128)(2,1)S(1)}, bf16[128,128]{1,0:T(8,128)(2,1)S(1)}, u32[]{:S(2)}, u32[]{:S(2)}) collective-permute-start(bf16[128,128]{1,0:T(8,128)(2,1)S(1)} %get-tuple-element.39), channel_id=1, source_target_pairs={{0,64},{1,65},{2,66},{3,67},{4,68},{5,69},{6,70},{7,71},{8,72},{9,... | collective-permute-start | bytes 98312 | tf_op jit(solution)/shard_map/ppermute | solution.py:52
  68.8 5.0 %cache_kernel.1.mine_ref = f32[2,2,64,128]{3,2,1,0:T(8,128)} custom-call(s32[5]{0:T(128)} %copy-done.8, bf16[1,128,256]{2,1,0:T(8,128)(2,1)} %q_ref.2, bf16[1,128,256]{2,1,0:T(8,128)(2,1)} %copy-done.10, bf16[128,128,256]{2,1,0:T(8,128)(2,1)} %cache_ref.1, s32[128,128]{1,0:T(8,128)} %broadcast_in_dim.26.len_ref, s32[1,128]{1,0:T(1,128)} %bitcast.19, ...), custom_call_target="tpu_custom_call" | custom-call | flops 1000000000 | bytes 8586260 | tf_op jit(solution)/shard_map/cache_kernel/pallas_call | solution.py:344
  82.6 3.3 %collective-permute-done.25.a2_ref = bf16[128,256]{1,0:T(8,128)(2,1)S(1)} collective-permute-done((bf16[128,256]{1,0:T(8,128)(2,1)S(1)}, bf16[128,256]{1,0:T(8,128)(2,1)S(1)}, u32[]{:S(2)}, u32[]{:S(2)}) %collective-permute-start.25) | collective-permute-done | bytes 65568 | tf_op jit(solution)/shard_map/ppermute | solution.py:42
  89.7 3.2 %collective-permute-start.31 = (bf16[128,1024]{1,0:T(8,128)(2,1)S(1)}, bf16[128,1024]{1,0:T(8,128)(2,1)S(1)}, u32[]{:S(2)}, u32[]{:S(2)}) collective-permute-start(bf16[128,1024]{1,0:T(8,128)(2,1)S(1)} %get-tuple-element.46.high_ref), channel_id=1, source_target_pairs={{0,12},{1,13},{2,14},{3,15},{4,0},{5,1},{6,2},{7,3},{8,4},{9,5},{1... | collective-permute-start | bytes 786440 | tf_op jit(solution)/shard_map/ppermute | solution.py:42
  92.9 3.2 %collective-permute-start.30 = (bf16[128,1024]{1,0:T(8,128)(2,1)S(1)}, bf16[128,1024]{1,0:T(8,128)(2,1)S(1)}, u32[]{:S(2)}, u32[]{:S(2)}) collective-permute-start(bf16[128,1024]{1,0:T(8,128)(2,1)S(1)} %get-tuple-element.45.low_ref), channel_id=1, source_target_pairs={{0,12},{1,13},{2,14},{3,15},{4,0},{5,1},{6,2},{7,3},{8,4},{9,5},{1... | collective-permute-start | bytes 786440 | tf_op jit(solution)/shard_map/ppermute | solution.py:42
  97.2 3.2 %collective-permute-start.33 = (bf16[128,1024]{1,0:T(8,128)(2,1)S(1)}, bf16[128,1024]{1,0:T(8,128)(2,1)S(1)}, u32[]{:S(2)}, u32[]{:S(2)}) collective-permute-start(bf16[128,1024]{1,0:T(8,128)(2,1)S(1)} %collective-permute-done.31.rh_ref), channel_id=1, source_target_pairs={{0,12},{1,13},{2,14},{3,15},{4,0},{5,1},{6,2},{7,3},{8,4},{9,5},{1... | collective-permute-start | bytes 786440 | tf_op jit(solution)/shard_map/ppermute | solution.py:42
  100.5 4.3 %collective-permute-done.32.fl_ref = bf16[128,1024]{1,0:T(8,128)(2,1)S(1)} collective-permute-done((bf16[128,1024]{1,0:T(8,128)(2,1)S(1)}, bf16[128,1024]{1,0:T(8,128)(2,1)S(1)}, u32[]{:S(2)}, u32[]{:S(2)}) %collective-permute-start.32) | collective-permute-done | bytes 262176 | tf_op jit(solution)/shard_map/ppermute | solution.py:42
  109.2 2.3 %collective-permute-done.34.ll_ref = bf16[128,1024]{1,0:T(8,128)(2,1)S(1)} collective-permute-done((bf16[128,1024]{1,0:T(8,128)(2,1)S(1)}, bf16[128,1024]{1,0:T(8,128)(2,1)S(1)}, u32[]{:S(2)}, u32[]{:S(2)}) %collective-permute-start.34) | collective-permute-done | bytes 262176 | tf_op jit(solution)/shard_map/ppermute | solution.py:42
  114.4 2.3 %collective-permute-done.36.rl_ref = bf16[128,1024]{1,0:T(8,128)(2,1)S(1)} collective-permute-done((bf16[128,1024]{1,0:T(8,128)(2,1)S(1)}, bf16[128,1024]{1,0:T(8,128)(2,1)S(1)}, u32[]{:S(2)}, u32[]{:S(2)}) %collective-permute-start.36) | collective-permute-done | bytes 262176 | tf_op jit(solution)/shard_map/ppermute | solution.py:42
  118.4 2.6 %collective-permute-done.39.fh_ref = bf16[128,1024]{1,0:T(8,128)(2,1)S(1)} collective-permute-done((bf16[128,1024]{1,0:T(8,128)(2,1)S(1)}, bf16[128,1024]{1,0:T(8,128)(2,1)S(1)}, u32[]{:S(2)}, u32[]{:S(2)}) %collective-permute-start.39) | collective-permute-done | bytes 262176 | tf_op jit(solution)/shard_map/ppermute | solution.py:42
  (113 shorter events, 44.3 us)
Async XLA Ops:
  3.1 8.1 %collective-permute-start = (bf16[128,512]{1,0:T(8,128)(2,1)}, bf16[128,512]{1,0:T(8,128)(2,1)S(1)}, u32[]{:S(2)}, u32[]{:S(2)}) collective-permute-start(bf16[128,512]{1,0:T(8,128)(2,1)} %bitcast.15), channel_id=1, source_target_pairs={{0,1},{1,2},{2,3},{3,0},{4,5},{5,6},{6,7},{7,4},{8,9},{9,10},{10,1... | collective-permute-start | bytes 393224 | tf_op jit(solution)/shard_map/ppermute | solution.py:42
  8.1 8.4 %collective-permute-start.4 = (bf16[2,128,512]{2,1,0:T(8,128)(2,1)S(1)}, bf16[2,128,512]{2,1,0:T(8,128)(2,1)S(1)}, u32[]{:S(2)}, u32[]{:S(2)}) collective-permute-start(bf16[2,128,512]{2,1,0:T(8,128)(2,1)S(1)} %pad_maximum_fusion.1.high_ref), channel_id=1, source_target_pairs={{0,12},{1,13},{2,14},{3,15},{4,0},{5,1},{6,2},{7,3},{8,4},{9,5},{1... | collective-permute-start | bytes 786440 | tf_op jit(solution)/shard_map/ppermute | solution.py:42
  12.1 8.0 %collective-permute-start.3 = (bf16[2,128,512]{2,1,0:T(8,128)(2,1)S(1)}, bf16[2,128,512]{2,1,0:T(8,128)(2,1)S(1)}, u32[]{:S(2)}, u32[]{:S(2)}) collective-permute-start(bf16[2,128,512]{2,1,0:T(8,128)(2,1)S(1)} %pad_maximum_fusion.low_ref), channel_id=1, source_target_pairs={{0,4},{1,5},{2,6},{3,7},{4,8},{5,9},{6,10},{7,11},{8,12},{9,13},{1... | collective-permute-start | bytes 786440 | tf_op jit(solution)/shard_map/ppermute | solution.py:42
  20.2 26.1 %collective-permute-start.15 = (bf16[256,2048]{1,0:T(8,128)(2,1)S(1)}, bf16[256,2048]{1,0:T(8,128)(2,1)S(1)}, u32[]{:S(2)}, u32[]{:S(2)}) collective-permute-start(bf16[256,2048]{1,0:T(8,128)(2,1)S(1)} %get-tuple-element.37), channel_id=1, source_target_pairs={{0,1},{1,2},{2,3},{3,0},{4,5},{5,6},{6,7},{7,4},{8,9},{9,10},{10,1... | collective-permute-start | bytes 3145736 | tf_op jit(solution)/shard_map/ppermute | solution.py:42
  20.4 25.9 %collective-permute-start.16 = (bf16[256,2048]{1,0:T(8,128)(2,1)S(1)}, bf16[256,2048]{1,0:T(8,128)(2,1)S(1)}, u32[]{:S(2)}, u32[]{:S(2)}) collective-permute-start(bf16[256,2048]{1,0:T(8,128)(2,1)S(1)} %get-tuple-element.38), channel_id=1, source_target_pairs={{0,3},{1,0},{2,1},{3,2},{4,7},{5,4},{6,5},{7,6},{8,11},{9,8},{10,9... | collective-permute-start | bytes 3145736 | tf_op jit(solution)/shard_map/ppermute | solution.py:42
  22.2 10.5 %collective-permute-start.5 = (bf16[2,128,512]{2,1,0:T(8,128)(2,1)S(1)}, bf16[2,128,512]{2,1,0:T(8,128)(2,1)S(1)}, u32[]{:S(2)}, u32[]{:S(2)}) collective-permute-start(bf16[2,128,512]{2,1,0:T(8,128)(2,1)S(1)} %pad_maximum_fusion.1.high_ref), channel_id=1, source_target_pairs={{0,4},{1,5},{2,6},{3,7},{4,8},{5,9},{6,10},{7,11},{8,12},{9,13},{1... | collective-permute-start | bytes 786440 | tf_op jit(solution)/shard_map/ppermute | solution.py:42
  22.2 11.3 %collective-permute-start.6 = (bf16[2,128,512]{2,1,0:T(8,128)(2,1)S(1)}, bf16[2,128,512]{2,1,0:T(8,128)(2,1)S(1)}, u32[]{:S(2)}, u32[]{:S(2)}) collective-permute-start(bf16[2,128,512]{2,1,0:T(8,128)(2,1)S(1)} %pad_maximum_fusion.low_ref), channel_id=1, source_target_pairs={{0,12},{1,13},{2,14},{3,15},{4,0},{5,1},{6,2},{7,3},{8,4},{9,5},{1... | collective-permute-start | bytes 786440 | tf_op jit(solution)/shard_map/ppermute | solution.py:42
  25.4 10.5 %collective-permute-start.8 = (bf16[2,128,512]{2,1,0:T(8,128)(2,1)S(1)}, bf16[2,128,512]{2,1,0:T(8,128)(2,1)S(1)}, u32[]{:S(2)}, u32[]{:S(2)}) collective-permute-start(bf16[2,128,512]{2,1,0:T(8,128)(2,1)S(1)} %collective-permute-done.4.r1_ref), channel_id=1, source_target_pairs={{0,12},{1,13},{2,14},{3,15},{4,0},{5,1},{6,2},{7,3},{8,4},{9,5},{1... | collective-permute-start | bytes 786440 | tf_op jit(solution)/shard_map/ppermute | solution.py:42
  32.7 7.6 %collective-permute-start.7 = (bf16[2,128,512]{2,1,0:T(8,128)(2,1)S(1)}, bf16[2,128,512]{2,1,0:T(8,128)(2,1)S(1)}, u32[]{:S(2)}, u32[]{:S(2)}) collective-permute-start(bf16[2,128,512]{2,1,0:T(8,128)(2,1)S(1)} %collective-permute-done.3.l0_ref), channel_id=1, source_target_pairs={{0,4},{1,5},{2,6},{3,7},{4,8},{5,9},{6,10},{7,11},{8,12},{9,13},{1... | collective-permute-start | bytes 786440 | tf_op jit(solution)/shard_map/ppermute | solution.py:42
  47.3 39.3 %collective-permute-start.27 = (bf16[256,2048]{1,0:T(8,128)(2,1)}, bf16[256,2048]{1,0:T(8,128)(2,1)}, u32[]{:S(2)}, u32[]{:S(2)}) collective-permute-start(bf16[256,2048]{1,0:T(8,128)(2,1)} %get-tuple-element.43), channel_id=1, source_target_pairs={{0,2},{1,3},{2,0},{3,1},{4,6},{5,7},{6,4},{7,5},{8,10},{9,11},{10,... | collective-permute-start | bytes 3145736 | tf_op jit(solution)/shard_map/ppermute | solution.py:42
  49.7 13.9 %collective-permute-start.22 = (bf16[1,128,256]{2,1,0:T(8,128)(2,1)S(1)}, bf16[1,128,256]{2,1,0:T(8,128)(2,1)S(1)}, u32[]{:S(2)}, u32[]{:S(2)}) collective-permute-start(bf16[1,128,256]{2,1,0:T(8,128)(2,1)S(1)} %copy-done.6), channel_id=1, source_target_pairs={{0,128},{1,129},{2,130},{3,131},{4,132},{5,133},{6,134},{7,135},{8... | collective-permute-start | bytes 196616 | tf_op jit(solution)/shard_map/ppermute | solution.py:52
  50.3 10.1 %collective-permute-start.12 = (bf16[2,128,128]{2,1,0:T(8,128)(2,1)S(1)}, bf16[2,128,128]{2,1,0:T(8,128)(2,1)S(1)}, u32[]{:S(2)}, u32[]{:S(2)}) collective-permute-start(bf16[2,128,128]{2,1,0:T(8,128)(2,1)S(1)} %get-tuple-element.33.span_ref), channel_id=1, source_target_pairs={{0,16},{1,17},{2,18},{3,19},{4,20},{5,21},{6,22},{7,23},{8,24},{9,... | collective-permute-start | bytes 196616 | tf_op jit(solution)/shard_map/ppermute | solution.py:52
  52.2 9.0 %collective-permute-start.13 = (bf16[2,128,128]{2,1,0:T(8,128)(2,1)S(1)}, bf16[2,128,128]{2,1,0:T(8,128)(2,1)S(1)}, u32[]{:S(2)}, u32[]{:S(2)}) collective-permute-start(bf16[2,128,128]{2,1,0:T(8,128)(2,1)S(1)} %get-tuple-element.33.span_ref), channel_id=1, source_target_pairs={{0,32},{1,33},{2,34},{3,35},{4,36},{5,37},{6,38},{7,39},{8,40},{9,... | collective-permute-start | bytes 196616 | tf_op jit(solution)/shard_map/ppermute | solution.py:52
  55.5 8.2 %collective-permute-start.14 = (bf16[2,128,128]{2,1,0:T(8,128)(2,1)S(1)}, bf16[2,128,128]{2,1,0:T(8,128)(2,1)S(1)}, u32[]{:S(2)}, u32[]{:S(2)}) collective-permute-start(bf16[2,128,128]{2,1,0:T(8,128)(2,1)S(1)} %get-tuple-element.33.span_ref), channel_id=1, source_target_pairs={{0,48},{1,49},{2,50},{3,51},{4,52},{5,53},{6,54},{7,55},{8,56},{9,... | collective-permute-start | bytes 196616 | tf_op jit(solution)/shard_map/ppermute | solution.py:52
  60.4 13.4 %collective-permute-start.18 = (bf16[2,128,128]{2,1,0:T(8,128)(2,1)S(1)}, bf16[2,128,128]{2,1,0:T(8,128)(2,1)S(1)}, u32[]{:S(2)}, u32[]{:S(2)}) collective-permute-start(bf16[2,128,128]{2,1,0:T(8,128)(2,1)S(1)} %collective-permute-done.12.z1_ref), channel_id=1, source_target_pairs={{0,128},{1,129},{2,130},{3,131},{4,132},{5,133},{6,134},{7,135},{8... | collective-permute-start | bytes 196616 | tf_op jit(solution)/shard_map/ppermute | solution.py:52
  61.3 13.4 %collective-permute-start.19 = (bf16[2,128,128]{2,1,0:T(8,128)(2,1)S(1)}, bf16[2,128,128]{2,1,0:T(8,128)(2,1)S(1)}, u32[]{:S(2)}, u32[]{:S(2)}) collective-permute-start(bf16[2,128,128]{2,1,0:T(8,128)(2,1)S(1)} %collective-permute-done.13.z2_ref), channel_id=1, source_target_pairs={{0,128},{1,129},{2,130},{3,131},{4,132},{5,133},{6,134},{7,135},{8... | collective-permute-start | bytes 196616 | tf_op jit(solution)/shard_map/ppermute | solution.py:52
  63.7 11.0 %collective-permute-start.20 = (bf16[2,128,128]{2,1,0:T(8,128)(2,1)S(1)}, bf16[2,128,128]{2,1,0:T(8,128)(2,1)S(1)}, u32[]{:S(2)}, u32[]{:S(2)}) collective-permute-start(bf16[2,128,128]{2,1,0:T(8,128)(2,1)S(1)} %collective-permute-done.14.z3_ref), channel_id=1, source_target_pairs={{0,128},{1,129},{2,130},{3,131},{4,132},{5,133},{6,134},{7,135},{8... | collective-permute-start | bytes 196616 | tf_op jit(solution)/shard_map/ppermute | solution.py:52
  63.7 10.4 %collective-permute-start.17 = (bf16[128,128]{1,0:T(8,128)(2,1)S(1)}, bf16[128,128]{1,0:T(8,128)(2,1)S(1)}, u32[]{:S(2)}, u32[]{:S(2)}) collective-permute-start(bf16[128,128]{1,0:T(8,128)(2,1)S(1)} %get-tuple-element.39), channel_id=1, source_target_pairs={{0,64},{1,65},{2,66},{3,67},{4,68},{5,69},{6,70},{7,71},{8,72},{9,... | collective-permute-start | bytes 98312 | tf_op jit(solution)/shard_map/ppermute | solution.py:52
  89.6 7.7 %collective-permute-start.28 = (bf16[128,1024]{1,0:T(8,128)(2,1)S(1)}, bf16[128,1024]{1,0:T(8,128)(2,1)S(1)}, u32[]{:S(2)}, u32[]{:S(2)}) collective-permute-start(bf16[128,1024]{1,0:T(8,128)(2,1)S(1)} %get-tuple-element.45.low_ref), channel_id=1, source_target_pairs={{0,4},{1,5},{2,6},{3,7},{4,8},{5,9},{6,10},{7,11},{8,12},{9,13},{1... | collective-permute-start | bytes 786440 | tf_op jit(solution)/shard_map/ppermute | solution.py:42
  92.9 7.6 %collective-permute-start.29 = (bf16[128,1024]{1,0:T(8,128)(2,1)S(1)}, bf16[128,1024]{1,0:T(8,128)(2,1)S(1)}, u32[]{:S(2)}, u32[]{:S(2)}) collective-permute-start(bf16[128,1024]{1,0:T(8,128)(2,1)S(1)} %get-tuple-element.46.high_ref), channel_id=1, source_target_pairs={{0,4},{1,5},{2,6},{3,7},{4,8},{5,9},{6,10},{7,11},{8,12},{9,13},{1... | collective-permute-start | bytes 786440 | tf_op jit(solution)/shard_map/ppermute | solution.py:42
  92.9 7.6 %collective-permute-start.30 = (bf16[128,1024]{1,0:T(8,128)(2,1)S(1)}, bf16[128,1024]{1,0:T(8,128)(2,1)S(1)}, u32[]{:S(2)}, u32[]{:S(2)}) collective-permute-start(bf16[128,1024]{1,0:T(8,128)(2,1)S(1)} %get-tuple-element.45.low_ref), channel_id=1, source_target_pairs={{0,12},{1,13},{2,14},{3,15},{4,0},{5,1},{6,2},{7,3},{8,4},{9,5},{1... | collective-permute-start | bytes 786440 | tf_op jit(solution)/shard_map/ppermute | solution.py:42
  105.9 7.6 %collective-permute-start.37 = (bf16[128,1024]{1,0:T(8,128)(2,1)S(1)}, bf16[128,1024]{1,0:T(8,128)(2,1)S(1)}, u32[]{:S(2)}, u32[]{:S(2)}) collective-permute-start(bf16[128,1024]{1,0:T(8,128)(2,1)S(1)} %get-tuple-element.48.th_ref), channel_id=1, source_target_pairs={{0,3},{1,0},{2,1},{3,2},{4,7},{5,4},{6,5},{7,6},{8,11},{9,8},{10,9... | collective-permute-start | bytes 786440 | tf_op jit(solution)/shard_map/ppermute | solution.py:42
  109.1 7.6 %collective-permute-start.36 = (bf16[128,1024]{1,0:T(8,128)(2,1)S(1)}, bf16[128,1024]{1,0:T(8,128)(2,1)S(1)}, u32[]{:S(2)}, u32[]{:S(2)}) collective-permute-start(bf16[128,1024]{1,0:T(8,128)(2,1)S(1)} %get-tuple-element.47.tl_ref), channel_id=1, source_target_pairs={{0,3},{1,0},{2,1},{3,2},{4,7},{5,4},{6,5},{7,6},{8,11},{9,8},{10,9... | collective-permute-start | bytes 786440 | tf_op jit(solution)/shard_map/ppermute | solution.py:42
  113.5 7.6 %collective-permute-start.39 = (bf16[128,1024]{1,0:T(8,128)(2,1)S(1)}, bf16[128,1024]{1,0:T(8,128)(2,1)S(1)}, u32[]{:S(2)}, u32[]{:S(2)}) collective-permute-start(bf16[128,1024]{1,0:T(8,128)(2,1)S(1)} %collective-permute-done.37.rh_ref), channel_id=1, source_target_pairs={{0,3},{1,0},{2,1},{3,2},{4,7},{5,4},{6,5},{7,6},{8,11},{9,8},{10,9... | collective-permute-start | bytes 786440 | tf_op jit(solution)/shard_map/ppermute | solution.py:42
  (31 other events, 260.1 us)

commit v4 on v2

--- a/solution.py
+++ b/solution.py
@@ -12,7 +12,7 @@
 NCTX = 8
 ROWS = 128
 WIDE = 512
-BLOCK = 16
+BLOCK = 32
 HALF = 64
 SCALE = HD ** -0.5
 NEG = -1e30
@@ -82,19 +82,23 @@
     return shift(block, 0, k)
 
 
+def lane_column(ref):
+    return jnp.broadcast_to(ref[...].astype(F32), (HD, HD)).T
+
+
 def cache_kernel(
-    info, q_ref, other_ref, cache_ref, len_ref, req_ref, slot_ref, out_ref, q_buf, buf, sems
+    info, q_ref, other_ref, cache_ref, len_ref, owner_ref, slot_ref, out_ref, q_buf, open_buf, buf,
+    sems,
 ):
     base = info[0] * HALF
     steps = HALF // BLOCK
-    copies = [
-        pltpu.make_async_copy(
-            cache_ref.at[pl.ds(base + i * BLOCK, BLOCK)], buf.at[i], sems.at[i]
-        )
-        for i in range(steps)
-    ]
-    for copy in copies:
-        copy.start()
+
+    def fetch(i):
+        start = pl.multiple_of(base + i * BLOCK, BLOCK)
+        return pltpu.make_async_copy(cache_ref.at[pl.ds(start, BLOCK)], buf.at[i], sems.at[i])
+
+    for i in range(steps):
+        fetch(i).start()
 
     @pl.when(info[0] == 0)
     def _():
@@ -104,48 +108,54 @@
     def _():
         q_buf[...] = q_ref[0, HALF:, :]
 
-    col_hit = (
-        lax.broadcasted_iota(jnp.int32, (HD, HD), 0) // PAGE == slot_ref[...]
-    ).astype(BF16)
-    lens = len_ref[pl.ds(base, HALF), :]
-    for i in range(steps):
-        copies[i].wait()
-        rows = slice(i * BLOCK, (i + 1) * BLOCK)
+    request = lax.broadcasted_iota(jnp.int32, (ROWS, HD), 0)
+    column = lax.broadcasted_iota(jnp.int32, (ROWS, HD), 1)
+    slot = slot_ref[...]
+    row_hit = (owner_ref[...] == info[3]) & (slot // PAGE == request)
+    col_hit = request // PAGE == lax.rem(slot, PAGE)
+    filled = nt(row_hit.astype(BF16), col_hit.astype(BF16))
+    inside = column.astype(F32) < lane_column(len_ref)
+    open_buf[...] = jnp.where(inside & (filled < 0.5), 1.0, 0.0)
+
+    shape = (BLOCK, HD, 2 * BLOCK)
+    own_key = lax.broadcasted_iota(jnp.int32, shape, 0) == lax.rem(
+        lax.broadcasted_iota(jnp.int32, shape, 2), BLOCK
+    )
+    row_of = lax.rem(lax.broadcasted_iota(jnp.int32, (2 * BLOCK, HD), 0), BLOCK)
+    lane = lax.broadcasted_iota(jnp.int32, (2 * BLOCK, HD), 1)
+
+    def step(i, carry):
+        fetch(i).wait()
+        rows = pl.ds(pl.multiple_of(i * BLOCK, BLOCK), BLOCK)
         q = q_buf[rows, :]
         q = jnp.concatenate([q[:, :HD], q[:, HD:]], axis=0)
         keys = buf[i, :, :, :HD].reshape(BLOCK * HD, HD)
         values = buf[i, :, :, HD:].reshape(BLOCK * HD, HD)
-        wide = nt(keys, q).reshape(BLOCK, HD, 2 * BLOCK)
-        shape = (BLOCK, HD, 2 * BLOCK)
-        own = lax.broadcasted_iota(jnp.int32, shape, 0) == lax.rem(
-            lax.broadcasted_iota(jnp.int32, shape, 2), BLOCK
-        )
-        scores = jnp.sum(jnp.where(own, wide, 0.0), axis=0).T * SCALE
-        row_hit = (
-            lax.broadcasted_iota(jnp.int32, (BLOCK, HD), 0) + base + i * BLOCK == req_ref[...]
-        ).astype(BF16)
-        filled = nt(row_hit, col_hit)
-        position = lax.broadcasted_iota(jnp.int32, (BLOCK, HD), 1)
-        open_ = jnp.where((position < lens[rows]) & (filled < 0.5), 1.0, 0.0)
+        wide = nt(keys, q).reshape(shape)
+        scores = jnp.sum(jnp.where(own_key, wide, 0.0), axis=0).T * SCALE
+        open_ = open_buf[pl.ds(pl.multiple_of(base + i * BLOCK, BLOCK), BLOCK), :]
         allowed = jnp.concatenate([open_, open_], axis=0) > 0.5
         scores = jnp.where(allowed, scores, NEG)
         top = jnp.max(scores, axis=1, keepdims=True)
         weights = jnp.where(allowed, jnp.exp(scores - top), 0.0)
         total = jnp.sum(weights, axis=1, keepdims=True)
-        spread = jnp.concatenate([weights] * BLOCK, axis=1)
-        shape = (2 * BLOCK, BLOCK * HD)
-        own = (
-            lax.rem(lax.broadcasted_iota(jnp.int32, shape, 0), BLOCK)
-            == lax.broadcasted_iota(jnp.int32, shape, 1) // HD
+        spread = jnp.concatenate(
+            [jnp.where(row_of == r, weights, 0.0).astype(BF16) for r in range(BLOCK)], axis=1
         )
-        spread = jnp.where(own, spread, 0.0).astype(BF16)
         summed = jnp.dot(spread, values, preferred_element_type=F32)
-        lane = lax.broadcasted_iota(jnp.int32, (2 * BLOCK, HD), 1)
         stats = jnp.where(lane < HALF, top, total)
         for h in range(2):
             part = slice(h * BLOCK, (h + 1) * BLOCK)
             out_ref[0, h, rows, :] = summed[part]
             out_ref[1, h, rows, :] = stats[part]
+        return carry
+
+    lax.fori_loop(0, steps, step, 0)
+
+
+def join_kernel(first_ref, second_ref, out_ref):
+    out_ref[0] = first_ref[...]
+    out_ref[1] = second_ref[...]
 
 
 def project_first(info, low_ref, high_ref, w_ref, acc_ref):
@@ -224,17 +234,9 @@
 
 def finish_kernel(
     info, q_ref, span_ref, new_ref, z1_ref, z2_ref, z3_ref, z4_ref, r1_ref, r2_ref, r3_ref, r4_ref,
-    len_ref, req_ref, pos_ref, mine_ref, theirs_ref, w_ref,
-    s0_ref, s1l_ref, s1h_ref, s2l_ref, s2h_ref, s3l_ref, s3h_ref, att_ref, w_buf, sems,
+    len_ref, owner_ref, slot_ref, mine_ref, theirs_ref, w_ref,
+    s0_ref, s1l_ref, s1h_ref, s2l_ref, s2h_ref, s3l_ref, s3h_ref, att_ref,
 ):
-    order = [(k, j) for k in (2, 1, 3, 0) for j in range(SIDE)]
-    copies = []
-    for n, (k, j) in enumerate(order):
-        start = pl.multiple_of(chunk(info, info[1] + k, j) * WIDE, WIDE)
-        copies.append(
-            pltpu.make_async_copy(w_ref.at[:, pl.ds(start, WIDE)], w_buf.at[n], sems.at[n])
-        )
-        copies[-1].start()
     row = lax.broadcasted_iota(jnp.int32, (ROWS, HD), 0)
     col = lax.broadcasted_iota(jnp.int32, (ROWS, HD), 1)
     ctx = info[3]
@@ -262,10 +264,19 @@
         refs = [span_ref] + [z for z, _ in near] + [None] + [r for _, r in near]
         keys = [r4_ref if r is None else r.at[0] for r in refs]
         values = [z4_ref if r is None else r.at[1] for r in refs]
-        allowed = [
-            (req_ref[pl.ds(p, 1), :] == row) & (pos_ref[pl.ds(p, 1), :] < len_ref[...])
-            for p in places
-        ]
+        slot = slot_ref[...]
+        request = jnp.where(owner_ref[...] == ctx, slot // PAGE, -1).astype(F32)
+        page = lax.rem(slot, PAGE).astype(F32)
+        in_page = (lax.rem(row, 2 * PAGE) == col // PAGE).astype(BF16)
+        lens = lane_column(len_ref)
+        pages = lax.broadcasted_iota(jnp.int32, (1, HD), 1) // (2 * PAGE)
+        allowed = []
+        for p in places:
+            picked = jnp.concatenate([request, page] * 8, axis=0)
+            picked = jnp.where(pages == p, picked, 0.0).astype(BF16)
+            token = jnp.dot(picked, in_page, preferred_element_type=F32)
+            position = token[1:2] * PAGE + lax.rem(col[:1], PAGE).astype(F32)
+            allowed.append((token[:1] == row.astype(F32)) & (position < lens))
         key_new = new_ref[0].astype(F32)
         value_new = new_ref[1].astype(F32)
         for h in range(2):
@@ -286,14 +297,15 @@
             att_ref[:, lanes] = attend(q, keys, values, allowed, start)
 
     att = att_ref[...]
-    outs = {1: (s1l_ref, s1h_ref), 2: (s2l_ref, s2h_ref), 3: (s3l_ref, s3h_ref)}
-    for n, (k, j) in enumerate(order):
-        copies[n].wait()
-        part = jnp.dot(att, w_buf[n], preferred_element_type=F32)
-        if k == 0:
-            s0_ref[j] = part
-        else:
-            outs[k][j // 2][j % 2] = part.astype(BF16)
+    sets = {1: (s1l_ref, s1h_ref), 2: (s2l_ref, s2h_ref), 3: (s3l_ref, s3h_ref)}
+    for k in (2, 1, 3, 0):
+        for j in range(SIDE):
+            start = pl.multiple_of(chunk(info, info[1] + k, j) * WIDE, WIDE)
+            part = jnp.dot(att, w_ref[:, pl.ds(start, WIDE)], preferred_element_type=F32)
+            if k == 0:
+                s0_ref[j] = part
+            else:
+                sets[k][j // 2][j % 2] = part.astype(BF16)
 
 
 def add_kernel(own_ref, got_ref, out_ref):
@@ -369,47 +381,31 @@
     dma = pltpu.SemaphoreType.DMA
     both = (0, 1)
     swap = lambda x: routed(x, both, lambda g, c, t: (1 - g, c, t))
-    half = st((2, ROWS, WIDE), BF16)
 
     h = hidden[0]
     near = [h] + [shift(h, 0, k) for k in range(1, SIDE)]
-    other_queries = swap(queries)
-    held = (jnp.stack(near[:2]), jnp.stack(near[2:]))
+    held = (
+        call(join_kernel, st((2, ROWS, WIDE), BF16), [VMEM] * 2, VMEM, 1000, *near[:2]),
+        jnp.stack(near[2:]),
+    )
     ll, lh, rl, rh, fl, fh = relay(*held, along_a)
-
-    lens = jnp.broadcast_to(cached_len[:, None], (ROWS, HD))
-    mine = page_owner == ctx
-    req = jnp.where(mine, page_slot // PAGE, -1)
-    slot = page_slot % PAGE
-    req_tok = jnp.repeat(req, PAGE).reshape(NCTX, ROWS)
-    pos_tok = (slot[:, None] * PAGE + jnp.arange(PAGE)[None, :]).reshape(NCTX, ROWS)
+    owners, slots, lens = page_owner[None], page_slot[None], cached_len[None]
 
     acc = call(
         project_first, st((ROWS, HD), F32), [SMEM] + [VMEM] * 3, VMEM, 70_000_000,
         info, *held, kv_weight,
     )
-    tied, ll, rh = lax.optimization_barrier((queries, ll, rh))
-    old = call(
-        cache_kernel, st((2, 2, HALF, HD), F32), [SMEM, VMEM, VMEM, HBM, VMEM, VMEM, VMEM], VMEM,
-        1_000_000_000, info, tied, other_queries, cache, lens, req[None], slot[None],
-        scratch=[
-            pltpu.VMEM((HALF, 2 * HD), BF16),
-            pltpu.VMEM((HALF // BLOCK, BLOCK, HD, 2 * HD), BF16),
-            dma((HALF // BLOCK,)),
-        ],
-        limit=54 << 20,
-    )
     acc = call(
         project_near, st((ROWS, HD), F32), [SMEM] + [VMEM] * 6, VMEM, 140_000_000,
         info, acc, ll, lh, rl, rh, kv_weight,
     )
-    acc, old = lax.optimization_barrier((acc, old))
-    other_old = swap(old)
     kv = call(
         project_far, st((ROWS, HD), BF16), [SMEM] + [VMEM] * 4, VMEM, 70_000_000,
         info, acc, fl, fh, kv_weight,
     )
 
+    kv, queries = lax.optimization_barrier((kv, queries))
+    other_queries = swap(queries)
     pair = routed(kv, both, lambda g, c, t: (g, c, t ^ 1))
     swapped = swap(kv)
     cross = routed(kv, both, lambda g, c, t: (1 - g, c, t ^ 1))
@@ -424,17 +420,27 @@
         )
 
     zs = [along_z(x, k) for k, x in ((1, span), (2, span), (3, span), (4, part))]
+    tied, zs[3] = lax.optimization_barrier((queries, zs[3]))
+    old = call(
+        cache_kernel, st((2, 2, HALF, HD), F32), [SMEM, VMEM, VMEM, HBM, VMEM, VMEM, VMEM], VMEM,
+        1000, info, tied, other_queries, cache, lens, owners, slots,
+        scratch=[
+            pltpu.VMEM((HALF, 2 * HD), BF16),
+            pltpu.VMEM((ROWS, HD), F32),
+            pltpu.VMEM((HALF // BLOCK, BLOCK, HD, 2 * HD), BF16),
+            dma((HALF // BLOCK,)),
+        ],
+        limit=51 << 20,
+    )
+    other_old = swap(old)
+
     rs = [swap(z) for z in zs]
     small = st((2, ROWS, WIDE), BF16)
     sets = call(
         finish_kernel, [st((SIDE, ROWS, WIDE), F32)] + [small] * 6,
-        [SMEM] + [VMEM] * 16 + [HBM], [VMEM] * 7, 800_000_000,
-        info, queries, span, new, *zs, *rs, lens, req_tok, pos_tok, old, other_old, out_weight,
-        scratch=[
-            pltpu.VMEM((ROWS, 2 * HD), BF16),
-            pltpu.VMEM((RANKS, 2 * HD, WIDE), BF16),
-            dma((RANKS,)),
-        ],
+        [SMEM] + [VMEM] * 17, [VMEM] * 7, 800_000_000,
+        info, queries, span, new, *zs, *rs, lens, owners, slots, old, other_old, out_weight,
+        scratch=[pltpu.VMEM((ROWS, 2 * HD), BF16)],
     )
     s0, s1l, s1h, s2l, s2h, s3l, s3h = sets
     to_right = shift(s2l, 1, 0)

time: 115 us -> 101 us (0.88)
  Pallas kernels: 18.3 us -> 14.2 us
  waiting for transfers between devices: 34.3 us -> 30.5 us
  other arithmetic: 2.84 us -> 0.03 us
  local copies, waits for them, and re-layouts: 5.93 us -> 3.33 us
    ppermute x13, waiting for transfers between devices: 10.5 us -> 6.06 us  [routed(): return lax.ppermute(block, ('group', 'ctx', 'tp'), route)]
    pallas_call x12 -> x13, Pallas kernels: 18.3 us -> 14.2 us  [call(): pl.pallas_call(kernel, out_shape=outs, in_specs=in_specs, out_specs=out_s...]
    unnamed x22 -> x16, local copies, waits for them, and re-layouts: 4.53 us -> 3.25 us
    broadcast_in_dim x1 -> x0, other arithmetic: 1.21 us -> none  [body(): slot[None]]
  transfers between devices with their start and end apart: 40 -> 40, of which waited for: 18 -> 17; matrix products, arithmetic and copies ran while one was open for 4% -> 0% of each run, Pallas kernels for 8% -> 9%
where the time goes in v4:
time: 101 us
  starting transfers between devices  52.6 us (52%)
  waiting for transfers between devices  30.5 us (30%)
  Pallas kernels  14.2 us (14%)
  local copies, waits for them, and re-layouts  3.33 us (3%)
    ppermute x27, starting transfers between devices, shift(): return lax.ppermute(block, ('group', 'tp'), tp_route(step_a, step_b))  38.9 us
    ppermute x27, waiting for transfers between devices, shift(): return lax.ppermute(block, ('group', 'tp'), tp_route(step_a, step_b))  24.5 us
    pallas_call x13, Pallas kernels, call(): pl.pallas_call(kernel, out_shape=outs, in_specs=in_specs, out_specs=out_s...  14.2 us
    ppermute x13, starting transfers between devices, routed(): return lax.ppermute(block, ('group', 'ctx', 'tp'), route)  13.8 us
    ppermute x13, waiting for transfers between devices, routed(): return lax.ppermute(block, ('group', 'ctx', 'tp'), route)  6.06 us
    unnamed x16, local copies, waits for them, and re-layouts  3.25 us
  transfers between devices with their start and end apart: 40, of which 17 were waited for; matrix products, arithmetic and copies ran while one was open for 0% of the time, Pallas kernels for 9%

profile of v4, /device:TPU:6, one launch (start us, length us, event | category | flops | bytes accessed | tf_op | source)
XLA Modules:
  0.0 101.1 jit_solution(6242059264738472818)
XLA Ops:
  0.0 2.2 %collective-permute-start = (bf16[128,512]{1,0:T(8,128)(2,1)}, bf16[128,512]{1,0:T(8,128)(2,1)S(1)}, u32[]{:S(2)}, u32[]{:S(2)}) collective-permute-start(bf16[128,512]{1,0:T(8,128)(2,1)} %bitcast.12), channel_id=1, source_target_pairs={{0,1},{1,2},{2,3},{3,0},{4,5},{5,6},{6,7},{7,4},{8,9},{9,10},{10,1... | collective-permute-start | bytes 393224 | tf_op jit(solution)/shard_map/ppermute | solution.py:41
  7.8 2.2 %collective-permute-done.2 = bf16[128,512]{1,0:T(8,128)(2,1)S(1)} collective-permute-done((bf16[128,512]{1,0:T(8,128)(2,1)}, bf16[128,512]{1,0:T(8,128)(2,1)S(1)}, u32[]{:S(2)}, u32[]{:S(2)}) %collective-permute-start.2) | collective-permute-done | bytes 131104 | tf_op jit(solution)/shard_map/ppermute | solution.py:41
  14.2 2.3 %collective-permute-done.6.r1_ref = bf16[2,128,512]{2,1,0:T(8,128)(2,1)S(1)} collective-permute-done((bf16[2,128,512]{2,1,0:T(8,128)(2,1)S(1)}, bf16[2,128,512]{2,1,0:T(8,128)(2,1)S(1)}, u32[]{:S(2)}, u32[]{:S(2)}) %collective-permute-start.6) | collective-permute-done | bytes 262176 | tf_op jit(solution)/shard_map/ppermute | solution.py:41
  16.5 2.9 %collective-permute-start.8 = (bf16[2,128,512]{2,1,0:T(8,128)(2,1)S(1)}, bf16[2,128,512]{2,1,0:T(8,128)(2,1)S(1)}, u32[]{:S(2)}, u32[]{:S(2)}) collective-permute-start(bf16[2,128,512]{2,1,0:T(8,128)(2,1)S(1)} %collective-permute-done.6.r1_ref), channel_id=1, source_target_pairs={{0,12},{1,13},{2,14},{3,15},{4,0},{5,1},{6,2},{7,3},{8,4},{9,5},{1... | collective-permute-start | bytes 786440 | tf_op jit(solution)/shard_map/ppermute | solution.py:41
  24.7 2.0 %collective-permute-start.10 = (bf16[128,128]{1,0:T(8,128)(2,1)S(1)}, bf16[128,128]{1,0:T(8,128)(2,1)S(1)}, u32[]{:S(2)}, u32[]{:S(2)}) collective-permute-start(bf16[128,128]{1,0:T(8,128)(2,1)S(1)} %project_far.1.own_ref), channel_id=1, source_target_pairs={{0,128},{1,129},{2,130},{3,131},{4,132},{5,133},{6,134},{7,135},{8... | collective-permute-start | bytes 98312 | tf_op jit(solution)/shard_map/ppermute | solution.py:51
  28.0 2.6 %collective-permute-done.9.pair_ref = bf16[128,128]{1,0:T(8,128)(2,1)S(1)} collective-permute-done((bf16[128,128]{1,0:T(8,128)(2,1)S(1)}, bf16[128,128]{1,0:T(8,128)(2,1)S(1)}, u32[]{:S(2)}, u32[]{:S(2)}) %collective-permute-start.9) | collective-permute-done | bytes 32800 | tf_op jit(solution)/shard_map/ppermute | solution.py:51
  31.2 7.3 %collective-permute-start.15 = (bf16[128,128]{1,0:T(8,128)(2,1)S(1)}, bf16[128,128]{1,0:T(8,128)(2,1)S(1)}, u32[]{:S(2)}, u32[]{:S(2)}) collective-permute-start(bf16[128,128]{1,0:T(8,128)(2,1)S(1)} %get-tuple-element.27), channel_id=1, source_target_pairs={{0,64},{1,65},{2,66},{3,67},{4,68},{5,69},{6,70},{7,71},{8,72},{9,... | collective-permute-start | bytes 98312 | tf_op jit(solution)/shard_map/ppermute | solution.py:51
  38.5 1.9 %collective-permute-start.14 = (bf16[2,128,128]{2,1,0:T(8,128)(2,1)S(1)}, bf16[2,128,128]{2,1,0:T(8,128)(2,1)S(1)}, u32[]{:S(2)}, u32[]{:S(2)}) collective-permute-start(bf16[2,128,128]{2,1,0:T(8,128)(2,1)S(1)} %get-tuple-element.25.span_ref), channel_id=1, source_target_pairs={{0,48},{1,49},{2,50},{3,51},{4,52},{5,53},{6,54},{7,55},{8,56},{9,... | collective-permute-start | bytes 196616 | tf_op jit(solution)/shard_map/ppermute | solution.py:51
  41.1 4.7 %cache_kernel.1.mine_ref = f32[2,2,64,128]{3,2,1,0:T(8,128)S(1)} custom-call(s32[5]{0:T(128)S(1)} %stack.32.info, bf16[1,128,256]{2,1,0:T(8,128)(2,1)S(1)} %copy-done.3, bf16[1,128,256]{2,1,0:T(8,128)(2,1)S(1)} %collective-permute-done.20.other_ref, bf16[128,128,256]{2,1,0:T(8,128)(2,1)} %cache_ref.1, s32[1,128]{1,0:T(1,128)S(1)} %bitcast.16, ...), custom_call_target="tpu_custom_call" | custom-call | flops 1000 | bytes 8521236 | tf_op jit(solution)/shard_map/cache_kernel/pallas_call | solution.py:359
  49.8 2.6 %finish_kernel.1 = (f32[4,128,512]{2,1,0:T(8,128)S(1)}, bf16[2,128,512]{2,1,0:T(8,128)(2,1)S(1)}, bf16[2,128,512]{2,1,0:T(8,128)(2,1)S(1)}, bf16[2,128,512]{2,1,...) custom-call(s32[5]{0:T(128)S(1)} %stack.32.info, ...), custom_call_target="tpu_custom_call" | custom-call | flops 800000000 | bytes 5113364 | tf_op jit(solution)/shard_map/finish_kernel/pallas_call | solution.py:359
  52.4 3.3 %collective-permute-start.26 = (bf16[2,128,512]{2,1,0:T(8,128)(2,1)S(1)}, bf16[2,128,512]{2,1,0:T(8,128)(2,1)S(1)}, u32[]{:S(2)}, u32[]{:S(2)}) collective-permute-start(bf16[2,128,512]{2,1,0:T(8,128)(2,1)S(1)} %get-tuple-element.36), channel_id=1, source_target_pairs={{0,12},{1,13},{2,14},{3,15},{4,0},{5,1},{6,2},{7,3},{8,4},{9,5},{1... | collective-permute-start | bytes 786440 | tf_op jit(solution)/shard_map/ppermute | solution.py:41
  55.8 3.2 %collective-permute-start.25 = (bf16[2,128,512]{2,1,0:T(8,128)(2,1)S(1)}, bf16[2,128,512]{2,1,0:T(8,128)(2,1)S(1)}, u32[]{:S(2)}, u32[]{:S(2)}) collective-permute-start(bf16[2,128,512]{2,1,0:T(8,128)(2,1)S(1)} %get-tuple-element.34), channel_id=1, source_target_pairs={{0,12},{1,13},{2,14},{3,15},{4,0},{5,1},{6,2},{7,3},{8,4},{9,5},{1... | collective-permute-start | bytes 786440 | tf_op jit(solution)/shard_map/ppermute | solution.py:41
  60.3 3.3 %collective-permute-start.27 = (bf16[2,128,512]{2,1,0:T(8,128)(2,1)S(1)}, bf16[2,128,512]{2,1,0:T(8,128)(2,1)S(1)}, u32[]{:S(2)}, u32[]{:S(2)}) collective-permute-start(bf16[2,128,512]{2,1,0:T(8,128)(2,1)S(1)} %add_kernel.3), channel_id=1, source_target_pairs={{0,12},{1,13},{2,14},{3,15},{4,0},{5,1},{6,2},{7,3},{8,4},{9,5},{1... | collective-permute-start | bytes 786440 | tf_op jit(solution)/shard_map/ppermute | solution.py:41
  63.5 4.2 %collective-permute-done.23.ll_ref = bf16[2,128,512]{2,1,0:T(8,128)(2,1)S(1)} collective-permute-done((bf16[2,128,512]{2,1,0:T(8,128)(2,1)S(1)}, bf16[2,128,512]{2,1,0:T(8,128)(2,1)S(1)}, u32[]{:S(2)}, u32[]{:S(2)}) %collective-permute-start.23) | collective-permute-done | bytes 262176 | tf_op jit(solution)/shard_map/ppermute | solution.py:41
  68.3 2.0 %collective-permute-start.31 = (bf16[2,128,512]{2,1,0:T(8,128)(2,1)S(1)}, bf16[2,128,512]{2,1,0:T(8,128)(2,1)S(1)}, u32[]{:S(2)}, u32[]{:S(2)}) collective-permute-start(bf16[2,128,512]{2,1,0:T(8,128)(2,1)S(1)} %get-tuple-element.38.high_ref), channel_id=1, source_target_pairs={{0,3},{1,0},{2,1},{3,2},{4,7},{5,4},{6,5},{7,6},{8,11},{9,8},{10,9... | collective-permute-start | bytes 786440 | tf_op jit(solution)/shard_map/ppermute | solution.py:41
  70.4 3.1 %collective-permute-start.29 = (bf16[2,128,512]{2,1,0:T(8,128)(2,1)S(1)}, bf16[2,128,512]{2,1,0:T(8,128)(2,1)S(1)}, u32[]{:S(2)}, u32[]{:S(2)}) collective-permute-start(bf16[2,128,512]{2,1,0:T(8,128)(2,1)S(1)} %get-tuple-element.38.high_ref), channel_id=1, source_target_pairs={{0,1},{1,2},{2,3},{3,0},{4,5},{5,6},{6,7},{7,4},{8,9},{9,10},{10,1... | collective-permute-start | bytes 786440 | tf_op jit(solution)/shard_map/ppermute | solution.py:41
  76.6 2.1 %collective-permute-done.30.rl_ref = bf16[2,128,512]{2,1,0:T(8,128)(2,1)S(1)} collective-permute-done((bf16[2,128,512]{2,1,0:T(8,128)(2,1)S(1)}, bf16[2,128,512]{2,1,0:T(8,128)(2,1)S(1)}, u32[]{:S(2)}, u32[]{:S(2)}) %collective-permute-start.30) | collective-permute-done | bytes 262176 | tf_op jit(solution)/shard_map/ppermute | solution.py:41
  78.7 2.3 %collective-permute-done.32.fl_ref = bf16[2,128,512]{2,1,0:T(8,128)(2,1)S(1)} collective-permute-done((bf16[2,128,512]{2,1,0:T(8,128)(2,1)S(1)}, bf16[2,128,512]{2,1,0:T(8,128)(2,1)S(1)}, u32[]{:S(2)}, u32[]{:S(2)}) %collective-permute-start.32) | collective-permute-done | bytes 262176 | tf_op jit(solution)/shard_map/ppermute | solution.py:41
  80.9 2.5 %collective-permute-done.33.fh_ref = bf16[2,128,512]{2,1,0:T(8,128)(2,1)S(1)} collective-permute-done((bf16[2,128,512]{2,1,0:T(8,128)(2,1)S(1)}, bf16[2,128,512]{2,1,0:T(8,128)(2,1)S(1)}, u32[]{:S(2)}, u32[]{:S(2)}) %collective-permute-start.33) | collective-permute-done | bytes 262176 | tf_op jit(solution)/shard_map/ppermute | solution.py:41
  84.1 3.1 %collective-permute-start.37 = (bf16[2,128,512]{2,1,0:T(8,128)(2,1)S(1)}, bf16[2,128,512]{2,1,0:T(8,128)(2,1)S(1)}, u32[]{:S(2)}, u32[]{:S(2)}) collective-permute-start(bf16[2,128,512]{2,1,0:T(8,128)(2,1)S(1)} %get-tuple-element.40.th_ref), channel_id=1, source_target_pairs={{0,12},{1,13},{2,14},{3,15},{4,0},{5,1},{6,2},{7,3},{8,4},{9,5},{1... | collective-permute-start | bytes 786440 | tf_op jit(solution)/shard_map/ppermute | solution.py:41
  87.3 1.9 %collective-permute-start.36 = (bf16[2,128,512]{2,1,0:T(8,128)(2,1)S(1)}, bf16[2,128,512]{2,1,0:T(8,128)(2,1)S(1)}, u32[]{:S(2)}, u32[]{:S(2)}) collective-permute-start(bf16[2,128,512]{2,1,0:T(8,128)(2,1)S(1)} %get-tuple-element.39.tl_ref), channel_id=1, source_target_pairs={{0,12},{1,13},{2,14},{3,15},{4,0},{5,1},{6,2},{7,3},{8,4},{9,5},{1... | collective-permute-start | bytes 786440 | tf_op jit(solution)/shard_map/ppermute | solution.py:41
  89.3 2.2 %collective-permute-done.34.ll_ref = bf16[2,128,512]{2,1,0:T(8,128)(2,1)S(1)} collective-permute-done((bf16[2,128,512]{2,1,0:T(8,128)(2,1)S(1)}, bf16[2,128,512]{2,1,0:T(8,128)(2,1)S(1)}, u32[]{:S(2)}, u32[]{:S(2)}) %collective-permute-start.34) | collective-permute-done | bytes 262176 | tf_op jit(solution)/shard_map/ppermute | solution.py:41
  91.5 3.3 %collective-permute-start.39 = (bf16[2,128,512]{2,1,0:T(8,128)(2,1)S(1)}, bf16[2,128,512]{2,1,0:T(8,128)(2,1)S(1)}, u32[]{:S(2)}, u32[]{:S(2)}) collective-permute-start(bf16[2,128,512]{2,1,0:T(8,128)(2,1)S(1)} %collective-permute-done.37.rh_ref), channel_id=1, source_target_pairs={{0,12},{1,13},{2,14},{3,15},{4,0},{5,1},{6,2},{7,3},{8,4},{9,5},{1... | collective-permute-start | bytes 786440 | tf_op jit(solution)/shard_map/ppermute | solution.py:41
  94.9 1.9 %collective-permute-done.35.lh_ref = bf16[2,128,512]{2,1,0:T(8,128)(2,1)S(1)} collective-permute-done((bf16[2,128,512]{2,1,0:T(8,128)(2,1)S(1)}, bf16[2,128,512]{2,1,0:T(8,128)(2,1)S(1)}, u32[]{:S(2)}, u32[]{:S(2)}) %collective-permute-start.35) | collective-permute-done | bytes 262176 | tf_op jit(solution)/shard_map/ppermute | solution.py:41
  (87 shorter events, 31.6 us)
Async XLA Ops:
  2.2 7.8 %collective-permute-start.2 = (bf16[128,512]{1,0:T(8,128)(2,1)}, bf16[128,512]{1,0:T(8,128)(2,1)S(1)}, u32[]{:S(2)}, u32[]{:S(2)}) collective-permute-start(bf16[128,512]{1,0:T(8,128)(2,1)} %bitcast.13), channel_id=1, source_target_pairs={{0,3},{1,0},{2,1},{3,2},{4,7},{5,4},{6,5},{7,6},{8,11},{9,8},{10,9... | collective-permute-start | bytes 393224 | tf_op jit(solution)/shard_map/ppermute | solution.py:41
  2.2 7.8 %collective-permute-start.1 = (bf16[128,512]{1,0:T(8,128)(2,1)}, bf16[128,512]{1,0:T(8,128)(2,1)S(1)}, u32[]{:S(2)}, u32[]{:S(2)}) collective-permute-start(bf16[128,512]{1,0:T(8,128)(2,1)} %bitcast.14), channel_id=1, source_target_pairs={{0,2},{1,3},{2,0},{3,1},{4,6},{5,7},{6,4},{7,5},{8,10},{9,11},{10,... | collective-permute-start | bytes 393224 | tf_op jit(solution)/shard_map/ppermute | solution.py:41
  6.1 7.8 %collective-permute-start.3 = (bf16[2,128,512]{2,1,0:T(8,128)(2,1)S(1)}, bf16[2,128,512]{2,1,0:T(8,128)(2,1)S(1)}, u32[]{:S(2)}, u32[]{:S(2)}) collective-permute-start(bf16[2,128,512]{2,1,0:T(8,128)(2,1)S(1)} %join_kernel.1.low_ref), channel_id=1, source_target_pairs={{0,4},{1,5},{2,6},{3,7},{4,8},{5,9},{6,10},{7,11},{8,12},{9,13},{1... | collective-permute-start | bytes 786440 | tf_op jit(solution)/shard_map/ppermute | solution.py:41
  11.8 10.1 %collective-permute-start.5 = (bf16[2,128,512]{2,1,0:T(8,128)(2,1)S(1)}, bf16[2,128,512]{2,1,0:T(8,128)(2,1)S(1)}, u32[]{:S(2)}, u32[]{:S(2)}) collective-permute-start(bf16[2,128,512]{2,1,0:T(8,128)(2,1)S(1)} %join_kernel.1.low_ref), channel_id=1, source_target_pairs={{0,12},{1,13},{2,14},{3,15},{4,0},{5,1},{6,2},{7,3},{8,4},{9,5},{1... | collective-permute-start | bytes 786440 | tf_op jit(solution)/shard_map/ppermute | solution.py:41
  12.6 9.4 %collective-permute-start.4 = (bf16[2,128,512]{2,1,0:T(8,128)(2,1)S(1)}, bf16[2,128,512]{2,1,0:T(8,128)(2,1)S(1)}, u32[]{:S(2)}, u32[]{:S(2)}) collective-permute-start(bf16[2,128,512]{2,1,0:T(8,128)(2,1)S(1)} %pad_maximum_fusion.high_ref), channel_id=1, source_target_pairs={{0,4},{1,5},{2,6},{3,7},{4,8},{5,9},{6,10},{7,11},{8,12},{9,13},{1... | collective-permute-start | bytes 786440 | tf_op jit(solution)/shard_map/ppermute | solution.py:41
  13.9 9.9 %collective-permute-start.7 = (bf16[2,128,512]{2,1,0:T(8,128)(2,1)S(1)}, bf16[2,128,512]{2,1,0:T(8,128)(2,1)S(1)}, u32[]{:S(2)}, u32[]{:S(2)}) collective-permute-start(bf16[2,128,512]{2,1,0:T(8,128)(2,1)S(1)} %collective-permute-done.3.l0_ref), channel_id=1, source_target_pairs={{0,4},{1,5},{2,6},{3,7},{4,8},{5,9},{6,10},{7,11},{8,12},{9,13},{1... | collective-permute-start | bytes 786440 | tf_op jit(solution)/shard_map/ppermute | solution.py:41
  26.8 14.2 %collective-permute-start.20 = (bf16[1,128,256]{2,1,0:T(8,128)(2,1)S(1)}, bf16[1,128,256]{2,1,0:T(8,128)(2,1)S(1)}, u32[]{:S(2)}, u32[]{:S(2)}) collective-permute-start(bf16[1,128,256]{2,1,0:T(8,128)(2,1)S(1)} %copy-done.3), channel_id=1, source_target_pairs={{0,128},{1,129},{2,130},{3,131},{4,132},{5,133},{6,134},{7,135},{8... | collective-permute-start | bytes 196616 | tf_op jit(solution)/shard_map/ppermute | solution.py:51
  31.2 9.9 %collective-permute-start.15 = (bf16[128,128]{1,0:T(8,128)(2,1)S(1)}, bf16[128,128]{1,0:T(8,128)(2,1)S(1)}, u32[]{:S(2)}, u32[]{:S(2)}) collective-permute-start(bf16[128,128]{1,0:T(8,128)(2,1)S(1)} %get-tuple-element.27), channel_id=1, source_target_pairs={{0,64},{1,65},{2,66},{3,67},{4,68},{5,69},{6,70},{7,71},{8,72},{9,... | collective-permute-start | bytes 98312 | tf_op jit(solution)/shard_map/ppermute | solution.py:51
  38.5 8.1 %collective-permute-start.14 = (bf16[2,128,128]{2,1,0:T(8,128)(2,1)S(1)}, bf16[2,128,128]{2,1,0:T(8,128)(2,1)S(1)}, u32[]{:S(2)}, u32[]{:S(2)}) collective-permute-start(bf16[2,128,128]{2,1,0:T(8,128)(2,1)S(1)} %get-tuple-element.25.span_ref), channel_id=1, source_target_pairs={{0,48},{1,49},{2,50},{3,51},{4,52},{5,53},{6,54},{7,55},{8,56},{9,... | collective-permute-start | bytes 196616 | tf_op jit(solution)/shard_map/ppermute | solution.py:51
  40.4 8.0 %collective-permute-start.12 = (bf16[2,128,128]{2,1,0:T(8,128)(2,1)S(1)}, bf16[2,128,128]{2,1,0:T(8,128)(2,1)S(1)}, u32[]{:S(2)}, u32[]{:S(2)}) collective-permute-start(bf16[2,128,128]{2,1,0:T(8,128)(2,1)S(1)} %get-tuple-element.25.span_ref), channel_id=1, source_target_pairs={{0,16},{1,17},{2,18},{3,19},{4,20},{5,21},{6,22},{7,23},{8,24},{9,... | collective-permute-start | bytes 196616 | tf_op jit(solution)/shard_map/ppermute | solution.py:51
  52.3 7.7 %collective-permute-start.22 = (bf16[2,128,512]{2,1,0:T(8,128)(2,1)S(1)}, bf16[2,128,512]{2,1,0:T(8,128)(2,1)S(1)}, u32[]{:S(2)}, u32[]{:S(2)}) collective-permute-start(bf16[2,128,512]{2,1,0:T(8,128)(2,1)S(1)} %get-tuple-element.32), channel_id=1, source_target_pairs={{0,4},{1,5},{2,6},{3,7},{4,8},{5,9},{6,10},{7,11},{8,12},{9,13},{1... | collective-permute-start | bytes 786440 | tf_op jit(solution)/shard_map/ppermute | solution.py:41
  52.4 7.7 %collective-permute-start.26 = (bf16[2,128,512]{2,1,0:T(8,128)(2,1)S(1)}, bf16[2,128,512]{2,1,0:T(8,128)(2,1)S(1)}, u32[]{:S(2)}, u32[]{:S(2)}) collective-permute-start(bf16[2,128,512]{2,1,0:T(8,128)(2,1)S(1)} %get-tuple-element.36), channel_id=1, source_target_pairs={{0,12},{1,13},{2,14},{3,15},{4,0},{5,1},{6,2},{7,3},{8,4},{9,5},{1... | collective-permute-start | bytes 786440 | tf_op jit(solution)/shard_map/ppermute | solution.py:41
  55.8 7.8 %collective-permute-start.24 = (bf16[2,128,512]{2,1,0:T(8,128)(2,1)S(1)}, bf16[2,128,512]{2,1,0:T(8,128)(2,1)S(1)}, u32[]{:S(2)}, u32[]{:S(2)}) collective-permute-start(bf16[2,128,512]{2,1,0:T(8,128)(2,1)S(1)} %get-tuple-element.33), channel_id=1, source_target_pairs={{0,4},{1,5},{2,6},{3,7},{4,8},{5,9},{6,10},{7,11},{8,12},{9,13},{1... | collective-permute-start | bytes 786440 | tf_op jit(solution)/shard_map/ppermute | solution.py:41
  55.8 7.8 %collective-permute-start.25 = (bf16[2,128,512]{2,1,0:T(8,128)(2,1)S(1)}, bf16[2,128,512]{2,1,0:T(8,128)(2,1)S(1)}, u32[]{:S(2)}, u32[]{:S(2)}) collective-permute-start(bf16[2,128,512]{2,1,0:T(8,128)(2,1)S(1)} %get-tuple-element.34), channel_id=1, source_target_pairs={{0,12},{1,13},{2,14},{3,15},{4,0},{5,1},{6,2},{7,3},{8,4},{9,5},{1... | collective-permute-start | bytes 786440 | tf_op jit(solution)/shard_map/ppermute | solution.py:41
  60.1 7.7 %collective-permute-start.23 = (bf16[2,128,512]{2,1,0:T(8,128)(2,1)S(1)}, bf16[2,128,512]{2,1,0:T(8,128)(2,1)S(1)}, u32[]{:S(2)}, u32[]{:S(2)}) collective-permute-start(bf16[2,128,512]{2,1,0:T(8,128)(2,1)S(1)} %add_kernel.2), channel_id=1, source_target_pairs={{0,4},{1,5},{2,6},{3,7},{4,8},{5,9},{6,10},{7,11},{8,12},{9,13},{1... | collective-permute-start | bytes 786440 | tf_op jit(solution)/shard_map/ppermute | solution.py:41
  68.3 7.6 %collective-permute-start.31 = (bf16[2,128,512]{2,1,0:T(8,128)(2,1)S(1)}, bf16[2,128,512]{2,1,0:T(8,128)(2,1)S(1)}, u32[]{:S(2)}, u32[]{:S(2)}) collective-permute-start(bf16[2,128,512]{2,1,0:T(8,128)(2,1)S(1)} %get-tuple-element.38.high_ref), channel_id=1, source_target_pairs={{0,3},{1,0},{2,1},{3,2},{4,7},{5,4},{6,5},{7,6},{8,11},{9,8},{10,9... | collective-permute-start | bytes 786440 | tf_op jit(solution)/shard_map/ppermute | solution.py:41
  70.2 8.5 %collective-permute-start.30 = (bf16[2,128,512]{2,1,0:T(8,128)(2,1)S(1)}, bf16[2,128,512]{2,1,0:T(8,128)(2,1)S(1)}, u32[]{:S(2)}, u32[]{:S(2)}) collective-permute-start(bf16[2,128,512]{2,1,0:T(8,128)(2,1)S(1)} %get-tuple-element.37.low_ref), channel_id=1, source_target_pairs={{0,3},{1,0},{2,1},{3,2},{4,7},{5,4},{6,5},{7,6},{8,11},{9,8},{10,9... | collective-permute-start | bytes 786440 | tf_op jit(solution)/shard_map/ppermute | solution.py:41
  70.4 8.3 %collective-permute-start.29 = (bf16[2,128,512]{2,1,0:T(8,128)(2,1)S(1)}, bf16[2,128,512]{2,1,0:T(8,128)(2,1)S(1)}, u32[]{:S(2)}, u32[]{:S(2)}) collective-permute-start(bf16[2,128,512]{2,1,0:T(8,128)(2,1)S(1)} %get-tuple-element.38.high_ref), channel_id=1, source_target_pairs={{0,1},{1,2},{2,3},{3,0},{4,5},{5,6},{6,7},{7,4},{8,9},{9,10},{10,1... | collective-permute-start | bytes 786440 | tf_op jit(solution)/shard_map/ppermute | solution.py:41
  75.9 7.6 %collective-permute-start.33 = (bf16[2,128,512]{2,1,0:T(8,128)(2,1)S(1)}, bf16[2,128,512]{2,1,0:T(8,128)(2,1)S(1)}, u32[]{:S(2)}, u32[]{:S(2)}) collective-permute-start(bf16[2,128,512]{2,1,0:T(8,128)(2,1)S(1)} %collective-permute-done.31.rh_ref), channel_id=1, source_target_pairs={{0,3},{1,0},{2,1},{3,2},{4,7},{5,4},{6,5},{7,6},{8,11},{9,8},{10,9... | collective-permute-start | bytes 786440 | tf_op jit(solution)/shard_map/ppermute | solution.py:41
  83.7 7.8 %collective-permute-start.34 = (bf16[2,128,512]{2,1,0:T(8,128)(2,1)S(1)}, bf16[2,128,512]{2,1,0:T(8,128)(2,1)S(1)}, u32[]{:S(2)}, u32[]{:S(2)}) collective-permute-start(bf16[2,128,512]{2,1,0:T(8,128)(2,1)S(1)} %get-tuple-element.39.tl_ref), channel_id=1, source_target_pairs={{0,4},{1,5},{2,6},{3,7},{4,8},{5,9},{6,10},{7,11},{8,12},{9,13},{1... | collective-permute-start | bytes 786440 | tf_op jit(solution)/shard_map/ppermute | solution.py:41
  87.3 7.6 %collective-permute-start.36 = (bf16[2,128,512]{2,1,0:T(8,128)(2,1)S(1)}, bf16[2,128,512]{2,1,0:T(8,128)(2,1)S(1)}, u32[]{:S(2)}, u32[]{:S(2)}) collective-permute-start(bf16[2,128,512]{2,1,0:T(8,128)(2,1)S(1)} %get-tuple-element.39.tl_ref), channel_id=1, source_target_pairs={{0,12},{1,13},{2,14},{3,15},{4,0},{5,1},{6,2},{7,3},{8,4},{9,5},{1... | collective-permute-start | bytes 786440 | tf_op jit(solution)/shard_map/ppermute | solution.py:41
  89.2 7.6 %collective-permute-start.35 = (bf16[2,128,512]{2,1,0:T(8,128)(2,1)S(1)}, bf16[2,128,512]{2,1,0:T(8,128)(2,1)S(1)}, u32[]{:S(2)}, u32[]{:S(2)}) collective-permute-start(bf16[2,128,512]{2,1,0:T(8,128)(2,1)S(1)} %get-tuple-element.40.th_ref), channel_id=1, source_target_pairs={{0,4},{1,5},{2,6},{3,7},{4,8},{5,9},{6,10},{7,11},{8,12},{9,13},{1... | collective-permute-start | bytes 786440 | tf_op jit(solution)/shard_map/ppermute | solution.py:41
  91.5 8.1 %collective-permute-start.38 = (bf16[2,128,512]{2,1,0:T(8,128)(2,1)S(1)}, bf16[2,128,512]{2,1,0:T(8,128)(2,1)S(1)}, u32[]{:S(2)}, u32[]{:S(2)}) collective-permute-start(bf16[2,128,512]{2,1,0:T(8,128)(2,1)S(1)} %collective-permute-done.34.ll_ref), channel_id=1, source_target_pairs={{0,4},{1,5},{2,6},{3,7},{4,8},{5,9},{6,10},{7,11},{8,12},{9,13},{1... | collective-permute-start | bytes 786440 | tf_op jit(solution)/shard_map/ppermute | solution.py:41
  91.5 8.1 %collective-permute-start.39 = (bf16[2,128,512]{2,1,0:T(8,128)(2,1)S(1)}, bf16[2,128,512]{2,1,0:T(8,128)(2,1)S(1)}, u32[]{:S(2)}, u32[]{:S(2)}) collective-permute-start(bf16[2,128,512]{2,1,0:T(8,128)(2,1)S(1)} %collective-permute-done.37.rh_ref), channel_id=1, source_target_pairs={{0,12},{1,13},{2,14},{3,15},{4,0},{5,1},{6,2},{7,3},{8,4},{9,5},{1... | collective-permute-start | bytes 786440 | tf_op jit(solution)/shard_map/ppermute | solution.py:41
  (24 other events, 144.7 us)

commit v5 on v4

--- a/solution.py
+++ b/solution.py
@@ -354,7 +354,18 @@
     place(info, ((2, fl_ref, fh_ref),), out_ref, sems)
 
 
+def with_scalars(kernel):
+    def wrapped(*refs):
+        kernel([ref[0] for ref in refs[:5]], *refs[5:])
+
+    wrapped.__name__ = kernel.__name__
+    return wrapped
+
+
 def call(kernel, outs, in_specs, out_specs, flops, *args, scratch=(), limit=24 << 20, aliases=None):
+    if in_specs[0] is SMEM:
+        kernel, in_specs, args = with_scalars(kernel), [SMEM] * 4 + in_specs, (*args[0], *args[1:])
+        aliases = {n + 4: m for n, m in (aliases or {}).items()}
     size = sum(x.size * x.dtype.itemsize for x in args)
     return pl.pallas_call(
         kernel,
@@ -376,7 +387,7 @@
     high, low = rank // SIDE, rank % SIDE
     a = jnp.where(group == 0, high, low)
     b = jnp.where(group == 0, low, high)
-    info = jnp.stack([group, a, b, ctx, rank % 2]).astype(jnp.int32)
+    info = [x.astype(jnp.int32).reshape(1) for x in (group, a, b, ctx, rank % 2)]
     st = jax.ShapeDtypeStruct
     dma = pltpu.SemaphoreType.DMA
     both = (0, 1)

time: 101 us -> 99.1 us (0.981)
  Pallas kernels: 14.2 us -> 9.67 us
  waiting for transfers between devices: 30.5 us -> 32.1 us
    pallas_call x13, Pallas kernels: 14.2 us -> 9.67 us  [call(): pl.pallas_call(kernel, out_shape=outs, in_specs=in_specs, out_specs=out_s...]
  transfers between devices with their start and end apart: 40 -> 40, of which waited for: 17 -> 18; matrix products, arithmetic and copies ran while one was open for 0% -> 0% of each run, Pallas kernels for 9% -> 6%
where the time goes in v5:
time: 99.1 us; the launch traced here: 98.9 us
  starting transfers between devices  52.9 us (53%)
  waiting for transfers between devices  32.1 us (32%)
  Pallas kernels  9.67 us (10%)
  local copies, waits for them, and re-layouts  3.8 us (4%)
    ppermute x27, starting transfers between devices, shift(): return lax.ppermute(block, ('group', 'tp'), tp_route(step_a, step_b))  39.3 us
    ppermute x27, waiting for transfers between devices, shift(): return lax.ppermute(block, ('group', 'tp'), tp_route(step_a, step_b))  25.2 us
    ppermute x13, starting transfers between devices, routed(): return lax.ppermute(block, ('group', 'ctx', 'tp'), route)  13.6 us
    pallas_call x13, Pallas kernels, call(): pl.pallas_call(kernel, out_shape=outs, in_specs=in_specs, out_specs=out_s...  9.67 us
    ppermute x13, waiting for transfers between devices, routed(): return lax.ppermute(block, ('group', 'ctx', 'tp'), route)  6.88 us
    unnamed x16, local copies, waits for them, and re-layouts  3.8 us
  transfers between devices with their start and end apart: 40, of which 18 were waited for; matrix products, arithmetic and copies ran while one was open for 0% of the time, Pallas kernels for 6%

profile of v5, /device:TPU:6, one launch (start us, length us, event | category | flops | bytes accessed | tf_op | source)
XLA Modules:
  0.0 98.9 jit_solution(14632188400702598865)
XLA Ops:
  0.0 2.2 %collective-permute-start = (bf16[128,512]{1,0:T(8,128)(2,1)}, bf16[128,512]{1,0:T(8,128)(2,1)S(1)}, u32[]{:S(2)}, u32[]{:S(2)}) collective-permute-start(bf16[128,512]{1,0:T(8,128)(2,1)} %bitcast.12), channel_id=1, source_target_pairs={{0,1},{1,2},{2,3},{3,0},{4,5},{5,6},{6,7},{7,4},{8,9},{9,10},{10,1... | collective-permute-start | bytes 393224 | tf_op jit(solution)/shard_map/ppermute | solution.py:41
  7.8 2.2 %collective-permute-done.2 = bf16[128,512]{1,0:T(8,128)(2,1)S(1)} collective-permute-done((bf16[128,512]{1,0:T(8,128)(2,1)}, bf16[128,512]{1,0:T(8,128)(2,1)S(1)}, u32[]{:S(2)}, u32[]{:S(2)}) %collective-permute-start.2) | collective-permute-done | bytes 131104 | tf_op jit(solution)/shard_map/ppermute | solution.py:41
  14.2 2.3 %collective-permute-done.6.refs_9_ = bf16[2,128,512]{2,1,0:T(8,128)(2,1)S(1)} collective-permute-done((bf16[2,128,512]{2,1,0:T(8,128)(2,1)S(1)}, bf16[2,128,512]{2,1,0:T(8,128)(2,1)S(1)}, u32[]{:S(2)}, u32[]{:S(2)}) %collective-permute-start.6) | collective-permute-done | bytes 262176 | tf_op jit(solution)/shard_map/ppermute | solution.py:41
  16.5 2.9 %collective-permute-start.8 = (bf16[2,128,512]{2,1,0:T(8,128)(2,1)S(1)}, bf16[2,128,512]{2,1,0:T(8,128)(2,1)S(1)}, u32[]{:S(2)}, u32[]{:S(2)}) collective-permute-start(bf16[2,128,512]{2,1,0:T(8,128)(2,1)S(1)} %collective-permute-done.6.refs_9_), channel_id=1, source_target_pairs={{0,12},{1,13},{2,14},{3,15},{4,0},{5,1},{6,2},{7,3},{8,4},{9,5},{1... | collective-permute-start | bytes 786440 | tf_op jit(solution)/shard_map/ppermute | solution.py:41
  23.7 2.0 %collective-permute-start.10 = (bf16[128,128]{1,0:T(8,128)(2,1)S(1)}, bf16[128,128]{1,0:T(8,128)(2,1)S(1)}, u32[]{:S(2)}, u32[]{:S(2)}) collective-permute-start(bf16[128,128]{1,0:T(8,128)(2,1)S(1)} %project_far.1.refs_5_), channel_id=1, source_target_pairs={{0,128},{1,129},{2,130},{3,131},{4,132},{5,133},{6,134},{7,135},{8... | collective-permute-start | bytes 98312 | tf_op jit(solution)/shard_map/ppermute | solution.py:51
  27.0 2.6 %collective-permute-done.9.refs_6_ = bf16[128,128]{1,0:T(8,128)(2,1)S(1)} collective-permute-done((bf16[128,128]{1,0:T(8,128)(2,1)S(1)}, bf16[128,128]{1,0:T(8,128)(2,1)S(1)}, u32[]{:S(2)}, u32[]{:S(2)}) %collective-permute-start.9) | collective-permute-done | bytes 32800 | tf_op jit(solution)/shard_map/ppermute | solution.py:51
  29.6 7.3 %collective-permute-start.15 = (bf16[128,128]{1,0:T(8,128)(2,1)S(1)}, bf16[128,128]{1,0:T(8,128)(2,1)S(1)}, u32[]{:S(2)}, u32[]{:S(2)}) collective-permute-start(bf16[128,128]{1,0:T(8,128)(2,1)S(1)} %get-tuple-element.27), channel_id=1, source_target_pairs={{0,64},{1,65},{2,66},{3,67},{4,68},{5,69},{6,70},{7,71},{8,72},{9,... | collective-permute-start | bytes 98312 | tf_op jit(solution)/shard_map/ppermute | solution.py:51
  36.9 1.9 %collective-permute-start.14 = (bf16[2,128,128]{2,1,0:T(8,128)(2,1)S(1)}, bf16[2,128,128]{2,1,0:T(8,128)(2,1)S(1)}, u32[]{:S(2)}, u32[]{:S(2)}) collective-permute-start(bf16[2,128,128]{2,1,0:T(8,128)(2,1)S(1)} %get-tuple-element.25.refs_6_), channel_id=1, source_target_pairs={{0,48},{1,49},{2,50},{3,51},{4,52},{5,53},{6,54},{7,55},{8,56},{9,... | collective-permute-start | bytes 196616 | tf_op jit(solution)/shard_map/ppermute | solution.py:51
  39.6 4.0 %cache_kernel.1.refs_19_ = f32[2,2,64,128]{3,2,1,0:T(8,128)S(1)} custom-call(s32[1]{0:T(128)} %bitcast.refs_0_, s32[1]{0:T(128)} %bitcast.1.refs_1_, s32[1]{0:T(128)} %bitcast.2.refs_2_, s32[1]{0:T(128)} %bitcast.3.refs_3_, s32[1]{0:T(128)} %bitcast.4.refs_4_, bf16[1,128,256]{2,1,0:T(8,128)(2,1)S(1)} %copy-done.3, ...), custom_call_target="tpu_custom_call" | custom-call | flops 1000 | bytes 8521236 | tf_op jit(solution)/shard_map/cache_kernel/pallas_call | solution.py:370
  48.2 2.0 %finish_kernel.1 = (f32[4,128,512]{2,1,0:T(8,128)S(1)}, bf16[2,128,512]{2,1,0:T(8,128)(2,1)S(1)}, bf16[2,128,512]{2,1,0:T(8,128)(2,1)S(1)}, bf16[2,128,512]{2,1,...) custom-call(s32[1]{0:T(128)} %bitcast.refs_0_, ...), custom_call_target="tpu_custom_call" | custom-call | flops 800000000 | bytes 5113364 | tf_op jit(solution)/shard_map/finish_kernel/pallas_call | solution.py:370
  50.3 3.8 %collective-permute-start.26 = (bf16[2,128,512]{2,1,0:T(8,128)(2,1)S(1)}, bf16[2,128,512]{2,1,0:T(8,128)(2,1)S(1)}, u32[]{:S(2)}, u32[]{:S(2)}) collective-permute-start(bf16[2,128,512]{2,1,0:T(8,128)(2,1)S(1)} %get-tuple-element.36), channel_id=1, source_target_pairs={{0,12},{1,13},{2,14},{3,15},{4,0},{5,1},{6,2},{7,3},{8,4},{9,5},{1... | collective-permute-start | bytes 786440 | tf_op jit(solution)/shard_map/ppermute | solution.py:41
  54.1 3.2 %collective-permute-start.25 = (bf16[2,128,512]{2,1,0:T(8,128)(2,1)S(1)}, bf16[2,128,512]{2,1,0:T(8,128)(2,1)S(1)}, u32[]{:S(2)}, u32[]{:S(2)}) collective-permute-start(bf16[2,128,512]{2,1,0:T(8,128)(2,1)S(1)} %get-tuple-element.34), channel_id=1, source_target_pairs={{0,12},{1,13},{2,14},{3,15},{4,0},{5,1},{6,2},{7,3},{8,4},{9,5},{1... | collective-permute-start | bytes 786440 | tf_op jit(solution)/shard_map/ppermute | solution.py:41
  58.6 3.3 %collective-permute-start.27 = (bf16[2,128,512]{2,1,0:T(8,128)(2,1)S(1)}, bf16[2,128,512]{2,1,0:T(8,128)(2,1)S(1)}, u32[]{:S(2)}, u32[]{:S(2)}) collective-permute-start(bf16[2,128,512]{2,1,0:T(8,128)(2,1)S(1)} %add_kernel.3), channel_id=1, source_target_pairs={{0,12},{1,13},{2,14},{3,15},{4,0},{5,1},{6,2},{7,3},{8,4},{9,5},{1... | collective-permute-start | bytes 786440 | tf_op jit(solution)/shard_map/ppermute | solution.py:41
  61.9 4.2 %collective-permute-done.23.ll_ref = bf16[2,128,512]{2,1,0:T(8,128)(2,1)S(1)} collective-permute-done((bf16[2,128,512]{2,1,0:T(8,128)(2,1)S(1)}, bf16[2,128,512]{2,1,0:T(8,128)(2,1)S(1)}, u32[]{:S(2)}, u32[]{:S(2)}) %collective-permute-start.23) | collective-permute-done | bytes 262176 | tf_op jit(solution)/shard_map/ppermute | solution.py:41
  66.6 2.0 %collective-permute-start.31 = (bf16[2,128,512]{2,1,0:T(8,128)(2,1)S(1)}, bf16[2,128,512]{2,1,0:T(8,128)(2,1)S(1)}, u32[]{:S(2)}, u32[]{:S(2)}) collective-permute-start(bf16[2,128,512]{2,1,0:T(8,128)(2,1)S(1)} %get-tuple-element.38.high_ref), channel_id=1, source_target_pairs={{0,3},{1,0},{2,1},{3,2},{4,7},{5,4},{6,5},{7,6},{8,11},{9,8},{10,9... | collective-permute-start | bytes 786440 | tf_op jit(solution)/shard_map/ppermute | solution.py:41
  68.7 3.1 %collective-permute-start.29 = (bf16[2,128,512]{2,1,0:T(8,128)(2,1)S(1)}, bf16[2,128,512]{2,1,0:T(8,128)(2,1)S(1)}, u32[]{:S(2)}, u32[]{:S(2)}) collective-permute-start(bf16[2,128,512]{2,1,0:T(8,128)(2,1)S(1)} %get-tuple-element.38.high_ref), channel_id=1, source_target_pairs={{0,1},{1,2},{2,3},{3,0},{4,5},{5,6},{6,7},{7,4},{8,9},{9,10},{10,1... | collective-permute-start | bytes 786440 | tf_op jit(solution)/shard_map/ppermute | solution.py:41
  75.0 2.1 %collective-permute-done.30.rl_ref = bf16[2,128,512]{2,1,0:T(8,128)(2,1)S(1)} collective-permute-done((bf16[2,128,512]{2,1,0:T(8,128)(2,1)S(1)}, bf16[2,128,512]{2,1,0:T(8,128)(2,1)S(1)}, u32[]{:S(2)}, u32[]{:S(2)}) %collective-permute-start.30) | collective-permute-done | bytes 262176 | tf_op jit(solution)/shard_map/ppermute | solution.py:41
  77.0 2.3 %collective-permute-done.32.fl_ref = bf16[2,128,512]{2,1,0:T(8,128)(2,1)S(1)} collective-permute-done((bf16[2,128,512]{2,1,0:T(8,128)(2,1)S(1)}, bf16[2,128,512]{2,1,0:T(8,128)(2,1)S(1)}, u32[]{:S(2)}, u32[]{:S(2)}) %collective-permute-start.32) | collective-permute-done | bytes 262176 | tf_op jit(solution)/shard_map/ppermute | solution.py:41
  79.3 2.5 %collective-permute-done.33.fh_ref = bf16[2,128,512]{2,1,0:T(8,128)(2,1)S(1)} collective-permute-done((bf16[2,128,512]{2,1,0:T(8,128)(2,1)S(1)}, bf16[2,128,512]{2,1,0:T(8,128)(2,1)S(1)}, u32[]{:S(2)}, u32[]{:S(2)}) %collective-permute-start.33) | collective-permute-done | bytes 262176 | tf_op jit(solution)/shard_map/ppermute | solution.py:41
  82.5 3.1 %collective-permute-start.37 = (bf16[2,128,512]{2,1,0:T(8,128)(2,1)S(1)}, bf16[2,128,512]{2,1,0:T(8,128)(2,1)S(1)}, u32[]{:S(2)}, u32[]{:S(2)}) collective-permute-start(bf16[2,128,512]{2,1,0:T(8,128)(2,1)S(1)} %get-tuple-element.40.refs_6_), channel_id=1, source_target_pairs={{0,12},{1,13},{2,14},{3,15},{4,0},{5,1},{6,2},{7,3},{8,4},{9,5},{1... | collective-permute-start | bytes 786440 | tf_op jit(solution)/shard_map/ppermute | solution.py:41
  85.6 1.9 %collective-permute-start.36 = (bf16[2,128,512]{2,1,0:T(8,128)(2,1)S(1)}, bf16[2,128,512]{2,1,0:T(8,128)(2,1)S(1)}, u32[]{:S(2)}, u32[]{:S(2)}) collective-permute-start(bf16[2,128,512]{2,1,0:T(8,128)(2,1)S(1)} %get-tuple-element.39.refs_5_), channel_id=1, source_target_pairs={{0,12},{1,13},{2,14},{3,15},{4,0},{5,1},{6,2},{7,3},{8,4},{9,5},{1... | collective-permute-start | bytes 786440 | tf_op jit(solution)/shard_map/ppermute | solution.py:41
  87.6 2.2 %collective-permute-done.34.refs_7_ = bf16[2,128,512]{2,1,0:T(8,128)(2,1)S(1)} collective-permute-done((bf16[2,128,512]{2,1,0:T(8,128)(2,1)S(1)}, bf16[2,128,512]{2,1,0:T(8,128)(2,1)S(1)}, u32[]{:S(2)}, u32[]{:S(2)}) %collective-permute-start.34) | collective-permute-done | bytes 262176 | tf_op jit(solution)/shard_map/ppermute | solution.py:41
  89.9 3.3 %collective-permute-start.39 = (bf16[2,128,512]{2,1,0:T(8,128)(2,1)S(1)}, bf16[2,128,512]{2,1,0:T(8,128)(2,1)S(1)}, u32[]{:S(2)}, u32[]{:S(2)}) collective-permute-start(bf16[2,128,512]{2,1,0:T(8,128)(2,1)S(1)} %collective-permute-done.37.refs_10_), channel_id=1, source_target_pairs={{0,12},{1,13},{2,14},{3,15},{4,0},{5,1},{6,2},{7,3},{8,4},{9,5},{1... | collective-permute-start | bytes 786440 | tf_op jit(solution)/shard_map/ppermute | solution.py:41
  93.2 1.9 %collective-permute-done.35.refs_8_ = bf16[2,128,512]{2,1,0:T(8,128)(2,1)S(1)} collective-permute-done((bf16[2,128,512]{2,1,0:T(8,128)(2,1)S(1)}, bf16[2,128,512]{2,1,0:T(8,128)(2,1)S(1)}, u32[]{:S(2)}, u32[]{:S(2)}) %collective-permute-start.35) | collective-permute-done | bytes 262176 | tf_op jit(solution)/shard_map/ppermute | solution.py:41
  (86 shorter events, 30.1 us)
Async XLA Ops:
  2.2 7.8 %collective-permute-start.2 = (bf16[128,512]{1,0:T(8,128)(2,1)}, bf16[128,512]{1,0:T(8,128)(2,1)S(1)}, u32[]{:S(2)}, u32[]{:S(2)}) collective-permute-start(bf16[128,512]{1,0:T(8,128)(2,1)} %bitcast.13), channel_id=1, source_target_pairs={{0,3},{1,0},{2,1},{3,2},{4,7},{5,4},{6,5},{7,6},{8,11},{9,8},{10,9... | collective-permute-start | bytes 393224 | tf_op jit(solution)/shard_map/ppermute | solution.py:41
  2.2 7.8 %collective-permute-start.1 = (bf16[128,512]{1,0:T(8,128)(2,1)}, bf16[128,512]{1,0:T(8,128)(2,1)S(1)}, u32[]{:S(2)}, u32[]{:S(2)}) collective-permute-start(bf16[128,512]{1,0:T(8,128)(2,1)} %bitcast.14), channel_id=1, source_target_pairs={{0,2},{1,3},{2,0},{3,1},{4,6},{5,7},{6,4},{7,5},{8,10},{9,11},{10,... | collective-permute-start | bytes 393224 | tf_op jit(solution)/shard_map/ppermute | solution.py:41
  6.1 7.8 %collective-permute-start.3 = (bf16[2,128,512]{2,1,0:T(8,128)(2,1)S(1)}, bf16[2,128,512]{2,1,0:T(8,128)(2,1)S(1)}, u32[]{:S(2)}, u32[]{:S(2)}) collective-permute-start(bf16[2,128,512]{2,1,0:T(8,128)(2,1)S(1)} %join_kernel.1.refs_5_), channel_id=1, source_target_pairs={{0,4},{1,5},{2,6},{3,7},{4,8},{5,9},{6,10},{7,11},{8,12},{9,13},{1... | collective-permute-start | bytes 786440 | tf_op jit(solution)/shard_map/ppermute | solution.py:41
  11.8 9.5 %collective-permute-start.5 = (bf16[2,128,512]{2,1,0:T(8,128)(2,1)S(1)}, bf16[2,128,512]{2,1,0:T(8,128)(2,1)S(1)}, u32[]{:S(2)}, u32[]{:S(2)}) collective-permute-start(bf16[2,128,512]{2,1,0:T(8,128)(2,1)S(1)} %join_kernel.1.refs_5_), channel_id=1, source_target_pairs={{0,12},{1,13},{2,14},{3,15},{4,0},{5,1},{6,2},{7,3},{8,4},{9,5},{1... | collective-permute-start | bytes 786440 | tf_op jit(solution)/shard_map/ppermute | solution.py:41
  12.6 8.7 %collective-permute-start.4 = (bf16[2,128,512]{2,1,0:T(8,128)(2,1)S(1)}, bf16[2,128,512]{2,1,0:T(8,128)(2,1)S(1)}, u32[]{:S(2)}, u32[]{:S(2)}) collective-permute-start(bf16[2,128,512]{2,1,0:T(8,128)(2,1)S(1)} %pad_maximum_fusion.refs_6_), channel_id=1, source_target_pairs={{0,4},{1,5},{2,6},{3,7},{4,8},{5,9},{6,10},{7,11},{8,12},{9,13},{1... | collective-permute-start | bytes 786440 | tf_op jit(solution)/shard_map/ppermute | solution.py:41
  13.9 9.2 %collective-permute-start.7 = (bf16[2,128,512]{2,1,0:T(8,128)(2,1)S(1)}, bf16[2,128,512]{2,1,0:T(8,128)(2,1)S(1)}, u32[]{:S(2)}, u32[]{:S(2)}) collective-permute-start(bf16[2,128,512]{2,1,0:T(8,128)(2,1)S(1)} %collective-permute-done.3.refs_6_), channel_id=1, source_target_pairs={{0,4},{1,5},{2,6},{3,7},{4,8},{5,9},{6,10},{7,11},{8,12},{9,13},{1... | collective-permute-start | bytes 786440 | tf_op jit(solution)/shard_map/ppermute | solution.py:41
  25.9 13.7 %collective-permute-start.20 = (bf16[1,128,256]{2,1,0:T(8,128)(2,1)S(1)}, bf16[1,128,256]{2,1,0:T(8,128)(2,1)S(1)}, u32[]{:S(2)}, u32[]{:S(2)}) collective-permute-start(bf16[1,128,256]{2,1,0:T(8,128)(2,1)S(1)} %copy-done.3), channel_id=1, source_target_pairs={{0,128},{1,129},{2,130},{3,131},{4,132},{5,133},{6,134},{7,135},{8... | collective-permute-start | bytes 196616 | tf_op jit(solution)/shard_map/ppermute | solution.py:51
  29.6 9.9 %collective-permute-start.15 = (bf16[128,128]{1,0:T(8,128)(2,1)S(1)}, bf16[128,128]{1,0:T(8,128)(2,1)S(1)}, u32[]{:S(2)}, u32[]{:S(2)}) collective-permute-start(bf16[128,128]{1,0:T(8,128)(2,1)S(1)} %get-tuple-element.27), channel_id=1, source_target_pairs={{0,64},{1,65},{2,66},{3,67},{4,68},{5,69},{6,70},{7,71},{8,72},{9,... | collective-permute-start | bytes 98312 | tf_op jit(solution)/shard_map/ppermute | solution.py:51
  38.9 8.0 %collective-permute-start.12 = (bf16[2,128,128]{2,1,0:T(8,128)(2,1)S(1)}, bf16[2,128,128]{2,1,0:T(8,128)(2,1)S(1)}, u32[]{:S(2)}, u32[]{:S(2)}) collective-permute-start(bf16[2,128,128]{2,1,0:T(8,128)(2,1)S(1)} %get-tuple-element.25.refs_6_), channel_id=1, source_target_pairs={{0,16},{1,17},{2,18},{3,19},{4,20},{5,21},{6,22},{7,23},{8,24},{9,... | collective-permute-start | bytes 196616 | tf_op jit(solution)/shard_map/ppermute | solution.py:51
  50.2 8.1 %collective-permute-start.22 = (bf16[2,128,512]{2,1,0:T(8,128)(2,1)S(1)}, bf16[2,128,512]{2,1,0:T(8,128)(2,1)S(1)}, u32[]{:S(2)}, u32[]{:S(2)}) collective-permute-start(bf16[2,128,512]{2,1,0:T(8,128)(2,1)S(1)} %get-tuple-element.32), channel_id=1, source_target_pairs={{0,4},{1,5},{2,6},{3,7},{4,8},{5,9},{6,10},{7,11},{8,12},{9,13},{1... | collective-permute-start | bytes 786440 | tf_op jit(solution)/shard_map/ppermute | solution.py:41
  50.3 8.2 %collective-permute-start.26 = (bf16[2,128,512]{2,1,0:T(8,128)(2,1)S(1)}, bf16[2,128,512]{2,1,0:T(8,128)(2,1)S(1)}, u32[]{:S(2)}, u32[]{:S(2)}) collective-permute-start(bf16[2,128,512]{2,1,0:T(8,128)(2,1)S(1)} %get-tuple-element.36), channel_id=1, source_target_pairs={{0,12},{1,13},{2,14},{3,15},{4,0},{5,1},{6,2},{7,3},{8,4},{9,5},{1... | collective-permute-start | bytes 786440 | tf_op jit(solution)/shard_map/ppermute | solution.py:41
  54.1 7.8 %collective-permute-start.24 = (bf16[2,128,512]{2,1,0:T(8,128)(2,1)S(1)}, bf16[2,128,512]{2,1,0:T(8,128)(2,1)S(1)}, u32[]{:S(2)}, u32[]{:S(2)}) collective-permute-start(bf16[2,128,512]{2,1,0:T(8,128)(2,1)S(1)} %get-tuple-element.33), channel_id=1, source_target_pairs={{0,4},{1,5},{2,6},{3,7},{4,8},{5,9},{6,10},{7,11},{8,12},{9,13},{1... | collective-permute-start | bytes 786440 | tf_op jit(solution)/shard_map/ppermute | solution.py:41
  54.1 7.8 %collective-permute-start.25 = (bf16[2,128,512]{2,1,0:T(8,128)(2,1)S(1)}, bf16[2,128,512]{2,1,0:T(8,128)(2,1)S(1)}, u32[]{:S(2)}, u32[]{:S(2)}) collective-permute-start(bf16[2,128,512]{2,1,0:T(8,128)(2,1)S(1)} %get-tuple-element.34), channel_id=1, source_target_pairs={{0,12},{1,13},{2,14},{3,15},{4,0},{5,1},{6,2},{7,3},{8,4},{9,5},{1... | collective-permute-start | bytes 786440 | tf_op jit(solution)/shard_map/ppermute | solution.py:41
  58.4 7.7 %collective-permute-start.23 = (bf16[2,128,512]{2,1,0:T(8,128)(2,1)S(1)}, bf16[2,128,512]{2,1,0:T(8,128)(2,1)S(1)}, u32[]{:S(2)}, u32[]{:S(2)}) collective-permute-start(bf16[2,128,512]{2,1,0:T(8,128)(2,1)S(1)} %add_kernel.2), channel_id=1, source_target_pairs={{0,4},{1,5},{2,6},{3,7},{4,8},{5,9},{6,10},{7,11},{8,12},{9,13},{1... | collective-permute-start | bytes 786440 | tf_op jit(solution)/shard_map/ppermute | solution.py:41
  58.6 7.5 %collective-permute-start.27 = (bf16[2,128,512]{2,1,0:T(8,128)(2,1)S(1)}, bf16[2,128,512]{2,1,0:T(8,128)(2,1)S(1)}, u32[]{:S(2)}, u32[]{:S(2)}) collective-permute-start(bf16[2,128,512]{2,1,0:T(8,128)(2,1)S(1)} %add_kernel.3), channel_id=1, source_target_pairs={{0,12},{1,13},{2,14},{3,15},{4,0},{5,1},{6,2},{7,3},{8,4},{9,5},{1... | collective-permute-start | bytes 786440 | tf_op jit(solution)/shard_map/ppermute | solution.py:41
  66.6 7.6 %collective-permute-start.31 = (bf16[2,128,512]{2,1,0:T(8,128)(2,1)S(1)}, bf16[2,128,512]{2,1,0:T(8,128)(2,1)S(1)}, u32[]{:S(2)}, u32[]{:S(2)}) collective-permute-start(bf16[2,128,512]{2,1,0:T(8,128)(2,1)S(1)} %get-tuple-element.38.high_ref), channel_id=1, source_target_pairs={{0,3},{1,0},{2,1},{3,2},{4,7},{5,4},{6,5},{7,6},{8,11},{9,8},{10,9... | collective-permute-start | bytes 786440 | tf_op jit(solution)/shard_map/ppermute | solution.py:41
  68.6 8.5 %collective-permute-start.30 = (bf16[2,128,512]{2,1,0:T(8,128)(2,1)S(1)}, bf16[2,128,512]{2,1,0:T(8,128)(2,1)S(1)}, u32[]{:S(2)}, u32[]{:S(2)}) collective-permute-start(bf16[2,128,512]{2,1,0:T(8,128)(2,1)S(1)} %get-tuple-element.37.low_ref), channel_id=1, source_target_pairs={{0,3},{1,0},{2,1},{3,2},{4,7},{5,4},{6,5},{7,6},{8,11},{9,8},{10,9... | collective-permute-start | bytes 786440 | tf_op jit(solution)/shard_map/ppermute | solution.py:41
  68.7 8.3 %collective-permute-start.29 = (bf16[2,128,512]{2,1,0:T(8,128)(2,1)S(1)}, bf16[2,128,512]{2,1,0:T(8,128)(2,1)S(1)}, u32[]{:S(2)}, u32[]{:S(2)}) collective-permute-start(bf16[2,128,512]{2,1,0:T(8,128)(2,1)S(1)} %get-tuple-element.38.high_ref), channel_id=1, source_target_pairs={{0,1},{1,2},{2,3},{3,0},{4,5},{5,6},{6,7},{7,4},{8,9},{9,10},{10,1... | collective-permute-start | bytes 786440 | tf_op jit(solution)/shard_map/ppermute | solution.py:41
  74.2 7.6 %collective-permute-start.33 = (bf16[2,128,512]{2,1,0:T(8,128)(2,1)S(1)}, bf16[2,128,512]{2,1,0:T(8,128)(2,1)S(1)}, u32[]{:S(2)}, u32[]{:S(2)}) collective-permute-start(bf16[2,128,512]{2,1,0:T(8,128)(2,1)S(1)} %collective-permute-done.31.rh_ref), channel_id=1, source_target_pairs={{0,3},{1,0},{2,1},{3,2},{4,7},{5,4},{6,5},{7,6},{8,11},{9,8},{10,9... | collective-permute-start | bytes 786440 | tf_op jit(solution)/shard_map/ppermute | solution.py:41
  82.1 7.8 %collective-permute-start.34 = (bf16[2,128,512]{2,1,0:T(8,128)(2,1)S(1)}, bf16[2,128,512]{2,1,0:T(8,128)(2,1)S(1)}, u32[]{:S(2)}, u32[]{:S(2)}) collective-permute-start(bf16[2,128,512]{2,1,0:T(8,128)(2,1)S(1)} %get-tuple-element.39.refs_5_), channel_id=1, source_target_pairs={{0,4},{1,5},{2,6},{3,7},{4,8},{5,9},{6,10},{7,11},{8,12},{9,13},{1... | collective-permute-start | bytes 786440 | tf_op jit(solution)/shard_map/ppermute | solution.py:41
  85.6 7.6 %collective-permute-start.36 = (bf16[2,128,512]{2,1,0:T(8,128)(2,1)S(1)}, bf16[2,128,512]{2,1,0:T(8,128)(2,1)S(1)}, u32[]{:S(2)}, u32[]{:S(2)}) collective-permute-start(bf16[2,128,512]{2,1,0:T(8,128)(2,1)S(1)} %get-tuple-element.39.refs_5_), channel_id=1, source_target_pairs={{0,12},{1,13},{2,14},{3,15},{4,0},{5,1},{6,2},{7,3},{8,4},{9,5},{1... | collective-permute-start | bytes 786440 | tf_op jit(solution)/shard_map/ppermute | solution.py:41
  87.6 7.6 %collective-permute-start.35 = (bf16[2,128,512]{2,1,0:T(8,128)(2,1)S(1)}, bf16[2,128,512]{2,1,0:T(8,128)(2,1)S(1)}, u32[]{:S(2)}, u32[]{:S(2)}) collective-permute-start(bf16[2,128,512]{2,1,0:T(8,128)(2,1)S(1)} %get-tuple-element.40.refs_6_), channel_id=1, source_target_pairs={{0,4},{1,5},{2,6},{3,7},{4,8},{5,9},{6,10},{7,11},{8,12},{9,13},{1... | collective-permute-start | bytes 786440 | tf_op jit(solution)/shard_map/ppermute | solution.py:41
  89.9 8.1 %collective-permute-start.38 = (bf16[2,128,512]{2,1,0:T(8,128)(2,1)S(1)}, bf16[2,128,512]{2,1,0:T(8,128)(2,1)S(1)}, u32[]{:S(2)}, u32[]{:S(2)}) collective-permute-start(bf16[2,128,512]{2,1,0:T(8,128)(2,1)S(1)} %collective-permute-done.34.refs_7_), channel_id=1, source_target_pairs={{0,4},{1,5},{2,6},{3,7},{4,8},{5,9},{6,10},{7,11},{8,12},{9,13},{1... | collective-permute-start | bytes 786440 | tf_op jit(solution)/shard_map/ppermute | solution.py:41
  89.9 8.1 %collective-permute-start.39 = (bf16[2,128,512]{2,1,0:T(8,128)(2,1)S(1)}, bf16[2,128,512]{2,1,0:T(8,128)(2,1)S(1)}, u32[]{:S(2)}, u32[]{:S(2)}) collective-permute-start(bf16[2,128,512]{2,1,0:T(8,128)(2,1)S(1)} %collective-permute-done.37.refs_10_), channel_id=1, source_target_pairs={{0,12},{1,13},{2,14},{3,15},{4,0},{5,1},{6,2},{7,3},{8,4},{9,5},{1... | collective-permute-start | bytes 786440 | tf_op jit(solution)/shard_map/ppermute | solution.py:41
  (24 other events, 142.5 us)

commit v6 on v5

--- a/solution.py
+++ b/solution.py
@@ -86,19 +86,24 @@
     return jnp.broadcast_to(ref[...].astype(F32), (HD, HD)).T
 
 
+def cache_rows(info, order_ref, cache_ref, out_ref, sems):
+    base = info[0] * HALF
+    copies = []
+    for i in range(HALF // BLOCK):
+        start = pl.multiple_of(base + i * BLOCK, BLOCK)
+        copies.append(
+            pltpu.make_async_copy(cache_ref.at[pl.ds(start, BLOCK)], out_ref.at[i], sems.at[i])
+        )
+        copies[-1].start()
+    for copy in copies:
+        copy.wait()
+
+
 def cache_kernel(
-    info, q_ref, other_ref, cache_ref, len_ref, owner_ref, slot_ref, out_ref, q_buf, open_buf, buf,
-    sems,
+    info, q_ref, other_ref, buf, len_ref, owner_ref, slot_ref, out_ref, q_buf, open_buf
 ):
     base = info[0] * HALF
     steps = HALF // BLOCK
-
-    def fetch(i):
-        start = pl.multiple_of(base + i * BLOCK, BLOCK)
-        return pltpu.make_async_copy(cache_ref.at[pl.ds(start, BLOCK)], buf.at[i], sems.at[i])
-
-    for i in range(steps):
-        fetch(i).start()
 
     @pl.when(info[0] == 0)
     def _():
@@ -125,7 +130,6 @@
     lane = lax.broadcasted_iota(jnp.int32, (2 * BLOCK, HD), 1)
 
     def step(i, carry):
-        fetch(i).wait()
         rows = pl.ds(pl.multiple_of(i * BLOCK, BLOCK), BLOCK)
         q = q_buf[rows, :]
         q = jnp.concatenate([q[:, :HD], q[:, HD:]], axis=0)
@@ -235,7 +239,7 @@
 def finish_kernel(
     info, q_ref, span_ref, new_ref, z1_ref, z2_ref, z3_ref, z4_ref, r1_ref, r2_ref, r3_ref, r4_ref,
     len_ref, owner_ref, slot_ref, mine_ref, theirs_ref, w_ref,
-    s0_ref, s1l_ref, s1h_ref, s2l_ref, s2h_ref, s3l_ref, s3h_ref, att_ref,
+    att_ref, s2l_ref, s2h_ref,
 ):
     row = lax.broadcasted_iota(jnp.int32, (ROWS, HD), 0)
     col = lax.broadcasted_iota(jnp.int32, (ROWS, HD), 1)
@@ -295,17 +299,22 @@
                 return top, total * old + new, summed * old + rounded * value_new
 
             att_ref[:, lanes] = attend(q, keys, values, allowed, start)
-
-    att = att_ref[...]
-    sets = {1: (s1l_ref, s1h_ref), 2: (s2l_ref, s2h_ref), 3: (s3l_ref, s3h_ref)}
-    for k in (2, 1, 3, 0):
+    for n, ref in enumerate((s2l_ref, s2h_ref)):
+        for m in range(2):
+            ref[m] = product(info, att_ref, w_ref, 2, 2 * n + m).astype(BF16)
+
+
+def product(info, att_ref, w_ref, k, j):
+    start = pl.multiple_of(chunk(info, info[1] + k, j) * WIDE, WIDE)
+    return jnp.dot(att_ref[...], w_ref[:, pl.ds(start, WIDE)], preferred_element_type=F32)
+
+
+def output_kernel(info, att_ref, w_ref, s0_ref, s1l_ref, s1h_ref, s3l_ref, s3h_ref):
+    for k, refs in ((1, (s1l_ref, s1h_ref)), (3, (s3l_ref, s3h_ref))):
         for j in range(SIDE):
-            start = pl.multiple_of(chunk(info, info[1] + k, j) * WIDE, WIDE)
-            part = jnp.dot(att, w_ref[:, pl.ds(start, WIDE)], preferred_element_type=F32)
-            if k == 0:
-                s0_ref[j] = part
-            else:
-                sets[k][j // 2][j % 2] = part.astype(BF16)
+            refs[j // 2][j % 2] = product(info, att_ref, w_ref, k, j).astype(BF16)
+    for j in range(SIDE):
+        s0_ref[j] = product(info, att_ref, w_ref, 0, j)
 
 
 def add_kernel(own_ref, got_ref, out_ref):
@@ -420,6 +429,11 @@
     pair = routed(kv, both, lambda g, c, t: (g, c, t ^ 1))
     swapped = swap(kv)
     cross = routed(kv, both, lambda g, c, t: (1 - g, c, t ^ 1))
+    cached = call(
+        cache_rows, st((HALF // BLOCK, BLOCK, HD, 2 * HD), BF16), [SMEM, VMEM, HBM], VMEM, 1000,
+        info, queries, cache, scratch=[dma((HALF // BLOCK,))], limit=49 << 20,
+    )
+    pair, cached = lax.optimization_barrier((pair, cached))
     span, new, part = call(
         pack_kernel, [st((2, ROWS, HD), BF16)] * 2 + [st((ROWS, HD), BF16)],
         [SMEM] + [VMEM] * 4, [VMEM] * 3, 1000, info, kv, pair, swapped, cross,
@@ -433,27 +447,23 @@
     zs = [along_z(x, k) for k, x in ((1, span), (2, span), (3, span), (4, part))]
     tied, zs[3] = lax.optimization_barrier((queries, zs[3]))
     old = call(
-        cache_kernel, st((2, 2, HALF, HD), F32), [SMEM, VMEM, VMEM, HBM, VMEM, VMEM, VMEM], VMEM,
-        1000, info, tied, other_queries, cache, lens, owners, slots,
-        scratch=[
-            pltpu.VMEM((HALF, 2 * HD), BF16),
-            pltpu.VMEM((ROWS, HD), F32),
-            pltpu.VMEM((HALF // BLOCK, BLOCK, HD, 2 * HD), BF16),
-            dma((HALF // BLOCK,)),
-        ],
-        limit=51 << 20,
+        cache_kernel, st((2, 2, HALF, HD), F32), [SMEM] + [VMEM] * 6, VMEM, 1000,
+        info, tied, other_queries, cached, lens, owners, slots,
+        scratch=[pltpu.VMEM((HALF, 2 * HD), BF16), pltpu.VMEM((ROWS, HD), F32)],
     )
     other_old = swap(old)
 
     rs = [swap(z) for z in zs]
     small = st((2, ROWS, WIDE), BF16)
-    sets = call(
-        finish_kernel, [st((SIDE, ROWS, WIDE), F32)] + [small] * 6,
-        [SMEM] + [VMEM] * 17, [VMEM] * 7, 800_000_000,
+    att, s2l, s2h = call(
+        finish_kernel, [st((ROWS, 2 * HD), BF16), small, small],
+        [SMEM] + [VMEM] * 17, [VMEM] * 3, 300_000_000,
         info, queries, span, new, *zs, *rs, lens, owners, slots, old, other_old, out_weight,
-        scratch=[pltpu.VMEM((ROWS, 2 * HD), BF16)],
-    )
-    s0, s1l, s1h, s2l, s2h, s3l, s3h = sets
+    )
+    s0, s1l, s1h, s3l, s3h = call(
+        output_kernel, [st((SIDE, ROWS, WIDE), F32)] + [small] * 4,
+        [SMEM, VMEM, VMEM], [VMEM] * 5, 400_000_000, info, att, out_weight,
+    )
     to_right = shift(s2l, 1, 0)
     to_left = shift(s2h, -1, 0)
     lh = shift(s1h, 1, 0)

time: 99.1 us -> 99 us (level)
  waiting for transfers between devices: 32.1 us -> 29.6 us
  starting transfers between devices: 52.9 us -> 54.1 us
    ppermute x13, waiting for transfers between devices: 6.88 us -> 4.58 us  [routed(): return lax.ppermute(block, ('group', 'ctx', 'tp'), route)]
    pallas_call x13 -> x15, Pallas kernels: 9.67 us -> 10.5 us  [call(): pl.pallas_call(kernel, out_shape=outs, in_specs=in_specs, out_specs=out_s...]
  transfers between devices with their start and end apart: 40 -> 40, of which waited for: 18 -> 18; matrix products, arithmetic and copies ran while one was open for 0% -> 0% of each run, Pallas kernels for 6% -> 7%
where the time goes in v6:
time: 99 us; the launch traced here: 98.8 us
  starting transfers between devices  54.1 us (55%)
  waiting for transfers between devices  29.6 us (30%)
  Pallas kernels  10.5 us (11%)
  local copies, waits for them, and re-layouts  4.11 us (4%)
    ppermute x27, starting transfers between devices, shift(): return lax.ppermute(block, ('group', 'tp'), tp_route(step_a, step_b))  39.5 us
    ppermute x27, waiting for transfers between devices, shift(): return lax.ppermute(block, ('group', 'tp'), tp_route(step_a, step_b))  25.1 us
    ppermute x13, starting transfers between devices, routed(): return lax.ppermute(block, ('group', 'ctx', 'tp'), route)  14.6 us
    pallas_call x15, Pallas kernels, call(): pl.pallas_call(kernel, out_shape=outs, in_specs=in_specs, out_specs=out_s...  10.5 us
    ppermute x13, waiting for transfers between devices, routed(): return lax.ppermute(block, ('group', 'ctx', 'tp'), route)  4.58 us
    unnamed x16, local copies, waits for them, and re-layouts  4.11 us
  transfers between devices with their start and end apart: 40, of which 18 were waited for; matrix products, arithmetic and copies ran while one was open for 0% of the time, Pallas kernels for 7%

profile of v6, /device:TPU:6, one launch (start us, length us, event | category | flops | bytes accessed | tf_op | source)
XLA Modules:
  0.0 98.8 jit_solution(6781882791639724455)
XLA Ops:
  0.0 2.2 %collective-permute-start = (bf16[128,512]{1,0:T(8,128)(2,1)}, bf16[128,512]{1,0:T(8,128)(2,1)S(1)}, u32[]{:S(2)}, u32[]{:S(2)}) collective-permute-start(bf16[128,512]{1,0:T(8,128)(2,1)} %bitcast.12), channel_id=1, source_target_pairs={{0,1},{1,2},{2,3},{3,0},{4,5},{5,6},{6,7},{7,4},{8,9},{9,10},{10,1... | collective-permute-start | bytes 393224 | tf_op jit(solution)/shard_map/ppermute | solution.py:41
  7.8 2.2 %collective-permute-done.2 = bf16[128,512]{1,0:T(8,128)(2,1)S(1)} collective-permute-done((bf16[128,512]{1,0:T(8,128)(2,1)}, bf16[128,512]{1,0:T(8,128)(2,1)S(1)}, u32[]{:S(2)}, u32[]{:S(2)}) %collective-permute-start.2) | collective-permute-done | bytes 131104 | tf_op jit(solution)/shard_map/ppermute | solution.py:41
  10.0 1.8 %collective-permute-start.6 = (bf16[2,128,512]{2,1,0:T(8,128)(2,1)S(1)}, bf16[2,128,512]{2,1,0:T(8,128)(2,1)S(1)}, u32[]{:S(2)}, u32[]{:S(2)}) collective-permute-start(bf16[2,128,512]{2,1,0:T(8,128)(2,1)S(1)} %pad_maximum_fusion.refs_6_), channel_id=1, source_target_pairs={{0,12},{1,13},{2,14},{3,15},{4,0},{5,1},{6,2},{7,3},{8,4},{9,5},{1... | collective-permute-start | bytes 786440 | tf_op jit(solution)/shard_map/ppermute | solution.py:41
  14.2 2.3 %collective-permute-done.6.refs_9_ = bf16[2,128,512]{2,1,0:T(8,128)(2,1)S(1)} collective-permute-done((bf16[2,128,512]{2,1,0:T(8,128)(2,1)S(1)}, bf16[2,128,512]{2,1,0:T(8,128)(2,1)S(1)}, u32[]{:S(2)}, u32[]{:S(2)}) %collective-permute-start.6) | collective-permute-done | bytes 262176 | tf_op jit(solution)/shard_map/ppermute | solution.py:41
  16.5 2.9 %collective-permute-start.8 = (bf16[2,128,512]{2,1,0:T(8,128)(2,1)S(1)}, bf16[2,128,512]{2,1,0:T(8,128)(2,1)S(1)}, u32[]{:S(2)}, u32[]{:S(2)}) collective-permute-start(bf16[2,128,512]{2,1,0:T(8,128)(2,1)S(1)} %collective-permute-done.6.refs_9_), channel_id=1, source_target_pairs={{0,12},{1,13},{2,14},{3,15},{4,0},{5,1},{6,2},{7,3},{8,4},{9,5},{1... | collective-permute-start | bytes 786440 | tf_op jit(solution)/shard_map/ppermute | solution.py:41
  23.7 2.0 %collective-permute-start.9 = (bf16[128,128]{1,0:T(8,128)(2,1)S(1)}, bf16[128,128]{1,0:T(8,128)(2,1)S(1)}, u32[]{:S(2)}, u32[]{:S(2)}) collective-permute-start(bf16[128,128]{1,0:T(8,128)(2,1)S(1)} %project_far.1.refs_5_), channel_id=1, source_target_pairs={{0,1},{1,0},{2,3},{3,2},{4,5},{5,4},{6,7},{7,6},{8,9},{9,8},{10,11... | collective-permute-start | bytes 98312 | tf_op jit(solution)/shard_map/ppermute | solution.py:51
  26.2 2.2 %cache_rows.1.refs_7_ = bf16[2,32,128,256]{3,2,1,0:T(8,128)(2,1)S(1)} custom-call(s32[1]{0:T(128)} %bitcast.refs_0_, s32[1]{0:T(128)} %bitcast.1.refs_1_, s32[1]{0:T(128)} %bitcast.2.refs_2_, s32[1]{0:T(128)} %bitcast.3.refs_3_, s32[1]{0:T(128)} %bitcast.4.refs_4_, bf16[1,128,256]{2,1,0:T(8,128)(2,1)S(1)} %copy-done.3, bf16[128,128,256]{2,1,0:T(8,128)(2,1)} %refs_6_.2), custom_call_target="tpu_custom_call" | custom-call | flops 1000 | bytes 8454164 | tf_op jit(solution)/shard_map/cache_rows/pallas_call | solution.py:379
  29.1 7.3 %collective-permute-start.15 = (bf16[128,128]{1,0:T(8,128)(2,1)S(1)}, bf16[128,128]{1,0:T(8,128)(2,1)S(1)}, u32[]{:S(2)}, u32[]{:S(2)}) collective-permute-start(bf16[128,128]{1,0:T(8,128)(2,1)S(1)} %get-tuple-element.31), channel_id=1, source_target_pairs={{0,64},{1,65},{2,66},{3,67},{4,68},{5,69},{6,70},{7,71},{8,72},{9,... | collective-permute-start | bytes 98312 | tf_op jit(solution)/shard_map/ppermute | solution.py:51
  36.4 1.9 %collective-permute-start.14 = (bf16[2,128,128]{2,1,0:T(8,128)(2,1)S(1)}, bf16[2,128,128]{2,1,0:T(8,128)(2,1)S(1)}, u32[]{:S(2)}, u32[]{:S(2)}) collective-permute-start(bf16[2,128,128]{2,1,0:T(8,128)(2,1)S(1)} %get-tuple-element.29.refs_6_), channel_id=1, source_target_pairs={{0,48},{1,49},{2,50},{3,51},{4,52},{5,53},{6,54},{7,55},{8,56},{9,... | collective-permute-start | bytes 196616 | tf_op jit(solution)/shard_map/ppermute | solution.py:51
  39.0 2.4 %cache_kernel.1.refs_19_ = f32[2,2,64,128]{3,2,1,0:T(8,128)S(1)} custom-call(s32[1]{0:T(128)} %bitcast.refs_0_, s32[1]{0:T(128)} %bitcast.1.refs_1_, s32[1]{0:T(128)} %bitcast.2.refs_2_, s32[1]{0:T(128)} %bitcast.3.refs_3_, s32[1]{0:T(128)} %bitcast.4.refs_4_, bf16[1,128,256]{2,1,0:T(8,128)(2,1)S(1)} %copy-done.3, ...), custom_call_target="tpu_custom_call" | custom-call | flops 1000 | bytes 4326932 | tf_op jit(solution)/shard_map/cache_kernel/pallas_call | solution.py:379
  41.4 1.7 %collective-permute-start.21 = (f32[2,2,64,128]{3,2,1,0:T(8,128)S(1)}, f32[2,2,64,128]{3,2,1,0:T(8,128)S(1)}, u32[]{:S(2)}, u32[]{:S(2)}) collective-permute-start(f32[2,2,64,128]{3,2,1,0:T(8,128)S(1)} %cache_kernel.1.refs_19_), channel_id=1, source_target_pairs={{0,128},{1,129},{2,130},{3,131},{4,132},{5,133},{6,134},{7,135},{8... | collective-permute-start | bytes 393224 | tf_op jit(solution)/shard_map/ppermute | solution.py:51
  49.4 3.7 %collective-permute-start.26 = (bf16[2,128,512]{2,1,0:T(8,128)(2,1)S(1)}, bf16[2,128,512]{2,1,0:T(8,128)(2,1)S(1)}, u32[]{:S(2)}, u32[]{:S(2)}) collective-permute-start(bf16[2,128,512]{2,1,0:T(8,128)(2,1)S(1)} %get-tuple-element.42), channel_id=1, source_target_pairs={{0,12},{1,13},{2,14},{3,15},{4,0},{5,1},{6,2},{7,3},{8,4},{9,5},{1... | collective-permute-start | bytes 786440 | tf_op jit(solution)/shard_map/ppermute | solution.py:41
  53.7 3.2 %collective-permute-start.25 = (bf16[2,128,512]{2,1,0:T(8,128)(2,1)S(1)}, bf16[2,128,512]{2,1,0:T(8,128)(2,1)S(1)}, u32[]{:S(2)}, u32[]{:S(2)}) collective-permute-start(bf16[2,128,512]{2,1,0:T(8,128)(2,1)S(1)} %get-tuple-element.40), channel_id=1, source_target_pairs={{0,12},{1,13},{2,14},{3,15},{4,0},{5,1},{6,2},{7,3},{8,4},{9,5},{1... | collective-permute-start | bytes 786440 | tf_op jit(solution)/shard_map/ppermute | solution.py:41
  57.5 3.3 %collective-permute-start.27 = (bf16[2,128,512]{2,1,0:T(8,128)(2,1)S(1)}, bf16[2,128,512]{2,1,0:T(8,128)(2,1)S(1)}, u32[]{:S(2)}, u32[]{:S(2)}) collective-permute-start(bf16[2,128,512]{2,1,0:T(8,128)(2,1)S(1)} %add_kernel.3), channel_id=1, source_target_pairs={{0,12},{1,13},{2,14},{3,15},{4,0},{5,1},{6,2},{7,3},{8,4},{9,5},{1... | collective-permute-start | bytes 786440 | tf_op jit(solution)/shard_map/ppermute | solution.py:41
  61.3 3.7 %collective-permute-done.23.ll_ref = bf16[2,128,512]{2,1,0:T(8,128)(2,1)S(1)} collective-permute-done((bf16[2,128,512]{2,1,0:T(8,128)(2,1)S(1)}, bf16[2,128,512]{2,1,0:T(8,128)(2,1)S(1)}, u32[]{:S(2)}, u32[]{:S(2)}) %collective-permute-start.23) | collective-permute-done | bytes 262176 | tf_op jit(solution)/shard_map/ppermute | solution.py:41
  68.6 2.1 %collective-permute-start.29 = (bf16[2,128,512]{2,1,0:T(8,128)(2,1)S(1)}, bf16[2,128,512]{2,1,0:T(8,128)(2,1)S(1)}, u32[]{:S(2)}, u32[]{:S(2)}) collective-permute-start(bf16[2,128,512]{2,1,0:T(8,128)(2,1)S(1)} %get-tuple-element.44.high_ref), channel_id=1, source_target_pairs={{0,1},{1,2},{2,3},{3,0},{4,5},{5,6},{6,7},{7,4},{8,9},{9,10},{10,1... | collective-permute-start | bytes 786440 | tf_op jit(solution)/shard_map/ppermute | solution.py:41
  71.9 2.2 %collective-permute-start.32 = (bf16[2,128,512]{2,1,0:T(8,128)(2,1)S(1)}, bf16[2,128,512]{2,1,0:T(8,128)(2,1)S(1)}, u32[]{:S(2)}, u32[]{:S(2)}) collective-permute-start(bf16[2,128,512]{2,1,0:T(8,128)(2,1)S(1)} %collective-permute-done.28.ll_ref), channel_id=1, source_target_pairs={{0,1},{1,2},{2,3},{3,0},{4,5},{5,6},{6,7},{7,4},{8,9},{9,10},{10,1... | collective-permute-start | bytes 786440 | tf_op jit(solution)/shard_map/ppermute | solution.py:41
  74.1 2.8 %collective-permute-done.30.rl_ref = bf16[2,128,512]{2,1,0:T(8,128)(2,1)S(1)} collective-permute-done((bf16[2,128,512]{2,1,0:T(8,128)(2,1)S(1)}, bf16[2,128,512]{2,1,0:T(8,128)(2,1)S(1)}, u32[]{:S(2)}, u32[]{:S(2)}) %collective-permute-start.30) | collective-permute-done | bytes 262176 | tf_op jit(solution)/shard_map/ppermute | solution.py:41
  78.3 3.4 %collective-permute-done.33.fh_ref = bf16[2,128,512]{2,1,0:T(8,128)(2,1)S(1)} collective-permute-done((bf16[2,128,512]{2,1,0:T(8,128)(2,1)S(1)}, bf16[2,128,512]{2,1,0:T(8,128)(2,1)S(1)}, u32[]{:S(2)}, u32[]{:S(2)}) %collective-permute-start.33) | collective-permute-done | bytes 262176 | tf_op jit(solution)/shard_map/ppermute | solution.py:41
  82.4 3.1 %collective-permute-start.37 = (bf16[2,128,512]{2,1,0:T(8,128)(2,1)S(1)}, bf16[2,128,512]{2,1,0:T(8,128)(2,1)S(1)}, u32[]{:S(2)}, u32[]{:S(2)}) collective-permute-start(bf16[2,128,512]{2,1,0:T(8,128)(2,1)S(1)} %get-tuple-element.46.refs_6_), channel_id=1, source_target_pairs={{0,12},{1,13},{2,14},{3,15},{4,0},{5,1},{6,2},{7,3},{8,4},{9,5},{1... | collective-permute-start | bytes 786440 | tf_op jit(solution)/shard_map/ppermute | solution.py:41
  85.5 1.9 %collective-permute-start.36 = (bf16[2,128,512]{2,1,0:T(8,128)(2,1)S(1)}, bf16[2,128,512]{2,1,0:T(8,128)(2,1)S(1)}, u32[]{:S(2)}, u32[]{:S(2)}) collective-permute-start(bf16[2,128,512]{2,1,0:T(8,128)(2,1)S(1)} %get-tuple-element.45.refs_5_), channel_id=1, source_target_pairs={{0,12},{1,13},{2,14},{3,15},{4,0},{5,1},{6,2},{7,3},{8,4},{9,5},{1... | collective-permute-start | bytes 786440 | tf_op jit(solution)/shard_map/ppermute | solution.py:41
  87.5 2.2 %collective-permute-done.34.refs_7_ = bf16[2,128,512]{2,1,0:T(8,128)(2,1)S(1)} collective-permute-done((bf16[2,128,512]{2,1,0:T(8,128)(2,1)S(1)}, bf16[2,128,512]{2,1,0:T(8,128)(2,1)S(1)}, u32[]{:S(2)}, u32[]{:S(2)}) %collective-permute-start.34) | collective-permute-done | bytes 262176 | tf_op jit(solution)/shard_map/ppermute | solution.py:41
  89.8 3.3 %collective-permute-start.39 = (bf16[2,128,512]{2,1,0:T(8,128)(2,1)S(1)}, bf16[2,128,512]{2,1,0:T(8,128)(2,1)S(1)}, u32[]{:S(2)}, u32[]{:S(2)}) collective-permute-start(bf16[2,128,512]{2,1,0:T(8,128)(2,1)S(1)} %collective-permute-done.37.refs_10_), channel_id=1, source_target_pairs={{0,12},{1,13},{2,14},{3,15},{4,0},{5,1},{6,2},{7,3},{8,4},{9,5},{1... | collective-permute-start | bytes 786440 | tf_op jit(solution)/shard_map/ppermute | solution.py:41
  93.1 1.9 %collective-permute-done.35.refs_8_ = bf16[2,128,512]{2,1,0:T(8,128)(2,1)S(1)} collective-permute-done((bf16[2,128,512]{2,1,0:T(8,128)(2,1)S(1)}, bf16[2,128,512]{2,1,0:T(8,128)(2,1)S(1)}, u32[]{:S(2)}, u32[]{:S(2)}) %collective-permute-start.35) | collective-permute-done | bytes 262176 | tf_op jit(solution)/shard_map/ppermute | solution.py:41
  (88 shorter events, 32.3 us)
Async XLA Ops:
  2.2 7.8 %collective-permute-start.2 = (bf16[128,512]{1,0:T(8,128)(2,1)}, bf16[128,512]{1,0:T(8,128)(2,1)S(1)}, u32[]{:S(2)}, u32[]{:S(2)}) collective-permute-start(bf16[128,512]{1,0:T(8,128)(2,1)} %bitcast.13), channel_id=1, source_target_pairs={{0,3},{1,0},{2,1},{3,2},{4,7},{5,4},{6,5},{7,6},{8,11},{9,8},{10,9... | collective-permute-start | bytes 393224 | tf_op jit(solution)/shard_map/ppermute | solution.py:41
  2.2 7.8 %collective-permute-start.1 = (bf16[128,512]{1,0:T(8,128)(2,1)}, bf16[128,512]{1,0:T(8,128)(2,1)S(1)}, u32[]{:S(2)}, u32[]{:S(2)}) collective-permute-start(bf16[128,512]{1,0:T(8,128)(2,1)} %bitcast.14), channel_id=1, source_target_pairs={{0,2},{1,3},{2,0},{3,1},{4,6},{5,7},{6,4},{7,5},{8,10},{9,11},{10,... | collective-permute-start | bytes 393224 | tf_op jit(solution)/shard_map/ppermute | solution.py:41
  6.1 7.8 %collective-permute-start.3 = (bf16[2,128,512]{2,1,0:T(8,128)(2,1)S(1)}, bf16[2,128,512]{2,1,0:T(8,128)(2,1)S(1)}, u32[]{:S(2)}, u32[]{:S(2)}) collective-permute-start(bf16[2,128,512]{2,1,0:T(8,128)(2,1)S(1)} %join_kernel.1.refs_5_), channel_id=1, source_target_pairs={{0,4},{1,5},{2,6},{3,7},{4,8},{5,9},{6,10},{7,11},{8,12},{9,13},{1... | collective-permute-start | bytes 786440 | tf_op jit(solution)/shard_map/ppermute | solution.py:41
  11.8 9.5 %collective-permute-start.5 = (bf16[2,128,512]{2,1,0:T(8,128)(2,1)S(1)}, bf16[2,128,512]{2,1,0:T(8,128)(2,1)S(1)}, u32[]{:S(2)}, u32[]{:S(2)}) collective-permute-start(bf16[2,128,512]{2,1,0:T(8,128)(2,1)S(1)} %join_kernel.1.refs_5_), channel_id=1, source_target_pairs={{0,12},{1,13},{2,14},{3,15},{4,0},{5,1},{6,2},{7,3},{8,4},{9,5},{1... | collective-permute-start | bytes 786440 | tf_op jit(solution)/shard_map/ppermute | solution.py:41
  12.6 8.7 %collective-permute-start.4 = (bf16[2,128,512]{2,1,0:T(8,128)(2,1)S(1)}, bf16[2,128,512]{2,1,0:T(8,128)(2,1)S(1)}, u32[]{:S(2)}, u32[]{:S(2)}) collective-permute-start(bf16[2,128,512]{2,1,0:T(8,128)(2,1)S(1)} %pad_maximum_fusion.refs_6_), channel_id=1, source_target_pairs={{0,4},{1,5},{2,6},{3,7},{4,8},{5,9},{6,10},{7,11},{8,12},{9,13},{1... | collective-permute-start | bytes 786440 | tf_op jit(solution)/shard_map/ppermute | solution.py:41
  13.9 9.5 %collective-permute-start.7 = (bf16[2,128,512]{2,1,0:T(8,128)(2,1)S(1)}, bf16[2,128,512]{2,1,0:T(8,128)(2,1)S(1)}, u32[]{:S(2)}, u32[]{:S(2)}) collective-permute-start(bf16[2,128,512]{2,1,0:T(8,128)(2,1)S(1)} %collective-permute-done.3.refs_6_), channel_id=1, source_target_pairs={{0,4},{1,5},{2,6},{3,7},{4,8},{5,9},{6,10},{7,11},{8,12},{9,13},{1... | collective-permute-start | bytes 786440 | tf_op jit(solution)/shard_map/ppermute | solution.py:41
  26.0 13.0 %collective-permute-start.20 = (bf16[1,128,256]{2,1,0:T(8,128)(2,1)S(1)}, bf16[1,128,256]{2,1,0:T(8,128)(2,1)S(1)}, u32[]{:S(2)}, u32[]{:S(2)}) collective-permute-start(bf16[1,128,256]{2,1,0:T(8,128)(2,1)S(1)} %copy-done.3), channel_id=1, source_target_pairs={{0,128},{1,129},{2,130},{3,131},{4,132},{5,133},{6,134},{7,135},{8... | collective-permute-start | bytes 196616 | tf_op jit(solution)/shard_map/ppermute | solution.py:51
  29.1 9.9 %collective-permute-start.15 = (bf16[128,128]{1,0:T(8,128)(2,1)S(1)}, bf16[128,128]{1,0:T(8,128)(2,1)S(1)}, u32[]{:S(2)}, u32[]{:S(2)}) collective-permute-start(bf16[128,128]{1,0:T(8,128)(2,1)S(1)} %get-tuple-element.31), channel_id=1, source_target_pairs={{0,64},{1,65},{2,66},{3,67},{4,68},{5,69},{6,70},{7,71},{8,72},{9,... | collective-permute-start | bytes 98312 | tf_op jit(solution)/shard_map/ppermute | solution.py:51
  38.3 8.0 %collective-permute-start.12 = (bf16[2,128,128]{2,1,0:T(8,128)(2,1)S(1)}, bf16[2,128,128]{2,1,0:T(8,128)(2,1)S(1)}, u32[]{:S(2)}, u32[]{:S(2)}) collective-permute-start(bf16[2,128,128]{2,1,0:T(8,128)(2,1)S(1)} %get-tuple-element.29.refs_6_), channel_id=1, source_target_pairs={{0,16},{1,17},{2,18},{3,19},{4,20},{5,21},{6,22},{7,23},{8,24},{9,... | collective-permute-start | bytes 196616 | tf_op jit(solution)/shard_map/ppermute | solution.py:51
  49.3 8.0 %collective-permute-start.22 = (bf16[2,128,512]{2,1,0:T(8,128)(2,1)S(1)}, bf16[2,128,512]{2,1,0:T(8,128)(2,1)S(1)}, u32[]{:S(2)}, u32[]{:S(2)}) collective-permute-start(bf16[2,128,512]{2,1,0:T(8,128)(2,1)S(1)} %get-tuple-element.38), channel_id=1, source_target_pairs={{0,4},{1,5},{2,6},{3,7},{4,8},{5,9},{6,10},{7,11},{8,12},{9,13},{1... | collective-permute-start | bytes 786440 | tf_op jit(solution)/shard_map/ppermute | solution.py:41
  49.4 8.1 %collective-permute-start.26 = (bf16[2,128,512]{2,1,0:T(8,128)(2,1)S(1)}, bf16[2,128,512]{2,1,0:T(8,128)(2,1)S(1)}, u32[]{:S(2)}, u32[]{:S(2)}) collective-permute-start(bf16[2,128,512]{2,1,0:T(8,128)(2,1)S(1)} %get-tuple-element.42), channel_id=1, source_target_pairs={{0,12},{1,13},{2,14},{3,15},{4,0},{5,1},{6,2},{7,3},{8,4},{9,5},{1... | collective-permute-start | bytes 786440 | tf_op jit(solution)/shard_map/ppermute | solution.py:41
  53.6 7.7 %collective-permute-start.24 = (bf16[2,128,512]{2,1,0:T(8,128)(2,1)S(1)}, bf16[2,128,512]{2,1,0:T(8,128)(2,1)S(1)}, u32[]{:S(2)}, u32[]{:S(2)}) collective-permute-start(bf16[2,128,512]{2,1,0:T(8,128)(2,1)S(1)} %get-tuple-element.39), channel_id=1, source_target_pairs={{0,4},{1,5},{2,6},{3,7},{4,8},{5,9},{6,10},{7,11},{8,12},{9,13},{1... | collective-permute-start | bytes 786440 | tf_op jit(solution)/shard_map/ppermute | solution.py:41
  53.7 7.6 %collective-permute-start.25 = (bf16[2,128,512]{2,1,0:T(8,128)(2,1)S(1)}, bf16[2,128,512]{2,1,0:T(8,128)(2,1)S(1)}, u32[]{:S(2)}, u32[]{:S(2)}) collective-permute-start(bf16[2,128,512]{2,1,0:T(8,128)(2,1)S(1)} %get-tuple-element.40), channel_id=1, source_target_pairs={{0,12},{1,13},{2,14},{3,15},{4,0},{5,1},{6,2},{7,3},{8,4},{9,5},{1... | collective-permute-start | bytes 786440 | tf_op jit(solution)/shard_map/ppermute | solution.py:41
  57.4 7.7 %collective-permute-start.23 = (bf16[2,128,512]{2,1,0:T(8,128)(2,1)S(1)}, bf16[2,128,512]{2,1,0:T(8,128)(2,1)S(1)}, u32[]{:S(2)}, u32[]{:S(2)}) collective-permute-start(bf16[2,128,512]{2,1,0:T(8,128)(2,1)S(1)} %add_kernel.2), channel_id=1, source_target_pairs={{0,4},{1,5},{2,6},{3,7},{4,8},{5,9},{6,10},{7,11},{8,12},{9,13},{1... | collective-permute-start | bytes 786440 | tf_op jit(solution)/shard_map/ppermute | solution.py:41
  57.5 7.5 %collective-permute-start.27 = (bf16[2,128,512]{2,1,0:T(8,128)(2,1)S(1)}, bf16[2,128,512]{2,1,0:T(8,128)(2,1)S(1)}, u32[]{:S(2)}, u32[]{:S(2)}) collective-permute-start(bf16[2,128,512]{2,1,0:T(8,128)(2,1)S(1)} %add_kernel.3), channel_id=1, source_target_pairs={{0,12},{1,13},{2,14},{3,15},{4,0},{5,1},{6,2},{7,3},{8,4},{9,5},{1... | collective-permute-start | bytes 786440 | tf_op jit(solution)/shard_map/ppermute | solution.py:41
  66.5 7.6 %collective-permute-start.31 = (bf16[2,128,512]{2,1,0:T(8,128)(2,1)S(1)}, bf16[2,128,512]{2,1,0:T(8,128)(2,1)S(1)}, u32[]{:S(2)}, u32[]{:S(2)}) collective-permute-start(bf16[2,128,512]{2,1,0:T(8,128)(2,1)S(1)} %get-tuple-element.44.high_ref), channel_id=1, source_target_pairs={{0,3},{1,0},{2,1},{3,2},{4,7},{5,4},{6,5},{7,6},{8,11},{9,8},{10,9... | collective-permute-start | bytes 786440 | tf_op jit(solution)/shard_map/ppermute | solution.py:41
  67.5 9.4 %collective-permute-start.30 = (bf16[2,128,512]{2,1,0:T(8,128)(2,1)S(1)}, bf16[2,128,512]{2,1,0:T(8,128)(2,1)S(1)}, u32[]{:S(2)}, u32[]{:S(2)}) collective-permute-start(bf16[2,128,512]{2,1,0:T(8,128)(2,1)S(1)} %get-tuple-element.43.low_ref), channel_id=1, source_target_pairs={{0,3},{1,0},{2,1},{3,2},{4,7},{5,4},{6,5},{7,6},{8,11},{9,8},{10,9... | collective-permute-start | bytes 786440 | tf_op jit(solution)/shard_map/ppermute | solution.py:41
  68.6 8.3 %collective-permute-start.29 = (bf16[2,128,512]{2,1,0:T(8,128)(2,1)S(1)}, bf16[2,128,512]{2,1,0:T(8,128)(2,1)S(1)}, u32[]{:S(2)}, u32[]{:S(2)}) collective-permute-start(bf16[2,128,512]{2,1,0:T(8,128)(2,1)S(1)} %get-tuple-element.44.high_ref), channel_id=1, source_target_pairs={{0,1},{1,2},{2,3},{3,0},{4,5},{5,6},{6,7},{7,4},{8,9},{9,10},{10,1... | collective-permute-start | bytes 786440 | tf_op jit(solution)/shard_map/ppermute | solution.py:41
  74.1 7.6 %collective-permute-start.33 = (bf16[2,128,512]{2,1,0:T(8,128)(2,1)S(1)}, bf16[2,128,512]{2,1,0:T(8,128)(2,1)S(1)}, u32[]{:S(2)}, u32[]{:S(2)}) collective-permute-start(bf16[2,128,512]{2,1,0:T(8,128)(2,1)S(1)} %collective-permute-done.31.rh_ref), channel_id=1, source_target_pairs={{0,3},{1,0},{2,1},{3,2},{4,7},{5,4},{6,5},{7,6},{8,11},{9,8},{10,9... | collective-permute-start | bytes 786440 | tf_op jit(solution)/shard_map/ppermute | solution.py:41
  81.9 7.8 %collective-permute-start.34 = (bf16[2,128,512]{2,1,0:T(8,128)(2,1)S(1)}, bf16[2,128,512]{2,1,0:T(8,128)(2,1)S(1)}, u32[]{:S(2)}, u32[]{:S(2)}) collective-permute-start(bf16[2,128,512]{2,1,0:T(8,128)(2,1)S(1)} %get-tuple-element.45.refs_5_), channel_id=1, source_target_pairs={{0,4},{1,5},{2,6},{3,7},{4,8},{5,9},{6,10},{7,11},{8,12},{9,13},{1... | collective-permute-start | bytes 786440 | tf_op jit(solution)/shard_map/ppermute | solution.py:41
  85.5 7.6 %collective-permute-start.36 = (bf16[2,128,512]{2,1,0:T(8,128)(2,1)S(1)}, bf16[2,128,512]{2,1,0:T(8,128)(2,1)S(1)}, u32[]{:S(2)}, u32[]{:S(2)}) collective-permute-start(bf16[2,128,512]{2,1,0:T(8,128)(2,1)S(1)} %get-tuple-element.45.refs_5_), channel_id=1, source_target_pairs={{0,12},{1,13},{2,14},{3,15},{4,0},{5,1},{6,2},{7,3},{8,4},{9,5},{1... | collective-permute-start | bytes 786440 | tf_op jit(solution)/shard_map/ppermute | solution.py:41
  87.4 7.6 %collective-permute-start.35 = (bf16[2,128,512]{2,1,0:T(8,128)(2,1)S(1)}, bf16[2,128,512]{2,1,0:T(8,128)(2,1)S(1)}, u32[]{:S(2)}, u32[]{:S(2)}) collective-permute-start(bf16[2,128,512]{2,1,0:T(8,128)(2,1)S(1)} %get-tuple-element.46.refs_6_), channel_id=1, source_target_pairs={{0,4},{1,5},{2,6},{3,7},{4,8},{5,9},{6,10},{7,11},{8,12},{9,13},{1... | collective-permute-start | bytes 786440 | tf_op jit(solution)/shard_map/ppermute | solution.py:41
  89.8 8.1 %collective-permute-start.38 = (bf16[2,128,512]{2,1,0:T(8,128)(2,1)S(1)}, bf16[2,128,512]{2,1,0:T(8,128)(2,1)S(1)}, u32[]{:S(2)}, u32[]{:S(2)}) collective-permute-start(bf16[2,128,512]{2,1,0:T(8,128)(2,1)S(1)} %collective-permute-done.34.refs_7_), channel_id=1, source_target_pairs={{0,4},{1,5},{2,6},{3,7},{4,8},{5,9},{6,10},{7,11},{8,12},{9,13},{1... | collective-permute-start | bytes 786440 | tf_op jit(solution)/shard_map/ppermute | solution.py:41
  89.8 8.1 %collective-permute-start.39 = (bf16[2,128,512]{2,1,0:T(8,128)(2,1)S(1)}, bf16[2,128,512]{2,1,0:T(8,128)(2,1)S(1)}, u32[]{:S(2)}, u32[]{:S(2)}) collective-permute-start(bf16[2,128,512]{2,1,0:T(8,128)(2,1)S(1)} %collective-permute-done.37.refs_10_), channel_id=1, source_target_pairs={{0,12},{1,13},{2,14},{3,15},{4,0},{5,1},{6,2},{7,3},{8,4},{9,5},{1... | collective-permute-start | bytes 786440 | tf_op jit(solution)/shard_map/ppermute | solution.py:41
  (24 other events, 154.0 us)

commit v7 on v6

--- a/solution.py
+++ b/solution.py
@@ -227,7 +227,7 @@
         top = jnp.maximum(top, s)
     top = jnp.max(top, axis=1, keepdims=True)
     top, total, summed = start(top)
-    sums = jnp.zeros((ROWS, HD), F32)
+    sums = jnp.zeros((2 * ROWS, HD), F32)
     for s, m, v in zip(scores, allowed, values):
         w = jnp.where(m, jnp.exp(s - top), 0.0)
         sums += w
@@ -241,8 +241,14 @@
     len_ref, owner_ref, slot_ref, mine_ref, theirs_ref, w_ref,
     att_ref, s2l_ref, s2h_ref,
 ):
-    row = lax.broadcasted_iota(jnp.int32, (ROWS, HD), 0)
-    col = lax.broadcasted_iota(jnp.int32, (ROWS, HD), 1)
+    row = lax.rem(lax.broadcasted_iota(jnp.int32, (2 * ROWS, HD), 0), ROWS)
+    col = lax.broadcasted_iota(jnp.int32, (2 * ROWS, HD), 1)
+    q = jnp.concatenate([q_ref[0, :, :HD], q_ref[0, :, HD:]], axis=0)
+
+    def put(out):
+        att_ref[:, :HD] = out[:ROWS]
+        att_ref[:, HD:] = out[ROWS:]
+
     ctx = info[3]
     near = [(z1_ref, r1_ref), (z2_ref, r2_ref), (z3_ref, r3_ref)]
 
@@ -254,12 +260,8 @@
         keys = [z4_ref if r is None else r.at[0] for r in refs]
         values = [r4_ref if r is None else r.at[1] for r in refs]
         allowed = [row - col >= (p - ctx) * ROWS for p in places]
-        zero = jnp.zeros((ROWS, HD), F32)
-        for h in range(2):
-            lanes = slice(h * HD, (h + 1) * HD)
-            att_ref[:, lanes] = attend(
-                q_ref[0, :, lanes], keys, values, allowed, lambda top: (top, 0.0, zero)
-            )
+        zero = jnp.zeros((2 * ROWS, HD), F32)
+        put(attend(q, keys, values, allowed, lambda top: (top, 0.0, zero)))
 
     @pl.when(info[0] == 1)
     def _():
@@ -271,8 +273,8 @@
         slot = slot_ref[...]
         request = jnp.where(owner_ref[...] == ctx, slot // PAGE, -1).astype(F32)
         page = lax.rem(slot, PAGE).astype(F32)
-        in_page = (lax.rem(row, 2 * PAGE) == col // PAGE).astype(BF16)
-        lens = lane_column(len_ref)
+        in_page = (lax.rem(row[:ROWS], 2 * PAGE) == col[:ROWS] // PAGE).astype(BF16)
+        lens = jnp.concatenate([lane_column(len_ref)] * 2, axis=0)
         pages = lax.broadcasted_iota(jnp.int32, (1, HD), 1) // (2 * PAGE)
         allowed = []
         for p in places:
@@ -281,24 +283,23 @@
             token = jnp.dot(picked, in_page, preferred_element_type=F32)
             position = token[1:2] * PAGE + lax.rem(col[:1], PAGE).astype(F32)
             allowed.append((token[:1] == row.astype(F32)) & (position < lens))
-        key_new = new_ref[0].astype(F32)
-        value_new = new_ref[1].astype(F32)
-        for h in range(2):
-            lanes = slice(h * HD, (h + 1) * HD)
-            q = q_ref[0, :, lanes]
-            fresh = jnp.sum(q.astype(F32) * key_new, axis=1, keepdims=True) * SCALE
-            summed = jnp.concatenate([theirs_ref[0, h], mine_ref[0, h]], axis=0)
-            stats = jnp.concatenate([theirs_ref[1, h], mine_ref[1, h]], axis=0)
-            highest, total = stats[:, :1], stats[:, HALF : HALF + 1]
-
-            def start(top):
-                top = jnp.maximum(jnp.maximum(top, fresh), highest)
-                old = jnp.exp(highest - top)
-                new = jnp.exp(fresh - top)
-                rounded = new.astype(BF16).astype(F32)
-                return top, total * old + new, summed * old + rounded * value_new
-
-            att_ref[:, lanes] = attend(q, keys, values, allowed, start)
+        key_new = jnp.concatenate([new_ref[0].astype(F32)] * 2, axis=0)
+        value_new = jnp.concatenate([new_ref[1].astype(F32)] * 2, axis=0)
+        fresh = jnp.sum(q.astype(F32) * key_new, axis=1, keepdims=True) * SCALE
+        pieces = [(ref, h) for h in range(2) for ref in (theirs_ref, mine_ref)]
+        summed = jnp.concatenate([ref[0, h] for ref, h in pieces], axis=0)
+        stats = jnp.concatenate([ref[1, h] for ref, h in pieces], axis=0)
+        highest, total = stats[:, :1], stats[:, HALF : HALF + 1]
+
+        def start(top):
+            top = jnp.maximum(jnp.maximum(top, fresh), highest)
+            old = jnp.exp(highest - top)
+            new = jnp.exp(fresh - top)
+            rounded = new.astype(BF16).astype(F32)
+            return top, total * old + new, summed * old + rounded * value_new
+
+        put(attend(q, keys, values, allowed, start))
+
     for n, ref in enumerate((s2l_ref, s2h_ref)):
         for m in range(2):
             ref[m] = product(info, att_ref, w_ref, 2, 2 * n + m).astype(BF16)

time: 99 us -> 98.8 us (level)
  no operation moved by 1% of the time
where the time goes in v7:
time: 98.8 us; the launch traced here: 98.7 us
  starting transfers between devices  54.1 us (55%)
  waiting for transfers between devices  29.6 us (30%)
  Pallas kernels  10.4 us (11%)
  local copies, waits for them, and re-layouts  4.11 us (4%)
    ppermute x27, starting transfers between devices, shift(): return lax.ppermute(block, ('group', 'tp'), tp_route(step_a, step_b))  39.5 us
    ppermute x27, waiting for transfers between devices, shift(): return lax.ppermute(block, ('group', 'tp'), tp_route(step_a, step_b))  25.1 us
    ppermute x13, starting transfers between devices, routed(): return lax.ppermute(block, ('group', 'ctx', 'tp'), route)  14.6 us
    pallas_call x15, Pallas kernels, call(): pl.pallas_call(kernel, out_shape=outs, in_specs=in_specs, out_specs=out_s...  10.4 us
    ppermute x13, waiting for transfers between devices, routed(): return lax.ppermute(block, ('group', 'ctx', 'tp'), route)  4.58 us
    unnamed x16, local copies, waits for them, and re-layouts  4.11 us
  transfers between devices with their start and end apart: 40, of which 18 were waited for; matrix products, arithmetic and copies ran while one was open for 0% of the time, Pallas kernels for 7%

profile of v7, /device:TPU:6, one launch (start us, length us, event | category | flops | bytes accessed | tf_op | source)
XLA Modules:
  0.0 98.7 jit_solution(2872039630437644031)
XLA Ops:
  0.0 2.2 %collective-permute-start = (bf16[128,512]{1,0:T(8,128)(2,1)}, bf16[128,512]{1,0:T(8,128)(2,1)S(1)}, u32[]{:S(2)}, u32[]{:S(2)}) collective-permute-start(bf16[128,512]{1,0:T(8,128)(2,1)} %bitcast.12), channel_id=1, source_target_pairs={{0,1},{1,2},{2,3},{3,0},{4,5},{5,6},{6,7},{7,4},{8,9},{9,10},{10,1... | collective-permute-start | bytes 393224 | tf_op jit(solution)/shard_map/ppermute | solution.py:41
  7.8 2.2 %collective-permute-done.2 = bf16[128,512]{1,0:T(8,128)(2,1)S(1)} collective-permute-done((bf16[128,512]{1,0:T(8,128)(2,1)}, bf16[128,512]{1,0:T(8,128)(2,1)S(1)}, u32[]{:S(2)}, u32[]{:S(2)}) %collective-permute-start.2) | collective-permute-done | bytes 131104 | tf_op jit(solution)/shard_map/ppermute | solution.py:41
  10.0 1.8 %collective-permute-start.6 = (bf16[2,128,512]{2,1,0:T(8,128)(2,1)S(1)}, bf16[2,128,512]{2,1,0:T(8,128)(2,1)S(1)}, u32[]{:S(2)}, u32[]{:S(2)}) collective-permute-start(bf16[2,128,512]{2,1,0:T(8,128)(2,1)S(1)} %pad_maximum_fusion.refs_6_), channel_id=1, source_target_pairs={{0,12},{1,13},{2,14},{3,15},{4,0},{5,1},{6,2},{7,3},{8,4},{9,5},{1... | collective-permute-start | bytes 786440 | tf_op jit(solution)/shard_map/ppermute | solution.py:41
  14.2 2.3 %collective-permute-done.6.refs_9_ = bf16[2,128,512]{2,1,0:T(8,128)(2,1)S(1)} collective-permute-done((bf16[2,128,512]{2,1,0:T(8,128)(2,1)S(1)}, bf16[2,128,512]{2,1,0:T(8,128)(2,1)S(1)}, u32[]{:S(2)}, u32[]{:S(2)}) %collective-permute-start.6) | collective-permute-done | bytes 262176 | tf_op jit(solution)/shard_map/ppermute | solution.py:41
  16.5 2.9 %collective-permute-start.8 = (bf16[2,128,512]{2,1,0:T(8,128)(2,1)S(1)}, bf16[2,128,512]{2,1,0:T(8,128)(2,1)S(1)}, u32[]{:S(2)}, u32[]{:S(2)}) collective-permute-start(bf16[2,128,512]{2,1,0:T(8,128)(2,1)S(1)} %collective-permute-done.6.refs_9_), channel_id=1, source_target_pairs={{0,12},{1,13},{2,14},{3,15},{4,0},{5,1},{6,2},{7,3},{8,4},{9,5},{1... | collective-permute-start | bytes 786440 | tf_op jit(solution)/shard_map/ppermute | solution.py:41
  23.7 2.0 %collective-permute-start.9 = (bf16[128,128]{1,0:T(8,128)(2,1)S(1)}, bf16[128,128]{1,0:T(8,128)(2,1)S(1)}, u32[]{:S(2)}, u32[]{:S(2)}) collective-permute-start(bf16[128,128]{1,0:T(8,128)(2,1)S(1)} %project_far.1.refs_5_), channel_id=1, source_target_pairs={{0,1},{1,0},{2,3},{3,2},{4,5},{5,4},{6,7},{7,6},{8,9},{9,8},{10,11... | collective-permute-start | bytes 98312 | tf_op jit(solution)/shard_map/ppermute | solution.py:51
  26.2 2.2 %cache_rows.1.refs_7_ = bf16[2,32,128,256]{3,2,1,0:T(8,128)(2,1)S(1)} custom-call(s32[1]{0:T(128)} %bitcast.refs_0_, s32[1]{0:T(128)} %bitcast.1.refs_1_, s32[1]{0:T(128)} %bitcast.2.refs_2_, s32[1]{0:T(128)} %bitcast.3.refs_3_, s32[1]{0:T(128)} %bitcast.4.refs_4_, bf16[1,128,256]{2,1,0:T(8,128)(2,1)S(1)} %copy-done.3, bf16[128,128,256]{2,1,0:T(8,128)(2,1)} %refs_6_.2), custom_call_target="tpu_custom_call" | custom-call | flops 1000 | bytes 8454164 | tf_op jit(solution)/shard_map/cache_rows/pallas_call | solution.py:380
  29.1 7.3 %collective-permute-start.15 = (bf16[128,128]{1,0:T(8,128)(2,1)S(1)}, bf16[128,128]{1,0:T(8,128)(2,1)S(1)}, u32[]{:S(2)}, u32[]{:S(2)}) collective-permute-start(bf16[128,128]{1,0:T(8,128)(2,1)S(1)} %get-tuple-element.31), channel_id=1, source_target_pairs={{0,64},{1,65},{2,66},{3,67},{4,68},{5,69},{6,70},{7,71},{8,72},{9,... | collective-permute-start | bytes 98312 | tf_op jit(solution)/shard_map/ppermute | solution.py:51
  36.4 1.9 %collective-permute-start.14 = (bf16[2,128,128]{2,1,0:T(8,128)(2,1)S(1)}, bf16[2,128,128]{2,1,0:T(8,128)(2,1)S(1)}, u32[]{:S(2)}, u32[]{:S(2)}) collective-permute-start(bf16[2,128,128]{2,1,0:T(8,128)(2,1)S(1)} %get-tuple-element.29.refs_6_), channel_id=1, source_target_pairs={{0,48},{1,49},{2,50},{3,51},{4,52},{5,53},{6,54},{7,55},{8,56},{9,... | collective-permute-start | bytes 196616 | tf_op jit(solution)/shard_map/ppermute | solution.py:51
  39.0 2.4 %cache_kernel.1.refs_19_ = f32[2,2,64,128]{3,2,1,0:T(8,128)S(1)} custom-call(s32[1]{0:T(128)} %bitcast.refs_0_, s32[1]{0:T(128)} %bitcast.1.refs_1_, s32[1]{0:T(128)} %bitcast.2.refs_2_, s32[1]{0:T(128)} %bitcast.3.refs_3_, s32[1]{0:T(128)} %bitcast.4.refs_4_, bf16[1,128,256]{2,1,0:T(8,128)(2,1)S(1)} %copy-done.3, ...), custom_call_target="tpu_custom_call" | custom-call | flops 1000 | bytes 4326932 | tf_op jit(solution)/shard_map/cache_kernel/pallas_call | solution.py:380
  41.4 1.7 %collective-permute-start.21 = (f32[2,2,64,128]{3,2,1,0:T(8,128)S(1)}, f32[2,2,64,128]{3,2,1,0:T(8,128)S(1)}, u32[]{:S(2)}, u32[]{:S(2)}) collective-permute-start(f32[2,2,64,128]{3,2,1,0:T(8,128)S(1)} %cache_kernel.1.refs_19_), channel_id=1, source_target_pairs={{0,128},{1,129},{2,130},{3,131},{4,132},{5,133},{6,134},{7,135},{8... | collective-permute-start | bytes 393224 | tf_op jit(solution)/shard_map/ppermute | solution.py:51
  49.2 3.7 %collective-permute-start.26 = (bf16[2,128,512]{2,1,0:T(8,128)(2,1)S(1)}, bf16[2,128,512]{2,1,0:T(8,128)(2,1)S(1)}, u32[]{:S(2)}, u32[]{:S(2)}) collective-permute-start(bf16[2,128,512]{2,1,0:T(8,128)(2,1)S(1)} %get-tuple-element.42), channel_id=1, source_target_pairs={{0,12},{1,13},{2,14},{3,15},{4,0},{5,1},{6,2},{7,3},{8,4},{9,5},{1... | collective-permute-start | bytes 786440 | tf_op jit(solution)/shard_map/ppermute | solution.py:41
  53.6 3.2 %collective-permute-start.25 = (bf16[2,128,512]{2,1,0:T(8,128)(2,1)S(1)}, bf16[2,128,512]{2,1,0:T(8,128)(2,1)S(1)}, u32[]{:S(2)}, u32[]{:S(2)}) collective-permute-start(bf16[2,128,512]{2,1,0:T(8,128)(2,1)S(1)} %get-tuple-element.40), channel_id=1, source_target_pairs={{0,12},{1,13},{2,14},{3,15},{4,0},{5,1},{6,2},{7,3},{8,4},{9,5},{1... | collective-permute-start | bytes 786440 | tf_op jit(solution)/shard_map/ppermute | solution.py:41
  57.4 3.3 %collective-permute-start.27 = (bf16[2,128,512]{2,1,0:T(8,128)(2,1)S(1)}, bf16[2,128,512]{2,1,0:T(8,128)(2,1)S(1)}, u32[]{:S(2)}, u32[]{:S(2)}) collective-permute-start(bf16[2,128,512]{2,1,0:T(8,128)(2,1)S(1)} %add_kernel.3), channel_id=1, source_target_pairs={{0,12},{1,13},{2,14},{3,15},{4,0},{5,1},{6,2},{7,3},{8,4},{9,5},{1... | collective-permute-start | bytes 786440 | tf_op jit(solution)/shard_map/ppermute | solution.py:41
  61.1 3.7 %collective-permute-done.23.ll_ref = bf16[2,128,512]{2,1,0:T(8,128)(2,1)S(1)} collective-permute-done((bf16[2,128,512]{2,1,0:T(8,128)(2,1)S(1)}, bf16[2,128,512]{2,1,0:T(8,128)(2,1)S(1)}, u32[]{:S(2)}, u32[]{:S(2)}) %collective-permute-start.23) | collective-permute-done | bytes 262176 | tf_op jit(solution)/shard_map/ppermute | solution.py:41
  68.5 2.1 %collective-permute-start.29 = (bf16[2,128,512]{2,1,0:T(8,128)(2,1)S(1)}, bf16[2,128,512]{2,1,0:T(8,128)(2,1)S(1)}, u32[]{:S(2)}, u32[]{:S(2)}) collective-permute-start(bf16[2,128,512]{2,1,0:T(8,128)(2,1)S(1)} %get-tuple-element.44.high_ref), channel_id=1, source_target_pairs={{0,1},{1,2},{2,3},{3,0},{4,5},{5,6},{6,7},{7,4},{8,9},{9,10},{10,1... | collective-permute-start | bytes 786440 | tf_op jit(solution)/shard_map/ppermute | solution.py:41
  71.7 2.2 %collective-permute-start.32 = (bf16[2,128,512]{2,1,0:T(8,128)(2,1)S(1)}, bf16[2,128,512]{2,1,0:T(8,128)(2,1)S(1)}, u32[]{:S(2)}, u32[]{:S(2)}) collective-permute-start(bf16[2,128,512]{2,1,0:T(8,128)(2,1)S(1)} %collective-permute-done.28.ll_ref), channel_id=1, source_target_pairs={{0,1},{1,2},{2,3},{3,0},{4,5},{5,6},{6,7},{7,4},{8,9},{9,10},{10,1... | collective-permute-start | bytes 786440 | tf_op jit(solution)/shard_map/ppermute | solution.py:41
  73.9 2.8 %collective-permute-done.30.rl_ref = bf16[2,128,512]{2,1,0:T(8,128)(2,1)S(1)} collective-permute-done((bf16[2,128,512]{2,1,0:T(8,128)(2,1)S(1)}, bf16[2,128,512]{2,1,0:T(8,128)(2,1)S(1)}, u32[]{:S(2)}, u32[]{:S(2)}) %collective-permute-start.30) | collective-permute-done | bytes 262176 | tf_op jit(solution)/shard_map/ppermute | solution.py:41
  78.1 3.4 %collective-permute-done.33.fh_ref = bf16[2,128,512]{2,1,0:T(8,128)(2,1)S(1)} collective-permute-done((bf16[2,128,512]{2,1,0:T(8,128)(2,1)S(1)}, bf16[2,128,512]{2,1,0:T(8,128)(2,1)S(1)}, u32[]{:S(2)}, u32[]{:S(2)}) %collective-permute-start.33) | collective-permute-done | bytes 262176 | tf_op jit(solution)/shard_map/ppermute | solution.py:41
  82.2 3.1 %collective-permute-start.37 = (bf16[2,128,512]{2,1,0:T(8,128)(2,1)S(1)}, bf16[2,128,512]{2,1,0:T(8,128)(2,1)S(1)}, u32[]{:S(2)}, u32[]{:S(2)}) collective-permute-start(bf16[2,128,512]{2,1,0:T(8,128)(2,1)S(1)} %get-tuple-element.46.refs_6_), channel_id=1, source_target_pairs={{0,12},{1,13},{2,14},{3,15},{4,0},{5,1},{6,2},{7,3},{8,4},{9,5},{1... | collective-permute-start | bytes 786440 | tf_op jit(solution)/shard_map/ppermute | solution.py:41
  85.3 1.9 %collective-permute-start.36 = (bf16[2,128,512]{2,1,0:T(8,128)(2,1)S(1)}, bf16[2,128,512]{2,1,0:T(8,128)(2,1)S(1)}, u32[]{:S(2)}, u32[]{:S(2)}) collective-permute-start(bf16[2,128,512]{2,1,0:T(8,128)(2,1)S(1)} %get-tuple-element.45.refs_5_), channel_id=1, source_target_pairs={{0,12},{1,13},{2,14},{3,15},{4,0},{5,1},{6,2},{7,3},{8,4},{9,5},{1... | collective-permute-start | bytes 786440 | tf_op jit(solution)/shard_map/ppermute | solution.py:41
  87.4 2.2 %collective-permute-done.34.refs_7_ = bf16[2,128,512]{2,1,0:T(8,128)(2,1)S(1)} collective-permute-done((bf16[2,128,512]{2,1,0:T(8,128)(2,1)S(1)}, bf16[2,128,512]{2,1,0:T(8,128)(2,1)S(1)}, u32[]{:S(2)}, u32[]{:S(2)}) %collective-permute-start.34) | collective-permute-done | bytes 262176 | tf_op jit(solution)/shard_map/ppermute | solution.py:41
  89.6 3.3 %collective-permute-start.39 = (bf16[2,128,512]{2,1,0:T(8,128)(2,1)S(1)}, bf16[2,128,512]{2,1,0:T(8,128)(2,1)S(1)}, u32[]{:S(2)}, u32[]{:S(2)}) collective-permute-start(bf16[2,128,512]{2,1,0:T(8,128)(2,1)S(1)} %collective-permute-done.37.refs_10_), channel_id=1, source_target_pairs={{0,12},{1,13},{2,14},{3,15},{4,0},{5,1},{6,2},{7,3},{8,4},{9,5},{1... | collective-permute-start | bytes 786440 | tf_op jit(solution)/shard_map/ppermute | solution.py:41
  92.9 1.9 %collective-permute-done.35.refs_8_ = bf16[2,128,512]{2,1,0:T(8,128)(2,1)S(1)} collective-permute-done((bf16[2,128,512]{2,1,0:T(8,128)(2,1)S(1)}, bf16[2,128,512]{2,1,0:T(8,128)(2,1)S(1)}, u32[]{:S(2)}, u32[]{:S(2)}) %collective-permute-start.35) | collective-permute-done | bytes 262176 | tf_op jit(solution)/shard_map/ppermute | solution.py:41
  (88 shorter events, 32.2 us)
Async XLA Ops:
  2.2 7.8 %collective-permute-start.2 = (bf16[128,512]{1,0:T(8,128)(2,1)}, bf16[128,512]{1,0:T(8,128)(2,1)S(1)}, u32[]{:S(2)}, u32[]{:S(2)}) collective-permute-start(bf16[128,512]{1,0:T(8,128)(2,1)} %bitcast.13), channel_id=1, source_target_pairs={{0,3},{1,0},{2,1},{3,2},{4,7},{5,4},{6,5},{7,6},{8,11},{9,8},{10,9... | collective-permute-start | bytes 393224 | tf_op jit(solution)/shard_map/ppermute | solution.py:41
  2.2 7.8 %collective-permute-start.1 = (bf16[128,512]{1,0:T(8,128)(2,1)}, bf16[128,512]{1,0:T(8,128)(2,1)S(1)}, u32[]{:S(2)}, u32[]{:S(2)}) collective-permute-start(bf16[128,512]{1,0:T(8,128)(2,1)} %bitcast.14), channel_id=1, source_target_pairs={{0,2},{1,3},{2,0},{3,1},{4,6},{5,7},{6,4},{7,5},{8,10},{9,11},{10,... | collective-permute-start | bytes 393224 | tf_op jit(solution)/shard_map/ppermute | solution.py:41
  6.1 7.8 %collective-permute-start.3 = (bf16[2,128,512]{2,1,0:T(8,128)(2,1)S(1)}, bf16[2,128,512]{2,1,0:T(8,128)(2,1)S(1)}, u32[]{:S(2)}, u32[]{:S(2)}) collective-permute-start(bf16[2,128,512]{2,1,0:T(8,128)(2,1)S(1)} %join_kernel.1.refs_5_), channel_id=1, source_target_pairs={{0,4},{1,5},{2,6},{3,7},{4,8},{5,9},{6,10},{7,11},{8,12},{9,13},{1... | collective-permute-start | bytes 786440 | tf_op jit(solution)/shard_map/ppermute | solution.py:41
  11.8 9.5 %collective-permute-start.5 = (bf16[2,128,512]{2,1,0:T(8,128)(2,1)S(1)}, bf16[2,128,512]{2,1,0:T(8,128)(2,1)S(1)}, u32[]{:S(2)}, u32[]{:S(2)}) collective-permute-start(bf16[2,128,512]{2,1,0:T(8,128)(2,1)S(1)} %join_kernel.1.refs_5_), channel_id=1, source_target_pairs={{0,12},{1,13},{2,14},{3,15},{4,0},{5,1},{6,2},{7,3},{8,4},{9,5},{1... | collective-permute-start | bytes 786440 | tf_op jit(solution)/shard_map/ppermute | solution.py:41
  12.6 8.7 %collective-permute-start.4 = (bf16[2,128,512]{2,1,0:T(8,128)(2,1)S(1)}, bf16[2,128,512]{2,1,0:T(8,128)(2,1)S(1)}, u32[]{:S(2)}, u32[]{:S(2)}) collective-permute-start(bf16[2,128,512]{2,1,0:T(8,128)(2,1)S(1)} %pad_maximum_fusion.refs_6_), channel_id=1, source_target_pairs={{0,4},{1,5},{2,6},{3,7},{4,8},{5,9},{6,10},{7,11},{8,12},{9,13},{1... | collective-permute-start | bytes 786440 | tf_op jit(solution)/shard_map/ppermute | solution.py:41
  13.9 9.5 %collective-permute-start.7 = (bf16[2,128,512]{2,1,0:T(8,128)(2,1)S(1)}, bf16[2,128,512]{2,1,0:T(8,128)(2,1)S(1)}, u32[]{:S(2)}, u32[]{:S(2)}) collective-permute-start(bf16[2,128,512]{2,1,0:T(8,128)(2,1)S(1)} %collective-permute-done.3.refs_6_), channel_id=1, source_target_pairs={{0,4},{1,5},{2,6},{3,7},{4,8},{5,9},{6,10},{7,11},{8,12},{9,13},{1... | collective-permute-start | bytes 786440 | tf_op jit(solution)/shard_map/ppermute | solution.py:41
  26.0 13.0 %collective-permute-start.20 = (bf16[1,128,256]{2,1,0:T(8,128)(2,1)S(1)}, bf16[1,128,256]{2,1,0:T(8,128)(2,1)S(1)}, u32[]{:S(2)}, u32[]{:S(2)}) collective-permute-start(bf16[1,128,256]{2,1,0:T(8,128)(2,1)S(1)} %copy-done.3), channel_id=1, source_target_pairs={{0,128},{1,129},{2,130},{3,131},{4,132},{5,133},{6,134},{7,135},{8... | collective-permute-start | bytes 196616 | tf_op jit(solution)/shard_map/ppermute | solution.py:51
  29.1 9.9 %collective-permute-start.15 = (bf16[128,128]{1,0:T(8,128)(2,1)S(1)}, bf16[128,128]{1,0:T(8,128)(2,1)S(1)}, u32[]{:S(2)}, u32[]{:S(2)}) collective-permute-start(bf16[128,128]{1,0:T(8,128)(2,1)S(1)} %get-tuple-element.31), channel_id=1, source_target_pairs={{0,64},{1,65},{2,66},{3,67},{4,68},{5,69},{6,70},{7,71},{8,72},{9,... | collective-permute-start | bytes 98312 | tf_op jit(solution)/shard_map/ppermute | solution.py:51
  38.3 8.0 %collective-permute-start.12 = (bf16[2,128,128]{2,1,0:T(8,128)(2,1)S(1)}, bf16[2,128,128]{2,1,0:T(8,128)(2,1)S(1)}, u32[]{:S(2)}, u32[]{:S(2)}) collective-permute-start(bf16[2,128,128]{2,1,0:T(8,128)(2,1)S(1)} %get-tuple-element.29.refs_6_), channel_id=1, source_target_pairs={{0,16},{1,17},{2,18},{3,19},{4,20},{5,21},{6,22},{7,23},{8,24},{9,... | collective-permute-start | bytes 196616 | tf_op jit(solution)/shard_map/ppermute | solution.py:51
  49.1 8.0 %collective-permute-start.22 = (bf16[2,128,512]{2,1,0:T(8,128)(2,1)S(1)}, bf16[2,128,512]{2,1,0:T(8,128)(2,1)S(1)}, u32[]{:S(2)}, u32[]{:S(2)}) collective-permute-start(bf16[2,128,512]{2,1,0:T(8,128)(2,1)S(1)} %get-tuple-element.38), channel_id=1, source_target_pairs={{0,4},{1,5},{2,6},{3,7},{4,8},{5,9},{6,10},{7,11},{8,12},{9,13},{1... | collective-permute-start | bytes 786440 | tf_op jit(solution)/shard_map/ppermute | solution.py:41
  49.2 8.1 %collective-permute-start.26 = (bf16[2,128,512]{2,1,0:T(8,128)(2,1)S(1)}, bf16[2,128,512]{2,1,0:T(8,128)(2,1)S(1)}, u32[]{:S(2)}, u32[]{:S(2)}) collective-permute-start(bf16[2,128,512]{2,1,0:T(8,128)(2,1)S(1)} %get-tuple-element.42), channel_id=1, source_target_pairs={{0,12},{1,13},{2,14},{3,15},{4,0},{5,1},{6,2},{7,3},{8,4},{9,5},{1... | collective-permute-start | bytes 786440 | tf_op jit(solution)/shard_map/ppermute | solution.py:41
  53.5 7.7 %collective-permute-start.24 = (bf16[2,128,512]{2,1,0:T(8,128)(2,1)S(1)}, bf16[2,128,512]{2,1,0:T(8,128)(2,1)S(1)}, u32[]{:S(2)}, u32[]{:S(2)}) collective-permute-start(bf16[2,128,512]{2,1,0:T(8,128)(2,1)S(1)} %get-tuple-element.39), channel_id=1, source_target_pairs={{0,4},{1,5},{2,6},{3,7},{4,8},{5,9},{6,10},{7,11},{8,12},{9,13},{1... | collective-permute-start | bytes 786440 | tf_op jit(solution)/shard_map/ppermute | solution.py:41
  53.6 7.6 %collective-permute-start.25 = (bf16[2,128,512]{2,1,0:T(8,128)(2,1)S(1)}, bf16[2,128,512]{2,1,0:T(8,128)(2,1)S(1)}, u32[]{:S(2)}, u32[]{:S(2)}) collective-permute-start(bf16[2,128,512]{2,1,0:T(8,128)(2,1)S(1)} %get-tuple-element.40), channel_id=1, source_target_pairs={{0,12},{1,13},{2,14},{3,15},{4,0},{5,1},{6,2},{7,3},{8,4},{9,5},{1... | collective-permute-start | bytes 786440 | tf_op jit(solution)/shard_map/ppermute | solution.py:41
  57.2 7.7 %collective-permute-start.23 = (bf16[2,128,512]{2,1,0:T(8,128)(2,1)S(1)}, bf16[2,128,512]{2,1,0:T(8,128)(2,1)S(1)}, u32[]{:S(2)}, u32[]{:S(2)}) collective-permute-start(bf16[2,128,512]{2,1,0:T(8,128)(2,1)S(1)} %add_kernel.2), channel_id=1, source_target_pairs={{0,4},{1,5},{2,6},{3,7},{4,8},{5,9},{6,10},{7,11},{8,12},{9,13},{1... | collective-permute-start | bytes 786440 | tf_op jit(solution)/shard_map/ppermute | solution.py:41
  57.4 7.5 %collective-permute-start.27 = (bf16[2,128,512]{2,1,0:T(8,128)(2,1)S(1)}, bf16[2,128,512]{2,1,0:T(8,128)(2,1)S(1)}, u32[]{:S(2)}, u32[]{:S(2)}) collective-permute-start(bf16[2,128,512]{2,1,0:T(8,128)(2,1)S(1)} %add_kernel.3), channel_id=1, source_target_pairs={{0,12},{1,13},{2,14},{3,15},{4,0},{5,1},{6,2},{7,3},{8,4},{9,5},{1... | collective-permute-start | bytes 786440 | tf_op jit(solution)/shard_map/ppermute | solution.py:41
  66.3 7.6 %collective-permute-start.31 = (bf16[2,128,512]{2,1,0:T(8,128)(2,1)S(1)}, bf16[2,128,512]{2,1,0:T(8,128)(2,1)S(1)}, u32[]{:S(2)}, u32[]{:S(2)}) collective-permute-start(bf16[2,128,512]{2,1,0:T(8,128)(2,1)S(1)} %get-tuple-element.44.high_ref), channel_id=1, source_target_pairs={{0,3},{1,0},{2,1},{3,2},{4,7},{5,4},{6,5},{7,6},{8,11},{9,8},{10,9... | collective-permute-start | bytes 786440 | tf_op jit(solution)/shard_map/ppermute | solution.py:41
  67.4 9.4 %collective-permute-start.30 = (bf16[2,128,512]{2,1,0:T(8,128)(2,1)S(1)}, bf16[2,128,512]{2,1,0:T(8,128)(2,1)S(1)}, u32[]{:S(2)}, u32[]{:S(2)}) collective-permute-start(bf16[2,128,512]{2,1,0:T(8,128)(2,1)S(1)} %get-tuple-element.43.low_ref), channel_id=1, source_target_pairs={{0,3},{1,0},{2,1},{3,2},{4,7},{5,4},{6,5},{7,6},{8,11},{9,8},{10,9... | collective-permute-start | bytes 786440 | tf_op jit(solution)/shard_map/ppermute | solution.py:41
  68.5 8.3 %collective-permute-start.29 = (bf16[2,128,512]{2,1,0:T(8,128)(2,1)S(1)}, bf16[2,128,512]{2,1,0:T(8,128)(2,1)S(1)}, u32[]{:S(2)}, u32[]{:S(2)}) collective-permute-start(bf16[2,128,512]{2,1,0:T(8,128)(2,1)S(1)} %get-tuple-element.44.high_ref), channel_id=1, source_target_pairs={{0,1},{1,2},{2,3},{3,0},{4,5},{5,6},{6,7},{7,4},{8,9},{9,10},{10,1... | collective-permute-start | bytes 786440 | tf_op jit(solution)/shard_map/ppermute | solution.py:41
  73.9 7.6 %collective-permute-start.33 = (bf16[2,128,512]{2,1,0:T(8,128)(2,1)S(1)}, bf16[2,128,512]{2,1,0:T(8,128)(2,1)S(1)}, u32[]{:S(2)}, u32[]{:S(2)}) collective-permute-start(bf16[2,128,512]{2,1,0:T(8,128)(2,1)S(1)} %collective-permute-done.31.rh_ref), channel_id=1, source_target_pairs={{0,3},{1,0},{2,1},{3,2},{4,7},{5,4},{6,5},{7,6},{8,11},{9,8},{10,9... | collective-permute-start | bytes 786440 | tf_op jit(solution)/shard_map/ppermute | solution.py:41
  81.8 7.8 %collective-permute-start.34 = (bf16[2,128,512]{2,1,0:T(8,128)(2,1)S(1)}, bf16[2,128,512]{2,1,0:T(8,128)(2,1)S(1)}, u32[]{:S(2)}, u32[]{:S(2)}) collective-permute-start(bf16[2,128,512]{2,1,0:T(8,128)(2,1)S(1)} %get-tuple-element.45.refs_5_), channel_id=1, source_target_pairs={{0,4},{1,5},{2,6},{3,7},{4,8},{5,9},{6,10},{7,11},{8,12},{9,13},{1... | collective-permute-start | bytes 786440 | tf_op jit(solution)/shard_map/ppermute | solution.py:41
  85.3 7.6 %collective-permute-start.36 = (bf16[2,128,512]{2,1,0:T(8,128)(2,1)S(1)}, bf16[2,128,512]{2,1,0:T(8,128)(2,1)S(1)}, u32[]{:S(2)}, u32[]{:S(2)}) collective-permute-start(bf16[2,128,512]{2,1,0:T(8,128)(2,1)S(1)} %get-tuple-element.45.refs_5_), channel_id=1, source_target_pairs={{0,12},{1,13},{2,14},{3,15},{4,0},{5,1},{6,2},{7,3},{8,4},{9,5},{1... | collective-permute-start | bytes 786440 | tf_op jit(solution)/shard_map/ppermute | solution.py:41
  87.3 7.6 %collective-permute-start.35 = (bf16[2,128,512]{2,1,0:T(8,128)(2,1)S(1)}, bf16[2,128,512]{2,1,0:T(8,128)(2,1)S(1)}, u32[]{:S(2)}, u32[]{:S(2)}) collective-permute-start(bf16[2,128,512]{2,1,0:T(8,128)(2,1)S(1)} %get-tuple-element.46.refs_6_), channel_id=1, source_target_pairs={{0,4},{1,5},{2,6},{3,7},{4,8},{5,9},{6,10},{7,11},{8,12},{9,13},{1... | collective-permute-start | bytes 786440 | tf_op jit(solution)/shard_map/ppermute | solution.py:41
  89.6 8.1 %collective-permute-start.38 = (bf16[2,128,512]{2,1,0:T(8,128)(2,1)S(1)}, bf16[2,128,512]{2,1,0:T(8,128)(2,1)S(1)}, u32[]{:S(2)}, u32[]{:S(2)}) collective-permute-start(bf16[2,128,512]{2,1,0:T(8,128)(2,1)S(1)} %collective-permute-done.34.refs_7_), channel_id=1, source_target_pairs={{0,4},{1,5},{2,6},{3,7},{4,8},{5,9},{6,10},{7,11},{8,12},{9,13},{1... | collective-permute-start | bytes 786440 | tf_op jit(solution)/shard_map/ppermute | solution.py:41
  89.6 8.1 %collective-permute-start.39 = (bf16[2,128,512]{2,1,0:T(8,128)(2,1)S(1)}, bf16[2,128,512]{2,1,0:T(8,128)(2,1)S(1)}, u32[]{:S(2)}, u32[]{:S(2)}) collective-permute-start(bf16[2,128,512]{2,1,0:T(8,128)(2,1)S(1)} %collective-permute-done.37.refs_10_), channel_id=1, source_target_pairs={{0,12},{1,13},{2,14},{3,15},{4,0},{5,1},{6,2},{7,3},{8,4},{9,5},{1... | collective-permute-start | bytes 786440 | tf_op jit(solution)/shard_map/ppermute | solution.py:41
  (24 other events, 154.0 us)

commit v8 on v7

--- a/solution.py
+++ b/solution.py
@@ -360,8 +360,24 @@
     place(info, ((0, tl_ref, th_ref), (1, ll_ref, lh_ref), (3, rl_ref, rh_ref)), out_ref, sems)
 
 
-def place_far(info, held_ref, fl_ref, fh_ref, out_ref, sems):
-    place(info, ((2, fl_ref, fh_ref),), out_ref, sems)
+def place_far(half, info, held_ref, far_ref, out_ref, sems):
+    copies = []
+    for m in range(2):
+        start = pl.multiple_of(chunk(info, info[1] + 2, 2 * half + m) * WIDE, WIDE)
+        copies.append(
+            pltpu.make_async_copy(far_ref.at[m], out_ref.at[:, pl.ds(start, WIDE)], sems.at[m])
+        )
+        copies[-1].start()
+    for copy in copies:
+        copy.wait()
+
+
+def place_low(*refs):
+    place_far(0, *refs)
+
+
+def place_high(*refs):
+    place_far(1, *refs)
 
 
 def with_scalars(kernel):
@@ -482,10 +498,11 @@
         place_near, whole, [SMEM] + [VMEM] * 6, HBM, 1000, info, *line, ll, lh, rl, rh,
         scratch=[dma((3 * SIDE,))],
     )
-    out = call(
-        place_far, whole, [SMEM, HBM, VMEM, VMEM], HBM, 1000, info, out, fl, fh,
-        scratch=[dma((SIDE,))], aliases={1: 0},
-    )
+    for kernel, far in ((place_low, fl), (place_high, fh)):
+        out = call(
+            kernel, whole, [SMEM, HBM, VMEM], HBM, 1000, info, out, far, scratch=[dma((2,))],
+            aliases={1: 0},
+        )
     return out[None]
 
 

time: 98.8 us -> 99.4 us (level)
    pallas_call x15 -> x16, Pallas kernels: 10.4 us -> 11 us  [call(): pl.pallas_call(kernel, out_shape=outs, in_specs=in_specs, out_specs=out_s...]
  transfers between devices with their start and end apart: 40 -> 40, of which waited for: 18 -> 19; matrix products, arithmetic and copies ran while one was open for 0% -> 0% of each run, Pallas kernels for 7% -> 8%
where the time goes in v8:
time: 99.4 us; the launch traced here: 99.3 us
  starting transfers between devices  54.1 us (54%)
  waiting for transfers between devices  29.9 us (30%)
  Pallas kernels  11 us (11%)
  local copies, waits for them, and re-layouts  3.8 us (4%)
    ppermute x27, starting transfers between devices, shift(): return lax.ppermute(block, ('group', 'tp'), tp_route(step_a, step_b))  39.6 us
    ppermute x27, waiting for transfers between devices, shift(): return lax.ppermute(block, ('group', 'tp'), tp_route(step_a, step_b))  25.3 us
    ppermute x13, starting transfers between devices, routed(): return lax.ppermute(block, ('group', 'ctx', 'tp'), route)  14.6 us
    pallas_call x16, Pallas kernels, call(): pl.pallas_call(kernel, out_shape=outs, in_specs=in_specs, out_specs=out_s...  11 us
    ppermute x13, waiting for transfers between devices, routed(): return lax.ppermute(block, ('group', 'ctx', 'tp'), route)  4.59 us
    unnamed x16, local copies, waits for them, and re-layouts  3.8 us
  transfers between devices with their start and end apart: 40, of which 19 were waited for; matrix products, arithmetic and copies ran while one was open for 0% of the time, Pallas kernels for 8%

profile of v8, /device:TPU:6, one launch (start us, length us, event | category | flops | bytes accessed | tf_op | source)
XLA Modules:
  0.0 99.3 jit_solution(15700399498388784651)
XLA Ops:
  0.0 2.2 %collective-permute-start = (bf16[128,512]{1,0:T(8,128)(2,1)}, bf16[128,512]{1,0:T(8,128)(2,1)S(1)}, u32[]{:S(2)}, u32[]{:S(2)}) collective-permute-start(bf16[128,512]{1,0:T(8,128)(2,1)} %bitcast.12), channel_id=1, source_target_pairs={{0,1},{1,2},{2,3},{3,0},{4,5},{5,6},{6,7},{7,4},{8,9},{9,10},{10,1... | collective-permute-start | bytes 393224 | tf_op jit(solution)/shard_map/ppermute | solution.py:41
  7.8 2.2 %collective-permute-done.2 = bf16[128,512]{1,0:T(8,128)(2,1)S(1)} collective-permute-done((bf16[128,512]{1,0:T(8,128)(2,1)}, bf16[128,512]{1,0:T(8,128)(2,1)S(1)}, u32[]{:S(2)}, u32[]{:S(2)}) %collective-permute-start.2) | collective-permute-done | bytes 131104 | tf_op jit(solution)/shard_map/ppermute | solution.py:41
  10.0 1.8 %collective-permute-start.6 = (bf16[2,128,512]{2,1,0:T(8,128)(2,1)S(1)}, bf16[2,128,512]{2,1,0:T(8,128)(2,1)S(1)}, u32[]{:S(2)}, u32[]{:S(2)}) collective-permute-start(bf16[2,128,512]{2,1,0:T(8,128)(2,1)S(1)} %pad_maximum_fusion.refs_6_), channel_id=1, source_target_pairs={{0,12},{1,13},{2,14},{3,15},{4,0},{5,1},{6,2},{7,3},{8,4},{9,5},{1... | collective-permute-start | bytes 786440 | tf_op jit(solution)/shard_map/ppermute | solution.py:41
  14.2 2.3 %collective-permute-done.6.refs_9_ = bf16[2,128,512]{2,1,0:T(8,128)(2,1)S(1)} collective-permute-done((bf16[2,128,512]{2,1,0:T(8,128)(2,1)S(1)}, bf16[2,128,512]{2,1,0:T(8,128)(2,1)S(1)}, u32[]{:S(2)}, u32[]{:S(2)}) %collective-permute-start.6) | collective-permute-done | bytes 262176 | tf_op jit(solution)/shard_map/ppermute | solution.py:41
  16.5 2.9 %collective-permute-start.8 = (bf16[2,128,512]{2,1,0:T(8,128)(2,1)S(1)}, bf16[2,128,512]{2,1,0:T(8,128)(2,1)S(1)}, u32[]{:S(2)}, u32[]{:S(2)}) collective-permute-start(bf16[2,128,512]{2,1,0:T(8,128)(2,1)S(1)} %collective-permute-done.6.refs_9_), channel_id=1, source_target_pairs={{0,12},{1,13},{2,14},{3,15},{4,0},{5,1},{6,2},{7,3},{8,4},{9,5},{1... | collective-permute-start | bytes 786440 | tf_op jit(solution)/shard_map/ppermute | solution.py:41
  23.6 2.0 %collective-permute-start.9 = (bf16[128,128]{1,0:T(8,128)(2,1)S(1)}, bf16[128,128]{1,0:T(8,128)(2,1)S(1)}, u32[]{:S(2)}, u32[]{:S(2)}) collective-permute-start(bf16[128,128]{1,0:T(8,128)(2,1)S(1)} %project_far.1.refs_5_), channel_id=1, source_target_pairs={{0,1},{1,0},{2,3},{3,2},{4,5},{5,4},{6,7},{7,6},{8,9},{9,8},{10,11... | collective-permute-start | bytes 98312 | tf_op jit(solution)/shard_map/ppermute | solution.py:51
  26.1 2.2 %cache_rows.1.refs_7_ = bf16[2,32,128,256]{3,2,1,0:T(8,128)(2,1)S(1)} custom-call(s32[1]{0:T(128)} %bitcast.refs_0_, s32[1]{0:T(128)} %bitcast.1.refs_1_, s32[1]{0:T(128)} %bitcast.2.refs_2_, s32[1]{0:T(128)} %bitcast.3.refs_3_, s32[1]{0:T(128)} %bitcast.4.refs_4_, bf16[1,128,256]{2,1,0:T(8,128)(2,1)S(1)} %copy-done.3, bf16[128,128,256]{2,1,0:T(8,128)(2,1)} %refs_6_.2), custom_call_target="tpu_custom_call" | custom-call | flops 1000 | bytes 8454164 | tf_op jit(solution)/shard_map/cache_rows/pallas_call | solution.py:396
  29.0 7.3 %collective-permute-start.15 = (bf16[128,128]{1,0:T(8,128)(2,1)S(1)}, bf16[128,128]{1,0:T(8,128)(2,1)S(1)}, u32[]{:S(2)}, u32[]{:S(2)}) collective-permute-start(bf16[128,128]{1,0:T(8,128)(2,1)S(1)} %get-tuple-element.31), channel_id=1, source_target_pairs={{0,64},{1,65},{2,66},{3,67},{4,68},{5,69},{6,70},{7,71},{8,72},{9,... | collective-permute-start | bytes 98312 | tf_op jit(solution)/shard_map/ppermute | solution.py:51
  36.3 1.9 %collective-permute-start.14 = (bf16[2,128,128]{2,1,0:T(8,128)(2,1)S(1)}, bf16[2,128,128]{2,1,0:T(8,128)(2,1)S(1)}, u32[]{:S(2)}, u32[]{:S(2)}) collective-permute-start(bf16[2,128,128]{2,1,0:T(8,128)(2,1)S(1)} %get-tuple-element.29.refs_6_), channel_id=1, source_target_pairs={{0,48},{1,49},{2,50},{3,51},{4,52},{5,53},{6,54},{7,55},{8,56},{9,... | collective-permute-start | bytes 196616 | tf_op jit(solution)/shard_map/ppermute | solution.py:51
  38.9 2.4 %cache_kernel.1.refs_19_ = f32[2,2,64,128]{3,2,1,0:T(8,128)S(1)} custom-call(s32[1]{0:T(128)} %bitcast.refs_0_, s32[1]{0:T(128)} %bitcast.1.refs_1_, s32[1]{0:T(128)} %bitcast.2.refs_2_, s32[1]{0:T(128)} %bitcast.3.refs_3_, s32[1]{0:T(128)} %bitcast.4.refs_4_, bf16[1,128,256]{2,1,0:T(8,128)(2,1)S(1)} %copy-done.3, ...), custom_call_target="tpu_custom_call" | custom-call | flops 1000 | bytes 4326932 | tf_op jit(solution)/shard_map/cache_kernel/pallas_call | solution.py:396
  41.3 1.7 %collective-permute-start.21 = (f32[2,2,64,128]{3,2,1,0:T(8,128)S(1)}, f32[2,2,64,128]{3,2,1,0:T(8,128)S(1)}, u32[]{:S(2)}, u32[]{:S(2)}) collective-permute-start(f32[2,2,64,128]{3,2,1,0:T(8,128)S(1)} %cache_kernel.1.refs_19_), channel_id=1, source_target_pairs={{0,128},{1,129},{2,130},{3,131},{4,132},{5,133},{6,134},{7,135},{8... | collective-permute-start | bytes 393224 | tf_op jit(solution)/shard_map/ppermute | solution.py:51
  49.1 3.8 %collective-permute-start.26 = (bf16[2,128,512]{2,1,0:T(8,128)(2,1)S(1)}, bf16[2,128,512]{2,1,0:T(8,128)(2,1)S(1)}, u32[]{:S(2)}, u32[]{:S(2)}) collective-permute-start(bf16[2,128,512]{2,1,0:T(8,128)(2,1)S(1)} %get-tuple-element.42), channel_id=1, source_target_pairs={{0,12},{1,13},{2,14},{3,15},{4,0},{5,1},{6,2},{7,3},{8,4},{9,5},{1... | collective-permute-start | bytes 786440 | tf_op jit(solution)/shard_map/ppermute | solution.py:41
  53.6 3.2 %collective-permute-start.25 = (bf16[2,128,512]{2,1,0:T(8,128)(2,1)S(1)}, bf16[2,128,512]{2,1,0:T(8,128)(2,1)S(1)}, u32[]{:S(2)}, u32[]{:S(2)}) collective-permute-start(bf16[2,128,512]{2,1,0:T(8,128)(2,1)S(1)} %get-tuple-element.40), channel_id=1, source_target_pairs={{0,12},{1,13},{2,14},{3,15},{4,0},{5,1},{6,2},{7,3},{8,4},{9,5},{1... | collective-permute-start | bytes 786440 | tf_op jit(solution)/shard_map/ppermute | solution.py:41
  57.4 3.3 %collective-permute-start.27 = (bf16[2,128,512]{2,1,0:T(8,128)(2,1)S(1)}, bf16[2,128,512]{2,1,0:T(8,128)(2,1)S(1)}, u32[]{:S(2)}, u32[]{:S(2)}) collective-permute-start(bf16[2,128,512]{2,1,0:T(8,128)(2,1)S(1)} %add_kernel.3), channel_id=1, source_target_pairs={{0,12},{1,13},{2,14},{3,15},{4,0},{5,1},{6,2},{7,3},{8,4},{9,5},{1... | collective-permute-start | bytes 786440 | tf_op jit(solution)/shard_map/ppermute | solution.py:41
  61.1 3.7 %collective-permute-done.23.ll_ref = bf16[2,128,512]{2,1,0:T(8,128)(2,1)S(1)} collective-permute-done((bf16[2,128,512]{2,1,0:T(8,128)(2,1)S(1)}, bf16[2,128,512]{2,1,0:T(8,128)(2,1)S(1)}, u32[]{:S(2)}, u32[]{:S(2)}) %collective-permute-start.23) | collective-permute-done | bytes 262176 | tf_op jit(solution)/shard_map/ppermute | solution.py:41
  68.5 2.1 %collective-permute-start.29 = (bf16[2,128,512]{2,1,0:T(8,128)(2,1)S(1)}, bf16[2,128,512]{2,1,0:T(8,128)(2,1)S(1)}, u32[]{:S(2)}, u32[]{:S(2)}) collective-permute-start(bf16[2,128,512]{2,1,0:T(8,128)(2,1)S(1)} %get-tuple-element.44.high_ref), channel_id=1, source_target_pairs={{0,1},{1,2},{2,3},{3,0},{4,5},{5,6},{6,7},{7,4},{8,9},{9,10},{10,1... | collective-permute-start | bytes 786440 | tf_op jit(solution)/shard_map/ppermute | solution.py:41
  71.7 2.2 %collective-permute-start.32 = (bf16[2,128,512]{2,1,0:T(8,128)(2,1)S(1)}, bf16[2,128,512]{2,1,0:T(8,128)(2,1)S(1)}, u32[]{:S(2)}, u32[]{:S(2)}) collective-permute-start(bf16[2,128,512]{2,1,0:T(8,128)(2,1)S(1)} %collective-permute-done.28.ll_ref), channel_id=1, source_target_pairs={{0,1},{1,2},{2,3},{3,0},{4,5},{5,6},{6,7},{7,4},{8,9},{9,10},{10,1... | collective-permute-start | bytes 786440 | tf_op jit(solution)/shard_map/ppermute | solution.py:41
  73.9 2.8 %collective-permute-done.30.rl_ref = bf16[2,128,512]{2,1,0:T(8,128)(2,1)S(1)} collective-permute-done((bf16[2,128,512]{2,1,0:T(8,128)(2,1)S(1)}, bf16[2,128,512]{2,1,0:T(8,128)(2,1)S(1)}, u32[]{:S(2)}, u32[]{:S(2)}) %collective-permute-start.30) | collective-permute-done | bytes 262176 | tf_op jit(solution)/shard_map/ppermute | solution.py:41
  78.1 3.4 %collective-permute-done.33.fh_ref = bf16[2,128,512]{2,1,0:T(8,128)(2,1)S(1)} collective-permute-done((bf16[2,128,512]{2,1,0:T(8,128)(2,1)S(1)}, bf16[2,128,512]{2,1,0:T(8,128)(2,1)S(1)}, u32[]{:S(2)}, u32[]{:S(2)}) %collective-permute-start.33) | collective-permute-done | bytes 262176 | tf_op jit(solution)/shard_map/ppermute | solution.py:41
  82.2 3.1 %collective-permute-start.37 = (bf16[2,128,512]{2,1,0:T(8,128)(2,1)S(1)}, bf16[2,128,512]{2,1,0:T(8,128)(2,1)S(1)}, u32[]{:S(2)}, u32[]{:S(2)}) collective-permute-start(bf16[2,128,512]{2,1,0:T(8,128)(2,1)S(1)} %get-tuple-element.46.refs_6_), channel_id=1, source_target_pairs={{0,12},{1,13},{2,14},{3,15},{4,0},{5,1},{6,2},{7,3},{8,4},{9,5},{1... | collective-permute-start | bytes 786440 | tf_op jit(solution)/shard_map/ppermute | solution.py:41
  85.3 1.9 %collective-permute-start.36 = (bf16[2,128,512]{2,1,0:T(8,128)(2,1)S(1)}, bf16[2,128,512]{2,1,0:T(8,128)(2,1)S(1)}, u32[]{:S(2)}, u32[]{:S(2)}) collective-permute-start(bf16[2,128,512]{2,1,0:T(8,128)(2,1)S(1)} %get-tuple-element.45.refs_5_), channel_id=1, source_target_pairs={{0,12},{1,13},{2,14},{3,15},{4,0},{5,1},{6,2},{7,3},{8,4},{9,5},{1... | collective-permute-start | bytes 786440 | tf_op jit(solution)/shard_map/ppermute | solution.py:41
  87.3 2.2 %collective-permute-done.34.refs_7_ = bf16[2,128,512]{2,1,0:T(8,128)(2,1)S(1)} collective-permute-done((bf16[2,128,512]{2,1,0:T(8,128)(2,1)S(1)}, bf16[2,128,512]{2,1,0:T(8,128)(2,1)S(1)}, u32[]{:S(2)}, u32[]{:S(2)}) %collective-permute-start.34) | collective-permute-done | bytes 262176 | tf_op jit(solution)/shard_map/ppermute | solution.py:41
  89.6 3.3 %collective-permute-start.39 = (bf16[2,128,512]{2,1,0:T(8,128)(2,1)S(1)}, bf16[2,128,512]{2,1,0:T(8,128)(2,1)S(1)}, u32[]{:S(2)}, u32[]{:S(2)}) collective-permute-start(bf16[2,128,512]{2,1,0:T(8,128)(2,1)S(1)} %collective-permute-done.37.refs_10_), channel_id=1, source_target_pairs={{0,12},{1,13},{2,14},{3,15},{4,0},{5,1},{6,2},{7,3},{8,4},{9,5},{1... | collective-permute-start | bytes 786440 | tf_op jit(solution)/shard_map/ppermute | solution.py:41
  92.9 1.9 %collective-permute-done.35.refs_8_ = bf16[2,128,512]{2,1,0:T(8,128)(2,1)S(1)} collective-permute-done((bf16[2,128,512]{2,1,0:T(8,128)(2,1)S(1)}, bf16[2,128,512]{2,1,0:T(8,128)(2,1)S(1)}, u32[]{:S(2)}, u32[]{:S(2)}) %collective-permute-start.35) | collective-permute-done | bytes 262176 | tf_op jit(solution)/shard_map/ppermute | solution.py:41
  (89 shorter events, 32.7 us)
Async XLA Ops:
  2.2 7.8 %collective-permute-start.2 = (bf16[128,512]{1,0:T(8,128)(2,1)}, bf16[128,512]{1,0:T(8,128)(2,1)S(1)}, u32[]{:S(2)}, u32[]{:S(2)}) collective-permute-start(bf16[128,512]{1,0:T(8,128)(2,1)} %bitcast.13), channel_id=1, source_target_pairs={{0,3},{1,0},{2,1},{3,2},{4,7},{5,4},{6,5},{7,6},{8,11},{9,8},{10,9... | collective-permute-start | bytes 393224 | tf_op jit(solution)/shard_map/ppermute | solution.py:41
  2.2 7.8 %collective-permute-start.1 = (bf16[128,512]{1,0:T(8,128)(2,1)}, bf16[128,512]{1,0:T(8,128)(2,1)S(1)}, u32[]{:S(2)}, u32[]{:S(2)}) collective-permute-start(bf16[128,512]{1,0:T(8,128)(2,1)} %bitcast.14), channel_id=1, source_target_pairs={{0,2},{1,3},{2,0},{3,1},{4,6},{5,7},{6,4},{7,5},{8,10},{9,11},{10,... | collective-permute-start | bytes 393224 | tf_op jit(solution)/shard_map/ppermute | solution.py:41
  6.1 7.8 %collective-permute-start.3 = (bf16[2,128,512]{2,1,0:T(8,128)(2,1)S(1)}, bf16[2,128,512]{2,1,0:T(8,128)(2,1)S(1)}, u32[]{:S(2)}, u32[]{:S(2)}) collective-permute-start(bf16[2,128,512]{2,1,0:T(8,128)(2,1)S(1)} %join_kernel.1.refs_5_), channel_id=1, source_target_pairs={{0,4},{1,5},{2,6},{3,7},{4,8},{5,9},{6,10},{7,11},{8,12},{9,13},{1... | collective-permute-start | bytes 786440 | tf_op jit(solution)/shard_map/ppermute | solution.py:41
  11.8 9.5 %collective-permute-start.5 = (bf16[2,128,512]{2,1,0:T(8,128)(2,1)S(1)}, bf16[2,128,512]{2,1,0:T(8,128)(2,1)S(1)}, u32[]{:S(2)}, u32[]{:S(2)}) collective-permute-start(bf16[2,128,512]{2,1,0:T(8,128)(2,1)S(1)} %join_kernel.1.refs_5_), channel_id=1, source_target_pairs={{0,12},{1,13},{2,14},{3,15},{4,0},{5,1},{6,2},{7,3},{8,4},{9,5},{1... | collective-permute-start | bytes 786440 | tf_op jit(solution)/shard_map/ppermute | solution.py:41
  12.6 8.7 %collective-permute-start.4 = (bf16[2,128,512]{2,1,0:T(8,128)(2,1)S(1)}, bf16[2,128,512]{2,1,0:T(8,128)(2,1)S(1)}, u32[]{:S(2)}, u32[]{:S(2)}) collective-permute-start(bf16[2,128,512]{2,1,0:T(8,128)(2,1)S(1)} %pad_maximum_fusion.refs_6_), channel_id=1, source_target_pairs={{0,4},{1,5},{2,6},{3,7},{4,8},{5,9},{6,10},{7,11},{8,12},{9,13},{1... | collective-permute-start | bytes 786440 | tf_op jit(solution)/shard_map/ppermute | solution.py:41
  13.9 9.2 %collective-permute-start.7 = (bf16[2,128,512]{2,1,0:T(8,128)(2,1)S(1)}, bf16[2,128,512]{2,1,0:T(8,128)(2,1)S(1)}, u32[]{:S(2)}, u32[]{:S(2)}) collective-permute-start(bf16[2,128,512]{2,1,0:T(8,128)(2,1)S(1)} %collective-permute-done.3.refs_6_), channel_id=1, source_target_pairs={{0,4},{1,5},{2,6},{3,7},{4,8},{5,9},{6,10},{7,11},{8,12},{9,13},{1... | collective-permute-start | bytes 786440 | tf_op jit(solution)/shard_map/ppermute | solution.py:41
  25.9 13.0 %collective-permute-start.20 = (bf16[1,128,256]{2,1,0:T(8,128)(2,1)S(1)}, bf16[1,128,256]{2,1,0:T(8,128)(2,1)S(1)}, u32[]{:S(2)}, u32[]{:S(2)}) collective-permute-start(bf16[1,128,256]{2,1,0:T(8,128)(2,1)S(1)} %copy-done.3), channel_id=1, source_target_pairs={{0,128},{1,129},{2,130},{3,131},{4,132},{5,133},{6,134},{7,135},{8... | collective-permute-start | bytes 196616 | tf_op jit(solution)/shard_map/ppermute | solution.py:51
  29.0 9.9 %collective-permute-start.15 = (bf16[128,128]{1,0:T(8,128)(2,1)S(1)}, bf16[128,128]{1,0:T(8,128)(2,1)S(1)}, u32[]{:S(2)}, u32[]{:S(2)}) collective-permute-start(bf16[128,128]{1,0:T(8,128)(2,1)S(1)} %get-tuple-element.31), channel_id=1, source_target_pairs={{0,64},{1,65},{2,66},{3,67},{4,68},{5,69},{6,70},{7,71},{8,72},{9,... | collective-permute-start | bytes 98312 | tf_op jit(solution)/shard_map/ppermute | solution.py:51
  38.2 8.0 %collective-permute-start.12 = (bf16[2,128,128]{2,1,0:T(8,128)(2,1)S(1)}, bf16[2,128,128]{2,1,0:T(8,128)(2,1)S(1)}, u32[]{:S(2)}, u32[]{:S(2)}) collective-permute-start(bf16[2,128,128]{2,1,0:T(8,128)(2,1)S(1)} %get-tuple-element.29.refs_6_), channel_id=1, source_target_pairs={{0,16},{1,17},{2,18},{3,19},{4,20},{5,21},{6,22},{7,23},{8,24},{9,... | collective-permute-start | bytes 196616 | tf_op jit(solution)/shard_map/ppermute | solution.py:51
  49.0 8.1 %collective-permute-start.22 = (bf16[2,128,512]{2,1,0:T(8,128)(2,1)S(1)}, bf16[2,128,512]{2,1,0:T(8,128)(2,1)S(1)}, u32[]{:S(2)}, u32[]{:S(2)}) collective-permute-start(bf16[2,128,512]{2,1,0:T(8,128)(2,1)S(1)} %get-tuple-element.38), channel_id=1, source_target_pairs={{0,4},{1,5},{2,6},{3,7},{4,8},{5,9},{6,10},{7,11},{8,12},{9,13},{1... | collective-permute-start | bytes 786440 | tf_op jit(solution)/shard_map/ppermute | solution.py:41
  49.1 8.2 %collective-permute-start.26 = (bf16[2,128,512]{2,1,0:T(8,128)(2,1)S(1)}, bf16[2,128,512]{2,1,0:T(8,128)(2,1)S(1)}, u32[]{:S(2)}, u32[]{:S(2)}) collective-permute-start(bf16[2,128,512]{2,1,0:T(8,128)(2,1)S(1)} %get-tuple-element.42), channel_id=1, source_target_pairs={{0,12},{1,13},{2,14},{3,15},{4,0},{5,1},{6,2},{7,3},{8,4},{9,5},{1... | collective-permute-start | bytes 786440 | tf_op jit(solution)/shard_map/ppermute | solution.py:41
  53.5 7.7 %collective-permute-start.24 = (bf16[2,128,512]{2,1,0:T(8,128)(2,1)S(1)}, bf16[2,128,512]{2,1,0:T(8,128)(2,1)S(1)}, u32[]{:S(2)}, u32[]{:S(2)}) collective-permute-start(bf16[2,128,512]{2,1,0:T(8,128)(2,1)S(1)} %get-tuple-element.39), channel_id=1, source_target_pairs={{0,4},{1,5},{2,6},{3,7},{4,8},{5,9},{6,10},{7,11},{8,12},{9,13},{1... | collective-permute-start | bytes 786440 | tf_op jit(solution)/shard_map/ppermute | solution.py:41
  53.6 7.6 %collective-permute-start.25 = (bf16[2,128,512]{2,1,0:T(8,128)(2,1)S(1)}, bf16[2,128,512]{2,1,0:T(8,128)(2,1)S(1)}, u32[]{:S(2)}, u32[]{:S(2)}) collective-permute-start(bf16[2,128,512]{2,1,0:T(8,128)(2,1)S(1)} %get-tuple-element.40), channel_id=1, source_target_pairs={{0,12},{1,13},{2,14},{3,15},{4,0},{5,1},{6,2},{7,3},{8,4},{9,5},{1... | collective-permute-start | bytes 786440 | tf_op jit(solution)/shard_map/ppermute | solution.py:41
  57.2 7.7 %collective-permute-start.23 = (bf16[2,128,512]{2,1,0:T(8,128)(2,1)S(1)}, bf16[2,128,512]{2,1,0:T(8,128)(2,1)S(1)}, u32[]{:S(2)}, u32[]{:S(2)}) collective-permute-start(bf16[2,128,512]{2,1,0:T(8,128)(2,1)S(1)} %add_kernel.2), channel_id=1, source_target_pairs={{0,4},{1,5},{2,6},{3,7},{4,8},{5,9},{6,10},{7,11},{8,12},{9,13},{1... | collective-permute-start | bytes 786440 | tf_op jit(solution)/shard_map/ppermute | solution.py:41
  57.4 7.5 %collective-permute-start.27 = (bf16[2,128,512]{2,1,0:T(8,128)(2,1)S(1)}, bf16[2,128,512]{2,1,0:T(8,128)(2,1)S(1)}, u32[]{:S(2)}, u32[]{:S(2)}) collective-permute-start(bf16[2,128,512]{2,1,0:T(8,128)(2,1)S(1)} %add_kernel.3), channel_id=1, source_target_pairs={{0,12},{1,13},{2,14},{3,15},{4,0},{5,1},{6,2},{7,3},{8,4},{9,5},{1... | collective-permute-start | bytes 786440 | tf_op jit(solution)/shard_map/ppermute | solution.py:41
  66.3 7.6 %collective-permute-start.31 = (bf16[2,128,512]{2,1,0:T(8,128)(2,1)S(1)}, bf16[2,128,512]{2,1,0:T(8,128)(2,1)S(1)}, u32[]{:S(2)}, u32[]{:S(2)}) collective-permute-start(bf16[2,128,512]{2,1,0:T(8,128)(2,1)S(1)} %get-tuple-element.44.high_ref), channel_id=1, source_target_pairs={{0,3},{1,0},{2,1},{3,2},{4,7},{5,4},{6,5},{7,6},{8,11},{9,8},{10,9... | collective-permute-start | bytes 786440 | tf_op jit(solution)/shard_map/ppermute | solution.py:41
  67.4 9.4 %collective-permute-start.30 = (bf16[2,128,512]{2,1,0:T(8,128)(2,1)S(1)}, bf16[2,128,512]{2,1,0:T(8,128)(2,1)S(1)}, u32[]{:S(2)}, u32[]{:S(2)}) collective-permute-start(bf16[2,128,512]{2,1,0:T(8,128)(2,1)S(1)} %get-tuple-element.43.low_ref), channel_id=1, source_target_pairs={{0,3},{1,0},{2,1},{3,2},{4,7},{5,4},{6,5},{7,6},{8,11},{9,8},{10,9... | collective-permute-start | bytes 786440 | tf_op jit(solution)/shard_map/ppermute | solution.py:41
  68.5 8.3 %collective-permute-start.29 = (bf16[2,128,512]{2,1,0:T(8,128)(2,1)S(1)}, bf16[2,128,512]{2,1,0:T(8,128)(2,1)S(1)}, u32[]{:S(2)}, u32[]{:S(2)}) collective-permute-start(bf16[2,128,512]{2,1,0:T(8,128)(2,1)S(1)} %get-tuple-element.44.high_ref), channel_id=1, source_target_pairs={{0,1},{1,2},{2,3},{3,0},{4,5},{5,6},{6,7},{7,4},{8,9},{9,10},{10,1... | collective-permute-start | bytes 786440 | tf_op jit(solution)/shard_map/ppermute | solution.py:41
  73.9 7.6 %collective-permute-start.33 = (bf16[2,128,512]{2,1,0:T(8,128)(2,1)S(1)}, bf16[2,128,512]{2,1,0:T(8,128)(2,1)S(1)}, u32[]{:S(2)}, u32[]{:S(2)}) collective-permute-start(bf16[2,128,512]{2,1,0:T(8,128)(2,1)S(1)} %collective-permute-done.31.rh_ref), channel_id=1, source_target_pairs={{0,3},{1,0},{2,1},{3,2},{4,7},{5,4},{6,5},{7,6},{8,11},{9,8},{10,9... | collective-permute-start | bytes 786440 | tf_op jit(solution)/shard_map/ppermute | solution.py:41
  81.8 7.8 %collective-permute-start.34 = (bf16[2,128,512]{2,1,0:T(8,128)(2,1)S(1)}, bf16[2,128,512]{2,1,0:T(8,128)(2,1)S(1)}, u32[]{:S(2)}, u32[]{:S(2)}) collective-permute-start(bf16[2,128,512]{2,1,0:T(8,128)(2,1)S(1)} %get-tuple-element.45.refs_5_), channel_id=1, source_target_pairs={{0,4},{1,5},{2,6},{3,7},{4,8},{5,9},{6,10},{7,11},{8,12},{9,13},{1... | collective-permute-start | bytes 786440 | tf_op jit(solution)/shard_map/ppermute | solution.py:41
  85.3 7.6 %collective-permute-start.36 = (bf16[2,128,512]{2,1,0:T(8,128)(2,1)S(1)}, bf16[2,128,512]{2,1,0:T(8,128)(2,1)S(1)}, u32[]{:S(2)}, u32[]{:S(2)}) collective-permute-start(bf16[2,128,512]{2,1,0:T(8,128)(2,1)S(1)} %get-tuple-element.45.refs_5_), channel_id=1, source_target_pairs={{0,12},{1,13},{2,14},{3,15},{4,0},{5,1},{6,2},{7,3},{8,4},{9,5},{1... | collective-permute-start | bytes 786440 | tf_op jit(solution)/shard_map/ppermute | solution.py:41
  87.2 7.6 %collective-permute-start.35 = (bf16[2,128,512]{2,1,0:T(8,128)(2,1)S(1)}, bf16[2,128,512]{2,1,0:T(8,128)(2,1)S(1)}, u32[]{:S(2)}, u32[]{:S(2)}) collective-permute-start(bf16[2,128,512]{2,1,0:T(8,128)(2,1)S(1)} %get-tuple-element.46.refs_6_), channel_id=1, source_target_pairs={{0,4},{1,5},{2,6},{3,7},{4,8},{5,9},{6,10},{7,11},{8,12},{9,13},{1... | collective-permute-start | bytes 786440 | tf_op jit(solution)/shard_map/ppermute | solution.py:41
  89.6 8.1 %collective-permute-start.38 = (bf16[2,128,512]{2,1,0:T(8,128)(2,1)S(1)}, bf16[2,128,512]{2,1,0:T(8,128)(2,1)S(1)}, u32[]{:S(2)}, u32[]{:S(2)}) collective-permute-start(bf16[2,128,512]{2,1,0:T(8,128)(2,1)S(1)} %collective-permute-done.34.refs_7_), channel_id=1, source_target_pairs={{0,4},{1,5},{2,6},{3,7},{4,8},{5,9},{6,10},{7,11},{8,12},{9,13},{1... | collective-permute-start | bytes 786440 | tf_op jit(solution)/shard_map/ppermute | solution.py:41
  89.6 8.8 %collective-permute-start.39 = (bf16[2,128,512]{2,1,0:T(8,128)(2,1)S(1)}, bf16[2,128,512]{2,1,0:T(8,128)(2,1)S(1)}, u32[]{:S(2)}, u32[]{:S(2)}) collective-permute-start(bf16[2,128,512]{2,1,0:T(8,128)(2,1)S(1)} %collective-permute-done.37.refs_10_), channel_id=1, source_target_pairs={{0,12},{1,13},{2,14},{3,15},{4,0},{5,1},{6,2},{7,3},{8,4},{9,5},{1... | collective-permute-start | bytes 786440 | tf_op jit(solution)/shard_map/ppermute | solution.py:41
  (24 other events, 141.3 us)
